TPU v7x, 256 devices: a whole 4x4x8 slice. The times are simulated.
256 devices in a mesh: dp: 16 (over x, y), ep: 8 (over z), tp: 2 (over core).
Axes of the slice: x: 4, y: 4, z: 8, core: 2. Of those that a mesh axis runs over, the one named last changes fastest.
Arguments:
- queries: bfloat16 [2048, 64, 576], P('dp', ('ep', 'tp')), may hold values from -18 to 18
- cache: bfloat16 [64, 256, 576], P('dp'), may hold values from -4 to 4
- span_latent: bfloat16 [64, 32, 576], P('dp'), may hold values from -4 to 4
- prefix_len: int32 [64], replicated, may hold values from 1 to 256, as said below
- destination: int32 [2, 16], replicated, may hold values from 0 to 15, each once within a row
- uv_weight: bfloat16 [64, 512, 128], P(('ep', 'tp')), may hold values from -0.25 to 0.25
- out_weight: bfloat16 [8192, 7168], P(('ep', 'tp'), 'dp'), may hold values from -0.0625 to 0.0625
- residual: bfloat16 [2048, 7168], P('dp'), may hold values from -6 to 6
- norm_gain: bfloat16 [7168], replicated, may hold values from 0.25 to 1.75
- routes: int32 [2048, 2], P('dp'), may hold values from 0 to 15, all different within a row; in each aligned block of 128 rows (0 to 127, 128 to 255, ...) at most 24 rows name the same one
- route_weight: bfloat16 [2048, 2], P('dp'), may hold values from 0.19921875 to 1
- gate_weight: bfloat16 [16, 7168, 2048], P('dp', None, ('ep', 'tp')), may hold values from -0.0625 to 0.0625
- up_weight: bfloat16 [16, 7168, 2048], P('dp', None, ('ep', 'tp')), may hold values from -0.0625 to 0.0625
- down_weight: bfloat16 [16, 2048, 7168], P('dp', ('ep', 'tp')), may hold values from -0.125 to 0.125
Outputs:
- output: bfloat16 [2048, 7168], P(('dp', 'ep', 'tp'))
Inputs may be any that keep to these rules, and one draw needn't show every extreme that they name: `prefix_len`: some request holds exactly 256 rows. `destination`: each row is a permutation of the ranks. `routes`: each row names 2 different experts; within the tokens of one rank no expert is named more than 24 times, a bound that some block reaches.
All inputs are finite; a program needn't handle non-finite values.
Results may differ from a plain program's by a relative error of at most 0.02.
Values may be sent and summed in bfloat16 or wider, within the bound.
No kernel may reach another device: no remote copies, remote signals or barrier semaphores. Data moves between devices by JAX's collectives and lax.ppermute only.
A program may use at most 128 MiB of HBM per device.

v0:
```python
import jax
import jax.numpy as jnp
from jax import lax
from jax.sharding import PartitionSpec as P

score_scale = 192.0 ** (-0.5)
norm_eps = 1e-06


def key_mask(lengths, prefix_rows, span_rows):
    key_index = jnp.arange(prefix_rows + span_rows, dtype=jnp.int32)
    query_index = jnp.arange(span_rows, dtype=jnp.int32)
    in_prefix = (key_index < prefix_rows) & (key_index < lengths[..., None])
    in_span = (key_index[None, :] >= prefix_rows) & (
        key_index[None, :] - prefix_rows <= query_index[:, None]
    )
    return in_prefix[..., None, :] | in_span


def rms_norm(rows, gain):
    widened = rows.astype(jnp.float32)
    factor = lax.rsqrt(jnp.mean(widened * widened, axis=-1, keepdims=True) + norm_eps)
    return (widened * factor * gain.astype(jnp.float32)).astype(jnp.bfloat16)


def slot_tables(route_rows, weight_rows, experts, capacity):
    top_k = route_rows.shape[1]
    flat_routes = route_rows.reshape(-1)
    hits = (flat_routes[:, None] == jnp.arange(experts, dtype=jnp.int32)[None, :]).astype(jnp.int32)
    earlier = jnp.cumsum(hits, axis=0) - hits
    position = jnp.sum(earlier * hits, axis=1)
    slot_of = flat_routes * capacity + position
    matches = jnp.arange(experts * capacity, dtype=jnp.int32)[:, None] == slot_of[None, :]
    matches = matches.reshape(experts * capacity, route_rows.shape[0], top_k)
    placer = jnp.any(matches, axis=-1).astype(jnp.bfloat16)
    combiner = jnp.sum(
        jnp.where(matches, weight_rows[None], jnp.zeros((), weight_rows.dtype)), axis=-1
    ).T
    return (placer, combiner)


def expert_pieces(rows_in, gate_weight, up_weight, down_weight):
    gate_proj = jnp.dot(rows_in, gate_weight[0], preferred_element_type=jnp.float32)
    up_proj = jnp.dot(rows_in, up_weight[0], preferred_element_type=jnp.float32)
    hidden = (jax.nn.silu(gate_proj) * up_proj).astype(jnp.bfloat16)
    return jnp.dot(hidden, down_weight[0], preferred_element_type=jnp.float32).astype(jnp.bfloat16)


def per_device(
    queries,
    cache,
    span_latent,
    prefix_len,
    destination,
    uv_weight,
    out_weight,
    residual,
    norm_gain,
    routes,
    route_weight,
    gate_weight,
    up_weight,
    down_weight,
):
    requests, prefix_rows, cached_width = cache.shape
    span_rows = span_latent.shape[1]
    tok_rows, heads_here = (queries.shape[0], queries.shape[1])
    latent_width, value_width = (uv_weight.shape[1], uv_weight.shape[2])
    rank_count = lax.axis_size("dp")
    members = lax.axis_size(("ep", "tp"))
    my_rank = lax.axis_index("dp")
    ranks = jnp.arange(rank_count, dtype=jnp.int32)
    source_first = jnp.sum(ranks * (destination[0] == my_rank).astype(jnp.int32))
    source_second = jnp.sum(ranks * (destination[1] == my_rank).astype(jnp.int32))
    moving = cache[requests - 2 :]
    out_full, arrived = (
        lax.all_gather(out_weight, "dp", axis=1, tiled=True),
        lax.all_gather(moving, "dp", axis=0, tiled=True),
    )
    incoming_first = lax.dynamic_index_in_dim(arrived, source_first * 2, 0, keepdims=True)
    incoming_second = lax.dynamic_index_in_dim(arrived, source_second * 2 + 1, 0, keepdims=True)
    prefixes = jnp.concatenate([cache[: requests - 2], incoming_first, incoming_second], axis=0)
    own_len = lax.dynamic_slice_in_dim(prefix_len, my_rank * requests, requests)
    moved_first = lax.dynamic_index_in_dim(
        prefix_len, source_first * requests + requests - 2, 0, keepdims=True
    )
    moved_second = lax.dynamic_index_in_dim(
        prefix_len, source_second * requests + requests - 1, 0, keepdims=True
    )
    lengths = jnp.concatenate([own_len[: requests - 2], moved_first, moved_second])
    keys_all = jnp.concatenate([prefixes, span_latent], axis=1)
    grouped = queries.reshape(requests, span_rows, heads_here, cached_width)
    scores = (
        jnp.einsum("jthc,jkc->jthk", grouped, keys_all, preferred_element_type=jnp.float32)
        * score_scale
    )
    allowed = key_mask(lengths, prefix_rows, span_rows)[:, :, None, :]
    scores = jnp.where(allowed, scores, -jnp.inf)
    highest = jnp.max(scores, axis=-1, keepdims=True)
    raised = jnp.exp(scores - highest)
    weights = (raised / jnp.sum(raised, axis=-1, keepdims=True)).astype(jnp.bfloat16)
    latent_out = jnp.einsum(
        "jthk,jkc->jthc", weights, keys_all[:, :, :latent_width], preferred_element_type=jnp.float32
    ).astype(jnp.bfloat16)
    latent_out = latent_out.reshape(tok_rows, heads_here, latent_width)
    values = jnp.einsum(
        "thc,hcv->thv", latent_out, uv_weight, preferred_element_type=jnp.float32
    ).astype(jnp.bfloat16)
    flat_values = values.reshape(tok_rows, heads_here * value_width)
    partial_sum = jnp.dot(flat_values, out_full, preferred_element_type=jnp.float32)
    attended = lax.psum(partial_sum.astype(jnp.bfloat16), ("ep", "tp")).astype(jnp.float32)
    mixed_rows = (residual.astype(jnp.float32) + attended).astype(jnp.bfloat16)
    normed = rms_norm(mixed_rows, norm_gain)
    model_width = normed.shape[1]
    top_k = routes.shape[1]
    capacity = max(2, 3 * tok_rows * top_k // (2 * rank_count))
    placer, combiner = slot_tables(routes, route_weight, rank_count, capacity)
    rows_here = tok_rows // members
    member = lax.axis_index(("ep", "tp"))
    own_rows = lax.dynamic_slice_in_dim(mixed_rows, member * rows_here, rows_here, 0)
    outgoing = jnp.dot(placer, normed, preferred_element_type=jnp.float32).astype(jnp.bfloat16)
    outgoing = outgoing.reshape(rank_count, capacity, model_width)
    received = lax.all_to_all(outgoing, "dp", split_axis=0, concat_axis=0, tiled=True)
    rows_in = received.reshape(rank_count * capacity, model_width)
    pieces = expert_pieces(rows_in, gate_weight, up_weight, down_weight)
    pieces = pieces.reshape(rank_count, capacity, model_width)
    returned = lax.all_to_all(pieces, "dp", split_axis=0, concat_axis=0, tiled=True)
    flat_back = returned.reshape(rank_count * capacity, model_width)
    moe_rows = lax.psum_scatter(
        jnp.dot(combiner, flat_back, preferred_element_type=jnp.float32).astype(jnp.bfloat16),
        ("ep", "tp"),
        scatter_dimension=0,
        tiled=True,
    ).astype(jnp.float32)
    return (own_rows.astype(jnp.float32) + moe_rows).astype(jnp.bfloat16)


def solution(mesh):
    in_specs = (
        P("dp", ("ep", "tp"), None),
        P("dp", None, None),
        P("dp", None, None),
        P(),
        P(),
        P(("ep", "tp"), None, None),
        P(("ep", "tp"), "dp"),
        P("dp", None),
        P(),
        P("dp", None),
        P("dp", None),
        P("dp", None, ("ep", "tp")),
        P("dp", None, ("ep", "tp")),
        P("dp", ("ep", "tp"), None),
    )
    out_specs = P(("dp", "ep", "tp"), None)
    return jax.shard_map(
        per_device, mesh=mesh, in_specs=in_specs, out_specs=out_specs, check_vma=False
    )
```

profile of v0, /device:TPU:1, one launch (start us, length us, event | category | flops | bytes accessed | tf_op | source)
XLA Modules:
  0.0 543.4 jit_solution(39429512091998673)
XLA Ops:
  6.5 2.3 fusion.54
  8.9 0.7 all-gather.5.cloned.1.call-update
  13.0 2.2 copy.62
  15.9 1.4 pad_add_fusion
  17.4 77.0 %all-gather.3.cloned.1.call-done = bf16[32,256,576]{1,2,0:T(8,128)(2,1)} async-done(((bf16[2,256,576]{1,2,0:T(8,128)(2,1)}), bf16[32,256,576]{1,2,0:T(8,128)(2,1)}) %all-gather.3.cloned.1.call-update) | async-done | bytes 9437200 | tf_op jit(solution)/shard_map/all_gather | solution.py:78
  94.4 1.1 constant_dynamic-slice_fusion.1
  95.9 1.9 fusion.22
  97.8 0.9 copy-done.4
  99.0 1.3 pad_maximum_fusion
  100.3 2.9 convolution_convert_fusion.4
  103.6 64.2 %all-gather.5.cloned.1.call-done = bf16[512,7168]{0,1:T(8,128)(2,1)} async-done(((bf16[512,448]{0,1:T(8,128)(2,1)}), bf16[512,7168]{0,1:T(8,128)(2,1)}) %all-gather.5.cloned.1.call-update) | async-done | bytes 7340048 | tf_op jit(solution)/shard_map/all_gather | solution.py:77
  167.8 6.9 %convolution_convert_fusion.3 = bf16[128,7168]{1,0:T(8,128)(2,1)} fusion(bf16[128,512]{0,1:T(8,128)(2,1)S(1)} %bitcast.88, bf16[512,7168]{0,1:T(8,128)(2,1)} %all-gather.5.cloned.1.call-done), kind=kOutput, calls=%fused_computation.4 | convolution fusion | flops 940441600 | bytes 9306112 | tf_op jit(solution)/shard_map/dot_general | solution.py:110
  176.3 112.2 %all-reduce.2.cloned.1.call-done = bf16[128,7168]{1,0:T(8,128)(2,1)} async-done(((bf16[128,7168]{1,0:T(8,128)(2,1)}), bf16[128,7168]{1,0:T(8,128)(2,1)}) %all-reduce.2.cloned.1.call-update) | async-done | bytes 1835024 | tf_op jit(solution)/shard_map/psum | solution.py:111
  288.5 2.8 fusion.1
  291.3 1.7 convolution_convert_fusion.1
  293.0 69.4 %all_to_all.10 = bf16[16,24,7168]{2,1,0:T(8,128)(2,1)S(1)} all-to-all(bf16[16,24,7168]{2,1,0:T(8,128)(2,1)S(1)} %bitcast.85), channel_id=1, replica_groups=mesh['dp'=16,'ep'=8,'tp'=2] {'dp'}, dimensions={0} | all-to-all | bytes 11010048 | tf_op jit(solution)/shard_map/all_to_all | solution.py:123
  362.5 2.4 copy-done.1
  364.8 1.6 fusion.8
  366.4 11.4 %convolution_convert_fusion = bf16[384,7168]{1,0:T(8,128)(2,1)} fusion(bf16[1,128,7168]{2,1,0:T(8,128)(2,1)S(1)} %copy-done, bf16[384,7168]{1,0:T(8,128)(2,1)} %bitcast.84, bf16[1,7168,128]{2,1,0:T(8,128)(2,1)} %param.26, f32[384,128]{1,0:T(8,128)S(1)} %fusion.8), kind=kOutput, calls=%fused_computation.1 | convolution fusion | flops 1412333568 | bytes 14876672 | tf_op jit(solution)/shard_map/dot_general | solution.py:46
  377.9 4.9 all-to-all-start.1
  382.9 66.4 %all-to-all-done.1 = bf16[16,24,7168]{2,1,0:T(8,128)(2,1)} async-done(((bf16[16,24,7168]{2,1,0:T(8,128)(2,1)}), bf16[16,24,7168]{2,1,0:T(8,128)(2,1)}, u32[]{:S(2)}, u32[]{:S(2)}) %all-to-all-start.1) | async-done | bytes 5505056 | tf_op jit(solution)/shard_map/all_to_all | solution.py:127
  449.3 5.0 convolution_convert_fusion.2
  454.3 80.9 %reduce-scatter.2.cloned.1.call-done = bf16[8,7168]{1,0:T(8,128)(2,1)} async-done(((bf16[128,7168]{1,0:T(8,128)(2,1)}), bf16[8,7168]{1,0:T(8,128)(2,1)}) %reduce-scatter.2.cloned.1.call-update) | async-done | bytes 114704 | tf_op jit(solution)/shard_map/reduce_scatter | solution.py:129
  535.2 1.6 add_convert_fusion.1
  (60 shorter events, 4.7 us)
Async XLA Ops:
  6.5 359.9 %copy-start = (bf16[1,128,7168]{2,1,0:T(8,128)(2,1)S(1)}, bf16[1,128,7168]{2,1,0:T(8,128)(2,1)}, u32[]{:S(2)}) copy-start(bf16[1,128,7168]{2,1,0:T(8,128)(2,1)} %param.27) | copy-start | bytes 5505028
  6.5 3.1 copy-start.10
  6.5 8.6 %copy-start.9 = (s32[64]{0:T(128)S(1)}, s32[64]{0:T(128)}, u32[]{:S(2)}) copy-start(s32[64]{0:T(128)} %param.17) | copy-start | bytes 772
  6.5 87.9 %all-gather.3.cloned.1.call-start = ((), (), s32[]{:S(2)}) async-start(), calls=%async_computation.3 | async-start | bytes 10027008 | tf_op jit(solution)/shard_map/all_gather | solution.py:78
  8.8 159.0 %all-gather.5.cloned.1.call-start = ((), (), s32[]{:S(2)}) async-start(), calls=%async_computation.4 | async-start | bytes 7798784 | tf_op jit(solution)/shard_map/all_gather | solution.py:77
  9.6 278.9 %all-reduce.2.cloned.1.call-start = ((), (), s32[]{:S(2)}) async-start(), calls=%async_computation.5 | async-start | bytes 3670016 | tf_op jit(solution)/shard_map/psum | solution.py:111
  95.9 3.1 copy-start.6
  97.8 0.9 copy-start.4
  100.3 2.9 copy-start.5
  167.8 6.9 %copy-start.8 = (s32[128,2]{0,1:T(2,128)S(1)}, s32[128,2]{0,1:T(2,128)}, u32[]{:S(2)}) copy-start(s32[128,2]{0,1:T(2,128)} %param.23) | copy-start | bytes 3076
  167.8 8.4 %copy-start.7 = (bf16[7168]{0:T(1024)(128)(2,1)S(1)}, bf16[7168]{0:T(1024)(128)(2,1)}, u32[]{:S(2)}) copy-start(bf16[7168]{0:T(1024)(128)(2,1)} %param.22) | copy-start | bytes 43012
  291.3 1.7 copy-start.2
  293.0 71.8 %copy-start.3 = (bf16[1,7168,128]{2,1,0:T(8,128)(2,1)S(1)}, bf16[1,7168,128]{2,1,0:T(8,128)(2,1)}, u32[]{:S(2)}) copy-start(bf16[1,7168,128]{2,1,0:T(8,128)(2,1)} %param.25) | copy-start | bytes 5505028
  362.4 2.4 copy-start.1
  377.9 5.0 copy-start.11
  377.9 71.4 %all-to-all-start.1 = ((bf16[16,24,7168]{2,1,0:T(8,128)(2,1)}), bf16[16,24,7168]{2,1,0:T(8,128)(2,1)}, u32[]{:S(2)}, u32[]{:S(2)}) async-start(bf16[16,24,7168]{2,1,0:T(8,128)(2,1)} %bitcast.86), calls=%async_computation.1 | async-start | bytes 11010048 | tf_op jit(solution)/shard_map/all_to_all | solution.py:127
  382.8 152.4 %reduce-scatter.2.cloned.1.call-start = ((), (), s32[]{:S(2)}) async-start(), calls=%async_computation.6 | async-start | bytes 1949696 | tf_op jit(solution)/shard_map/reduce_scatter | solution.py:129
Sparse Core Ops, SparseCore 0:
  9.8 84.5 all-gather.2
  96.9 70.8 all-gather.4
  174.8 113.6 all-reduce.1
  454.4 80.7 reduce-scatter.1
where the time goes:
time: 546 us; the launch traced here: 543 us
  waiting for transfers between devices  401 us (73%)
  blocking collectives  69.4 us (13%)
  matrix products  31.7 us (6%)
  between operations  15.8 us (3%)
  local copies, waits for them, and re-layouts  11.1 us (2%)
  other arithmetic  8.97 us (2%)
    psum x1, waiting for transfers between devices, per_device(): lax.psum(partial_sum.astype(jnp.bfloat16), ('ep', 'tp')).astype(jnp.float32)  112 us
    reduce_scatter x1, waiting for transfers between devices, per_device(): lax.psum_scatter(jnp.dot(combiner, flat_back, preferred_element_type=jnp....  80.9 us
    all_gather x1, waiting for transfers between devices, per_device(): lax.all_gather(moving, 'dp', axis=0, tiled=True)  77 us
    all_to_all x1, blocking collectives, per_device(): lax.all_to_all(outgoing, 'dp', split_axis=0, concat_axis=0, tiled=True)  69.4 us
    all_to_all x1, waiting for transfers between devices, per_device(): lax.all_to_all(pieces, 'dp', split_axis=0, concat_axis=0, tiled=True)  66.4 us
    all_gather x1, waiting for transfers between devices, per_device(): lax.all_gather(out_weight, 'dp', axis=1, tiled=True)  64.2 us
    dot_general x1, matrix products, expert_pieces(): jnp.dot(hidden, down_weight[0], preferred_element_type=jnp.float32)  11.4 us
  transfers between devices with their start and end apart: 5, of which 5 were waited for; matrix products, arithmetic and copies ran while one was open for 3% of the time, Pallas kernels for 0%

commit v1 on v0

v1 whole, which is shorter than its diff:
```python
import jax
import jax.numpy as jnp
from jax import lax
from jax.sharding import Mesh, PartitionSpec as P

score_scale = 192.0 ** (-0.5)
norm_eps = 1e-06
DP = ("dx", "dy")
MEM = ("ep", "tp")
bf16 = jnp.bfloat16
f32 = jnp.float32


def attend(grouped, keys, lengths, prefix_rows, latent_width):
    span_rows = grouped.shape[1]
    scores = jnp.einsum("jthc,jkc->jthk", grouped, keys, preferred_element_type=f32) * score_scale
    key_index = jnp.arange(keys.shape[1], dtype=jnp.int32)
    query_index = jnp.arange(span_rows, dtype=jnp.int32)
    in_prefix = (key_index < prefix_rows) & (key_index < lengths[:, None])
    in_span = (key_index[None, :] >= prefix_rows) & (
        key_index[None, :] - prefix_rows <= query_index[:, None]
    )
    allowed = (in_prefix[:, None, :] | in_span)[:, :, None, :]
    scores = jnp.where(allowed, scores, -jnp.inf)
    highest = jnp.max(scores, axis=-1, keepdims=True)
    raised = jnp.exp(scores - highest)
    weights = (raised / jnp.sum(raised, axis=-1, keepdims=True)).astype(bf16)
    return jnp.einsum(
        "jthk,jkc->jthc", weights, keys[:, :, :latent_width], preferred_element_type=f32
    ).astype(bf16)


def slots_of(route_rows, experts, capacity):
    top_k = route_rows.shape[1]
    flat_routes = route_rows.reshape(-1)
    hits = (flat_routes[:, None] == jnp.arange(experts, dtype=jnp.int32)[None, :]).astype(jnp.int32)
    earlier = jnp.cumsum(hits, axis=0) - hits
    position = jnp.sum(earlier * hits, axis=1)
    return (flat_routes * capacity + position).reshape(-1, top_k).T


def per_device(
    queries,
    cache,
    span_latent,
    prefix_len,
    destination,
    uv_weight,
    out_weight,
    residual,
    norm_gain,
    routes,
    route_weight,
    gate_weight,
    up_weight,
    down_weight,
):
    requests, prefix_rows, cached_width = cache.shape
    span_rows = span_latent.shape[1]
    tok_rows, heads_here = queries.shape[0], queries.shape[1]
    latent_width, value_width = uv_weight.shape[1], uv_weight.shape[2]
    model_width = residual.shape[1]
    nx, ny = lax.axis_size("dx"), lax.axis_size("dy")
    rank_count = nx * ny
    members = lax.axis_size(MEM)
    my_rank = lax.axis_index(DP)
    member = lax.axis_index(MEM)
    core = lax.axis_index("tp")
    col = model_width // members
    core_swap = [(0, 1), (1, 0)]
    swap = [
        (x * members + a * ny + b, a * members + x * ny + b)
        for x in range(nx)
        for a in range(nx)
        for b in range(ny)
    ]
    swap_axes = ("dx", "ep", "tp")

    ranks = jnp.arange(rank_count, dtype=jnp.int32)
    source_first = jnp.sum(ranks * (destination[0] == my_rank).astype(jnp.int32))
    source_second = jnp.sum(ranks * (destination[1] == my_rank).astype(jnp.int32))
    part = prefix_rows // members
    moving = lax.dynamic_slice_in_dim(cache[requests - 2 :], member * part, part, 1)
    arrived = lax.all_to_all(
        jnp.broadcast_to(moving[None], (rank_count,) + moving.shape), DP, 0, 0, tiled=True
    )
    chosen = jnp.stack(
        [
            lax.dynamic_index_in_dim(arrived[:, 0], source_first, 0, keepdims=False),
            lax.dynamic_index_in_dim(arrived[:, 1], source_second, 0, keepdims=False),
        ]
    )
    moved = lax.all_gather(chosen, MEM, axis=1, tiled=True)
    own_len = lax.dynamic_slice_in_dim(prefix_len, my_rank * requests, requests)
    moved_first = lax.dynamic_index_in_dim(prefix_len, source_first * requests + requests - 2, 0)
    moved_second = lax.dynamic_index_in_dim(prefix_len, source_second * requests + requests - 1, 0)

    out_cols = lax.all_gather(out_weight, "dy", axis=0)
    down_cols = lax.all_to_all(
        down_weight[0].reshape(-1, members, col).transpose(1, 0, 2), MEM, 0, 0, tiled=True
    )
    residual_t = lax.ppermute(
        lax.dynamic_slice_in_dim(residual, member * col, col, 1), swap_axes, swap
    )
    capacity = max(2, 3 * tok_rows * routes.shape[1] // (2 * rank_count))
    slots = slots_of(routes, rank_count, capacity)
    slots_t = lax.ppermute(slots, swap_axes, swap)

    grouped = queries.reshape(requests, span_rows, heads_here, cached_width)
    keys_own = jnp.concatenate([cache[: requests - 2], span_latent[: requests - 2]], axis=1)
    keys_moved = jnp.concatenate([moved, span_latent[requests - 2 :]], axis=1)
    latent_own = attend(
        grouped[: requests - 2], keys_own, own_len[: requests - 2], prefix_rows, latent_width
    )
    latent_moved = attend(
        grouped[requests - 2 :],
        keys_moved,
        jnp.concatenate([moved_first, moved_second]),
        prefix_rows,
        latent_width,
    )
    latent_out = jnp.concatenate([latent_own, latent_moved], axis=0)
    latent_out = latent_out.reshape(tok_rows, heads_here, latent_width)
    values = jnp.einsum("thc,hcv->thv", latent_out, uv_weight, preferred_element_type=f32)
    values = values.astype(bf16).reshape(tok_rows, heads_here * value_width)

    values_x = lax.all_gather(values, "dx", axis=0)
    half = ny // 2
    out_cols = out_cols.reshape((half, 2) + out_weight.shape)
    weight_mine = lax.dynamic_index_in_dim(out_cols, core, 1, keepdims=False)
    weight_other = lax.dynamic_index_in_dim(out_cols, 1 - core, 1, keepdims=False)
    sent = jnp.einsum("atk,bkc->abtc", values_x, weight_other, preferred_element_type=f32)
    sent = lax.ppermute(sent.astype(bf16), "tp", core_swap)
    kept = jnp.einsum("atk,bkc->abtc", values_x, weight_mine, preferred_element_type=f32)
    shares = (kept + sent.astype(f32)).astype(bf16).reshape(nx * half, tok_rows, col)
    shares = lax.all_to_all(shares, "ep", 0, 0, tiled=True)
    attended = jnp.sum(shares.astype(f32), axis=0)
    mixed_t = (residual_t.astype(f32) + attended).astype(bf16)
    mixed = lax.ppermute(mixed_t, swap_axes, swap)

    slot_index = jnp.arange(rank_count * capacity, dtype=jnp.int32)
    placer = jnp.any(slot_index[:, None, None] == slots_t[None], axis=1).astype(bf16)
    outgoing = jnp.dot(placer, mixed_t, preferred_element_type=f32).astype(bf16)
    outgoing = outgoing.reshape(rank_count, capacity, col)
    received = lax.all_to_all(outgoing, DP, 0, 0, tiled=True)
    received = received.reshape(nx, ny, capacity, col).transpose(1, 2, 0, 3)
    received = received.reshape(ny * capacity, nx * col)
    rows_in = lax.all_gather(received, MEM, axis=0)
    rows_in = rows_in.reshape(nx, ny, ny * capacity, nx * col)

    gain = norm_gain.astype(f32)[:, None]
    weight_in = jnp.concatenate([gate_weight[0], up_weight[0]], axis=1)
    weight_in = (weight_in.astype(f32) * gain).astype(bf16)
    weight_in = weight_in.reshape(nx, ny, col, -1).transpose(1, 0, 2, 3)
    weight_in = weight_in.reshape(ny, nx * col, -1)
    widened = rows_in.astype(f32)
    mean_square = jnp.sum(widened * widened, axis=(1, 3)) / model_width
    factor = lax.rsqrt(mean_square + norm_eps)[..., None]
    proj = jnp.einsum("abrk,bkf->arf", rows_in, weight_in, preferred_element_type=f32) * factor
    ff = gate_weight.shape[2]
    hidden = (jax.nn.silu(proj[..., :ff]) * proj[..., ff:]).astype(bf16)
    hidden = hidden.reshape(rank_count * capacity, ff)
    hidden_all = lax.all_gather(hidden, MEM, axis=0)
    expert_out = jnp.einsum("mrf,mfc->rc", hidden_all, down_cols, preferred_element_type=f32)
    expert_out = expert_out.astype(bf16).reshape(rank_count, capacity, col)

    returned = lax.all_to_all(expert_out, DP, 0, 0, tiled=True)
    returned = returned.reshape(rank_count * capacity, col)
    matches = slots[:, :, None] == slot_index[None, None, :]
    combiner = jnp.sum(
        jnp.where(matches, route_weight.T[:, :, None], jnp.zeros((), route_weight.dtype)), axis=0
    )
    moe = jnp.dot(combiner, returned, preferred_element_type=f32)
    total = (mixed.astype(f32) + moe).astype(bf16)
    total = lax.all_to_all(total.reshape(members, tok_rows // members, col), MEM, 0, 0, tiled=True)
    return total.transpose(1, 0, 2).reshape(tok_rows // members, model_width)


def solution(mesh):
    dp, ep, tp = mesh.devices.shape
    nx = 1
    while nx * nx < dp:
        nx *= 2
    grid = Mesh(mesh.devices.reshape(nx, dp // nx, ep, tp), DP + MEM)
    in_specs = (
        P(DP, MEM, None),
        P(DP, None, None),
        P(DP, None, None),
        P(),
        P(),
        P(MEM, None, None),
        P(MEM, DP),
        P(DP, None),
        P(),
        P(DP, None),
        P(DP, None),
        P(DP, None, MEM),
        P(DP, None, MEM),
        P(DP, MEM, None),
    )
    out_specs = P(DP + MEM, None)
    return jax.shard_map(
        per_device, mesh=grid, in_specs=in_specs, out_specs=out_specs, check_vma=False
    )
```

time: 546 us -> 323 us (0.59)
  waiting for transfers between devices: 401 us -> 136 us
  starting transfers between devices: 5.04 us -> 31.3 us
  local copies, waits for them, and re-layouts: 11.1 us -> 34.1 us
  matrix products: 31.7 us -> 21.3 us
    psum x1 -> x0, waiting for transfers between devices: 112 us -> none  [per_device(): lax.psum(partial_sum.astype(jnp.bfloat16), ('ep', 'tp')).astype(jnp.float32)]
    reduce_scatter x1 -> x0, waiting for transfers between devices: 80.9 us -> none  [per_device(): lax.psum_scatter(jnp.dot(combiner, flat_back, preferred_element_type=jnp....]
    all_gather x2 -> x3, waiting for transfers between devices: 141 us -> 101 us  [the longest x1 64.4 us: per_device(): rows_in = lax.all_gather(received, MEM, axis=0)]
    all_to_all x1 -> x4, waiting for transfers between devices: 66.4 us -> 31.5 us  [the longest x1 23 us: per_device(): shares = lax.all_to_all(shares, 'ep', 0, 0, tiled=True)]
    all_gather x0 -> x2, blocking collectives: none -> 33.9 us  [the longest x1 22.5 us: per_device(): moved = lax.all_gather(chosen, MEM, axis=1, tiled=True)]
    all_to_all x1 -> x2, blocking collectives: 69.4 us -> 35.8 us  [the longest x1 18.9 us: per_device(): lax.all_to_all(total.reshape(members, tok_rows // members, col), MEM, 0,...]
    all_to_all x1 -> x4, starting transfers between devices: 4.92 us -> 26.5 us  [the longest x1 8.81 us: per_device(): lax.all_to_all(down_weight[0].reshape(-1, members, col).transpose(1, 0, 2...]
    dot_general x7 -> x10, matrix products: 31.3 us -> 18 us  [the longest x1 5.26 us: per_device(): jnp.einsum('abrk,bkf->arf', rows_in, weight_in, preferred_element_type=f32)]
  transfers between devices with their start and end apart: 5 -> 11, of which waited for: 5 -> 5; matrix products, arithmetic and copies ran while one was open for 3% -> 13% of each run, Pallas kernels for 0% -> 0%
where the time goes in v1:
time: 323 us; the launch traced here: 321 us
  waiting for transfers between devices  136 us (42%)
  blocking collectives  69.7 us (22%)
  local copies, waits for them, and re-layouts  34.1 us (11%)
  starting transfers between devices  31.3 us (10%)
  matrix products  21.3 us (7%)
  between operations  18.4 us (6%)
  other arithmetic  10.9 us (3%)
    all_gather x1, waiting for transfers between devices, per_device(): rows_in = lax.all_gather(received, MEM, axis=0)  64.4 us
    all_gather x1, waiting for transfers between devices, per_device(): hidden_all = lax.all_gather(hidden, MEM, axis=0)  37 us
    all_to_all x1, waiting for transfers between devices, per_device(): shares = lax.all_to_all(shares, 'ep', 0, 0, tiled=True)  23 us
    all_gather x1, blocking collectives, per_device(): moved = lax.all_gather(chosen, MEM, axis=1, tiled=True)  22.5 us
    all_to_all x1, blocking collectives, per_device(): lax.all_to_all(total.reshape(members, tok_rows // members, col), MEM, 0,...  18.9 us
    all_to_all x1, blocking collectives, per_device(): received = lax.all_to_all(outgoing, DP, 0, 0, tiled=True)  16.9 us
    all_gather x1, blocking collectives, per_device(): values_x = lax.all_gather(values, 'dx', axis=0)  11.4 us
    unnamed x40, local copies, waits for them, and re-layouts  8.93 us
  transfers between devices with their start and end apart: 11, of which 5 were waited for; matrix products, arithmetic and copies ran while one was open for 13% of the time, Pallas kernels for 0%

profile of v1, /device:TPU:1, one launch (start us, length us, event | category | flops | bytes accessed | tf_op | source)
XLA Modules:
  0.0 321.4 jit_solution(11381347833820795534)
XLA Ops:
  6.5 2.3 fusion.66
  10.0 7.6 %all-to-all-start = ((bf16[16,2,16,576]{3,2,1,0:T(8,128)(2,1)}), bf16[16,2,16,576]{3,2,1,0:T(8,128)(2,1)S(1)}, u32[]{:S(2)}, u32[]{:S(2)}) async-start(bf16[16,2,16,576]{3,2,1,0:T(8,128)(2,1)} %broadcast_in_dim.31), calls=%async_computation | async-start | bytes 1310720 | tf_op jit(solution)/shard_map/all_to_all | solution.py:84
  28.5 2.4 fusion.76
  34.7 2.4 fusion.14
  37.1 2.4 convolution_convert_fusion.3
  39.7 22.5 %all_gather.20 = bf16[2,256,576]{2,1,0:T(8,128)(2,1)S(1)} all-gather(bf16[2,16,576]{2,1,0:T(8,128)(2,1)S(1)} %pad_maximum_fusion.3), channel_id=1, replica_groups=mesh['dx'=4,'dy'=4,'ep'=8,'tp'=2] {'ep','tp'}, dimensions={1}, use_global_device_ids=true | all-gather | bytes 626688 | tf_op jit(solution)/shard_map/all_gather | solution.py:93
  67.2 11.4 %all_gather.21 = bf16[4,128,512]{2,1,0:T(8,128)(2,1)S(1)} all-gather(bf16[1,128,512]{2,1,0:T(8,128)(2,1)S(1)} %copy.143), channel_id=1, replica_groups=mesh['dx'=4,'dy'=4,'ep'=8,'tp'=2] {'dx'}, dimensions={0}, use_global_device_ids=true | all-gather | bytes 655360 | tf_op jit(solution)/shard_map/all_gather | solution.py:127
  78.6 5.5 %reshape.197 = bf16[2,2,512,448]{2,1,0,3:T(2,128)(2,1)} reshape(bf16[2048,448]{0,1:T(8,128)(2,1)} %all-gather.9.cloned.1.call-done) | data formatting | bytes 3670016 | tf_op jit(solution)/shard_map/reshape | solution.py:129
  84.1 5.8 %constant_dynamic-slice_fusion.2 = (bf16[2,1,512,448]{2,1,0,3:T(2,128)(2,1)S(1)}, bf16[2,1,512,448]{2,1,0,3:T(2,128)(2,1)S(1)}) fusion(bf16[2,2,512,448]{2,1,0,3:T(2,128)(2,1)} %reshape.197, s32[]{:T(128)S(6)} %select_n.42, s32[]{:T(128)S(6)} %select_n.51), kind=kLoop, calls=%fused_computation.88 | loop fusion | bytes 3670024 | tf_op jit(solution)/shard_map/jit(dynamic_index_in_dim)/dynamic_slice | solution.py:130
  90.6 2.7 collective-permute-start.1
  97.1 3.6 %all-to-all-start.1 = ((bf16[8,128,448]{1,2,0:T(8,128)(2,1)}), bf16[8,128,448]{1,2,0:T(8,128)(2,1)S(1)}, u32[]{:S(2)}, u32[]{:S(2)}) async-start(bf16[8,128,448]{1,2,0:T(8,128)(2,1)} %bitcast.28), calls=%async_computation.1 | async-start | bytes 1835008 | tf_op jit(solution)/shard_map/all_to_all | solution.py:136
  103.9 23.0 %all-to-all-done.1 = bf16[8,128,448]{1,2,0:T(8,128)(2,1)S(1)} async-done(((bf16[8,128,448]{1,2,0:T(8,128)(2,1)}), bf16[8,128,448]{1,2,0:T(8,128)(2,1)S(1)}, u32[]{:S(2)}, u32[]{:S(2)}) %all-to-all-start.1) | async-done | bytes 917536 | tf_op jit(solution)/shard_map/all_to_all | solution.py:136
  127.6 16.9 %all_to_all.30 = bf16[16,24,448]{2,1,0:T(8,128)(2,1)S(1)} all-to-all(bf16[16,24,448]{2,1,0:T(8,128)(2,1)S(1)} %bitcast.159), channel_id=1, replica_groups=mesh['dx'=4,'dy'=4,'ep'=8,'tp'=2] {'dx','dy'}, dimensions={0} | all-to-all | bytes 688128 | tf_op jit(solution)/shard_map/all_to_all | solution.py:145
  145.9 3.9 %copy.153 = bf16[1,128,7168]{1,2,0:T(8,128)(2,1)} copy(bf16[1,128,7168]{2,1,0:T(8,128)(2,1)} %param.27) | data formatting | bytes 3670016 | tf_op args[13]
  149.8 8.8 %all-to-all-start.3 = ((bf16[16,128,448]{1,2,0:T(8,128)(2,1)}), bf16[16,128,448]{1,2,0:T(8,128)(2,1)}, u32[]{:S(2)}, u32[]{:S(2)}) async-start(bf16[16,128,448]{1,2,0:T(8,128)(2,1)} %bitcast.153), calls=%async_computation.3 | async-start | bytes 3670016 | tf_op jit(solution)/shard_map/all_to_all | solution.py:99
  158.8 2.6 fusion.2
  163.6 64.4 %all-gather.5.cloned.1.call-done = bf16[16,96,1792]{2,1,0:T(8,128)(2,1)} async-done(((bf16[1,96,1792]{2,1,0:T(8,128)(2,1)}), bf16[16,96,1792]{2,1,0:T(8,128)(2,1)}) %all-gather.5.cloned.1.call-update) | async-done | bytes 5505040 | tf_op jit(solution)/shard_map/all_gather | solution.py:148
  228.0 3.7 %multiply_reduce_fusion = f32[16,96]{1,0:T(8,128)S(1)} fusion(bf16[16,96,1792]{2,1,0:T(8,128)(2,1)} %all-gather.5.cloned.1.call-done), kind=kLoop, calls=%fused_computation.2 | loop fusion | flops 8256000 | bytes 5511168 | tf_op jit(solution)/shard_map/reduce_sum | solution.py:157
  231.8 5.3 %fusion.10 = f32[4,96,256]{2,1,0:T(8,128)S(1)} fusion(bf16[4,4,96,1792]{3,2,1,0:T(8,128)(2,1)} %bitcast.154, bf16[4,1792,256,1]{2,1,0,3:T(8,128)(2,1)} %bitcast.155, f32[4,96]{1,0:T(4,128)S(1)} %add_rsqrt_fusion), kind=kOutput, calls=%fused_computation.20 | convolution fusion | flops 1409384448 | bytes 9569792 | tf_op jit(solution)/shard_map/abrk,bkf->arf/dot_general | solution.py:159
  237.8 37.0 %all-gather.7.cloned.1.call-done = bf16[16,384,128]{2,1,0:T(8,128)(2,1)} async-done(((bf16[1,384,128]{2,1,0:T(8,128)(2,1)}), bf16[16,384,128]{2,1,0:T(8,128)(2,1)}) %all-gather.7.cloned.1.call-update) | async-done | bytes 1572880 | tf_op jit(solution)/shard_map/all_gather | solution.py:163
  274.8 3.1 fusion.7
  278.8 6.5 %all-to-all-start.4 = ((bf16[16,24,448]{2,1,0:T(8,128)(2,1)}), bf16[16,24,448]{2,1,0:T(8,128)(2,1)S(1)}, u32[]{:S(2)}, u32[]{:S(2)}) async-start(bf16[16,24,448]{2,1,0:T(8,128)(2,1)} %bitcast.48), calls=%async_computation.4 | async-start | bytes 786432 | tf_op jit(solution)/shard_map/all_to_all | solution.py:167
  286.2 8.5 %all-to-all-done.4 = bf16[16,24,448]{2,1,0:T(8,128)(2,1)S(1)} async-done(((bf16[16,24,448]{2,1,0:T(8,128)(2,1)}), bf16[16,24,448]{2,1,0:T(8,128)(2,1)S(1)}, u32[]{:S(2)}, u32[]{:S(2)}) %all-to-all-start.4) | async-done | bytes 344096 | tf_op jit(solution)/shard_map/all_to_all | solution.py:167
  295.2 18.9 %all_to_all.31 = bf16[16,8,448]{2,1,0:T(8,128)(2,1)S(1)} all-to-all(bf16[16,8,448]{2,1,0:T(8,128)(2,1)S(1)} %bitcast.163), channel_id=1, replica_groups=mesh['dx'=4,'dy'=4,'ep'=8,'tp'=2] {'ep','tp'}, dimensions={0} | all-to-all | bytes 229376 | tf_op jit(solution)/shard_map/all_to_all | solution.py:175
  (114 shorter events, 31.9 us)
Async XLA Ops:
  6.5 96.4 %copy-start = (bf16[128,7168]{1,0:T(8,128)(2,1)S(1)}, bf16[128,7168]{1,0:T(8,128)(2,1)}, u32[]{:S(2)}) copy-start(bf16[128,7168]{1,0:T(8,128)(2,1)} %param.21) | copy-start | bytes 5505028
  8.8 9.6 %copy-start.15 = (s32[2,16]{1,0:T(2,128)S(1)}, s32[2,16]{1,0:T(2,128)}, u32[]{:S(2)}) copy-start(s32[2,16]{1,0:T(2,128)} %param.18) | copy-start | bytes 388
  8.8 11.5 %copy-start.7 = (bf16[4,32,576]{2,1,0:T(8,128)(2,1)S(1)}, bf16[4,32,576]{2,1,0:T(8,128)(2,1)}, u32[]{:S(2)}) copy-start(bf16[4,32,576]{2,1,0:T(8,128)(2,1)} %param.16) | copy-start | bytes 442372
  8.8 12.2 %copy-start.1 = (bf16[128,4,576]{0,2,1:T(8,128)(2,1)S(1)}, bf16[128,4,576]{0,2,1:T(8,128)(2,1)}, u32[]{:S(2)}) copy-start(bf16[128,4,576]{0,2,1:T(8,128)(2,1)} %param.14) | copy-start | bytes 1769476
  10.0 29.5 %all-to-all-start = ((bf16[16,2,16,576]{3,2,1,0:T(8,128)(2,1)}), bf16[16,2,16,576]{3,2,1,0:T(8,128)(2,1)S(1)}, u32[]{:S(2)}, u32[]{:S(2)}) async-start(bf16[16,2,16,576]{3,2,1,0:T(8,128)(2,1)} %broadcast_in_dim.31), calls=%async_computation | async-start | bytes 1310720 | tf_op jit(solution)/shard_map/all_to_all | solution.py:84
  17.6 61.0 %all-gather.9.cloned.1.call-start = ((), (), s32[]{:S(2)}) async-start(), calls=%async_computation.8 | async-start | bytes 2293760 | tf_op jit(solution)/shard_map/all_gather | solution.py:98
  21.0 7.5 %copy-start.9 = (bf16[2,32,576]{2,1,0:T(8,128)(2,1)S(1)}, bf16[2,32,576]{2,1,0:T(8,128)(2,1)}, u32[]{:S(2)}) copy-start(bf16[2,32,576]{2,1,0:T(8,128)(2,1)} %get-tuple-element.15) | copy-start | bytes 221188
  24.9 6.0 %copy-start.11 = (pred[2,32,288]{2,1,0:T(8,128)(4,1)}, pred[2,32,288]{2,1,0:T(8,128)(4,1)S(1)}, u32[]{:S(2)}) copy-start(pred[2,32,288]{2,1,0:T(8,128)(4,1)S(1)} %get-tuple-element.17) | copy-start | bytes 55300
  27.1 6.2 %copy-start.2 = (bf16[64,4,576]{0,2,1:T(8,128)(2,1)S(1)}, bf16[64,4,576]{0,2,1:T(8,128)(2,1)}, u32[]{:S(2)}) copy-start(bf16[64,4,576]{0,2,1:T(8,128)(2,1)} %get-tuple-element.14) | copy-start | bytes 884740
  28.4 4.8 %copy-start.5 = (bf16[64,4,576]{2,0,1:T(8,128)(2,1)}, bf16[64,4,576]{2,0,1:T(8,128)(2,1)S(1)}, u32[]{:S(2)}) copy-start(bf16[64,4,576]{2,0,1:T(8,128)(2,1)S(1)} %copy.168) | copy-start | bytes 884740
  39.5 22.6 %copy-start.8 = (bf16[2,32,576]{2,1,0:T(8,128)(2,1)S(1)}, bf16[2,32,576]{2,1,0:T(8,128)(2,1)}, u32[]{:S(2)}) copy-start(bf16[2,32,576]{2,1,0:T(8,128)(2,1)} %get-tuple-element.16) | copy-start | bytes 221188
  39.5 22.6 %copy-start.10 = (pred[2,32,288]{2,1,0:T(8,128)(4,1)S(1)}, pred[2,32,288]{2,1,0:T(8,128)(4,1)}, u32[]{:S(2)}) copy-start(pred[2,32,288]{2,1,0:T(8,128)(4,1)} %get-tuple-element.18) | copy-start | bytes 55300
  90.6 4.8 %collective-permute-start.1 = (bf16[4,2,128,448]{2,3,0,1:T(8,128)(2,1)S(1)}, bf16[4,2,128,448]{2,3,0,1:T(8,128)(2,1)S(1)}, u32[]{:S(2)}, u32[]{:S(2)}) collective-permute-start(bf16[4,2,128,448]{2,3,0,1:T(8,128)(2,1)S(1)} %fusion.4), channel_id=1, source_target_pairs={{0,1},{1,0},{2,3},{3,2},{4,5},{5,4},{6,7},{7,6},{8,9},{9,8},{10,11... | collective-permute-start | bytes 2752520 | tf_op jit(solution)/shard_map/ppermute | solution.py:133
  96.1 4.6 %copy-start.13 = (s32[128,2]{0,1:T(2,128)S(1)}, s32[128,2]{0,1:T(2,128)}, u32[]{:S(2)}) copy-start(s32[128,2]{0,1:T(2,128)} %param.23) | copy-start | bytes 3076
  97.1 29.9 %all-to-all-start.1 = ((bf16[8,128,448]{1,2,0:T(8,128)(2,1)}), bf16[8,128,448]{1,2,0:T(8,128)(2,1)S(1)}, u32[]{:S(2)}, u32[]{:S(2)}) async-start(bf16[8,128,448]{1,2,0:T(8,128)(2,1)} %bitcast.28), calls=%async_computation.1 | async-start | bytes 1835008 | tf_op jit(solution)/shard_map/all_to_all | solution.py:136
  100.6 127.4 %all-gather.5.cloned.1.call-start = ((), (), s32[]{:S(2)}) async-start(), calls=%async_computation.6 | async-start | bytes 5849088 | tf_op jit(solution)/shard_map/all_gather | solution.py:148
  102.2 1.6 collective-permute-start.3
  103.2 23.9 %collective-permute-start = (bf16[128,448]{0,1:T(8,128)(2,1)S(1)}, bf16[128,448]{0,1:T(8,128)(2,1)S(1)}, u32[]{:S(2)}, u32[]{:S(2)}) collective-permute-start(bf16[128,448]{0,1:T(8,128)(2,1)S(1)} %copy.165), channel_id=1, source_target_pairs={{0,0},{1,1},{2,2},{3,3},{4,64},{5,65},{6,66},{7,67},{8,128},{9,129... | collective-permute-start | bytes 344072 | tf_op jit(solution)/shard_map/ppermute | solution.py:102
  149.8 8.9 %copy-start.12 = (bf16[7168]{0:T(1024)(128)(2,1)S(1)}, bf16[7168]{0:T(1024)(128)(2,1)}, u32[]{:S(2)}) copy-start(bf16[7168]{0:T(1024)(128)(2,1)} %param.22) | copy-start | bytes 43012
  149.8 88.0 %all-to-all-start.3 = ((bf16[16,128,448]{1,2,0:T(8,128)(2,1)}), bf16[16,128,448]{1,2,0:T(8,128)(2,1)}, u32[]{:S(2)}, u32[]{:S(2)}) async-start(bf16[16,128,448]{1,2,0:T(8,128)(2,1)} %bitcast.153), calls=%async_computation.3 | async-start | bytes 3670016 | tf_op jit(solution)/shard_map/all_to_all | solution.py:99
  158.6 116.2 %all-gather.7.cloned.1.call-start = ((), (), s32[]{:S(2)}) async-start(), calls=%async_computation.7 | async-start | bytes 1671168 | tf_op jit(solution)/shard_map/all_gather | solution.py:163
  237.8 47.6 %copy-start.16 = (bf16[128,2]{0,1:T(2,128)(2,1)S(1)}, bf16[128,2]{0,1:T(2,128)(2,1)}, u32[]{:S(2)}) copy-start(bf16[128,2]{0,1:T(2,128)(2,1)} %param.24) | copy-start | bytes 1540
  278.8 15.9 %all-to-all-start.4 = ((bf16[16,24,448]{2,1,0:T(8,128)(2,1)}), bf16[16,24,448]{2,1,0:T(8,128)(2,1)S(1)}, u32[]{:S(2)}, u32[]{:S(2)}) async-start(bf16[16,24,448]{2,1,0:T(8,128)(2,1)} %bitcast.48), calls=%async_computation.4 | async-start | bytes 786432 | tf_op jit(solution)/shard_map/all_to_all | solution.py:167
  285.5 9.5 %collective-permute-start.2 = (bf16[128,448]{0,1:T(8,128)(2,1)S(1)}, bf16[128,448]{0,1:T(8,128)(2,1)S(1)}, u32[]{:S(2)}, u32[]{:S(2)}) collective-permute-start(bf16[128,448]{0,1:T(8,128)(2,1)S(1)} %add_convert_fusion.1), channel_id=1, source_target_pairs={{0,0},{1,1},{2,2},{3,3},{4,64},{5,65},{6,66},{7,67},{8,128},{9,129... | collective-permute-start | bytes 344072 | tf_op jit(solution)/shard_map/ppermute | solution.py:139
  (4 other events, 11.0 us)
Sparse Core Ops, SparseCore 0:
  20.3 34.6 all-gather.8
  146.1 81.9 all-gather.4
  237.9 36.8 all-gather.6

commit v2 on v1

--- a/solution.py
+++ b/solution.py
@@ -1,6 +1,10 @@
+import functools
+
 import jax
 import jax.numpy as jnp
 from jax import lax
+from jax.experimental import pallas as pl
+from jax.experimental.pallas import tpu as pltpu
 from jax.sharding import Mesh, PartitionSpec as P
 
 score_scale = 192.0 ** (-0.5)
@@ -37,6 +41,98 @@
     earlier = jnp.cumsum(hits, axis=0) - hits
     position = jnp.sum(earlier * hits, axis=1)
     return (flat_routes * capacity + position).reshape(-1, top_k).T
+
+
+def share_kernel(core_ref, values_ref, weight_ref, out_ref):
+    nx, _, rows, cols = out_ref.shape
+    product = jnp.dot(values_ref[...], weight_ref[0], preferred_element_type=f32)
+    out_ref[...] = product.astype(bf16).reshape(nx, 1, rows, cols)
+
+
+def share_sum_kernel(core_ref, values_ref, weight_ref, other_ref, out_ref):
+    nx, _, rows, cols = out_ref.shape
+    product = jnp.dot(values_ref[...], weight_ref[0], preferred_element_type=f32)
+    product = product.reshape(nx, 1, rows, cols) + other_ref[...].astype(f32)
+    out_ref[...] = product.astype(bf16)
+
+
+def project(core, values, weights, other=None):
+    blocks, depth, cols = weights.shape
+    half = blocks // 2
+    total = values.shape[0]
+    nx = blocks
+    rows = total // nx
+    piece = pl.BlockSpec((nx, 1, rows, cols), lambda i, c: (0, i, 0, 0))
+    in_specs = [
+        pl.BlockSpec((total, depth), lambda i, c: (0, 0)),
+        pl.BlockSpec((1, depth, cols), lambda i, c: (2 * i + c[0], 0, 0)),
+    ]
+    operands = [values, weights]
+    if other is not None:
+        in_specs.append(piece)
+        operands.append(other)
+    return pl.pallas_call(
+        share_kernel if other is None else share_sum_kernel,
+        out_shape=jax.ShapeDtypeStruct((nx, half, rows, cols), bf16),
+        grid_spec=pltpu.PrefetchScalarGridSpec(
+            num_scalar_prefetch=1, grid=(half,), in_specs=in_specs, out_specs=piece
+        ),
+        compiler_params=pltpu.CompilerParams(vmem_limit_bytes=32 << 20),
+        cost_estimate=pl.CostEstimate(
+            flops=2 * total * depth * cols * half,
+            bytes_accessed=2 * (total * depth + half * depth * cols + half * total * cols),
+            transcendentals=0,
+        ),
+    )(core, *operands)
+
+
+def hidden_kernel(width, rows_ref, weight_ref, out_ref, total, squares):
+    step = pl.program_id(0)
+    groups, _, rows, depth = rows_ref.shape
+    block = rows_ref[...].reshape(groups * rows, depth)
+    widened = block.astype(f32)
+    square = jnp.sum(widened * widened, axis=1, keepdims=True)
+    product = jnp.dot(block, weight_ref[0], preferred_element_type=f32)
+
+    @pl.when(step == 0)
+    def _():
+        total[...] = product
+        squares[...] = square
+
+    @pl.when(step > 0)
+    def _():
+        total[...] += product
+        squares[...] += square
+
+    @pl.when(step == pl.num_programs(0) - 1)
+    def _():
+        factor = lax.rsqrt(squares[...] / width + norm_eps)
+        ff = out_ref.shape[1]
+        gate = total[:, :ff] * factor
+        up = total[:, ff:] * factor
+        out_ref[...] = (gate / (1.0 + jnp.exp(-gate)) * up).astype(bf16)
+
+
+def hidden_of(rows_in, weight_in, width):
+    nx, ny, rows, depth = rows_in.shape
+    ff2 = weight_in.shape[2]
+    return pl.pallas_call(
+        functools.partial(hidden_kernel, width),
+        out_shape=jax.ShapeDtypeStruct((nx * rows, ff2 // 2), bf16),
+        grid=(ny,),
+        in_specs=[
+            pl.BlockSpec((nx, 1, rows, depth), lambda i: (0, i, 0, 0)),
+            pl.BlockSpec((1, depth, ff2), lambda i: (i, 0, 0)),
+        ],
+        out_specs=pl.BlockSpec((nx * rows, ff2 // 2), lambda i: (0, 0)),
+        scratch_shapes=[pltpu.VMEM((nx * rows, ff2), f32), pltpu.VMEM((nx * rows, 1), f32)],
+        compiler_params=pltpu.CompilerParams(vmem_limit_bytes=40 << 20),
+        cost_estimate=pl.CostEstimate(
+            flops=2 * nx * ny * rows * depth * ff2,
+            bytes_accessed=2 * (nx * ny * rows * depth + ny * depth * ff2),
+            transcendentals=nx * rows * ff2,
+        ),
+    )(rows_in, weight_in)
 
 
 def per_device(
@@ -106,6 +202,12 @@
     slots = slots_of(routes, rank_count, capacity)
     slots_t = lax.ppermute(slots, swap_axes, swap)
 
+    gain = norm_gain.astype(f32)[:, None]
+    weight_in = jnp.concatenate([gate_weight[0], up_weight[0]], axis=1)
+    weight_in = (weight_in.astype(f32) * gain).astype(bf16)
+    weight_in = weight_in.reshape(nx, ny, col, -1).transpose(1, 0, 2, 3)
+    weight_in = weight_in.reshape(ny, nx * col, -1)
+
     grouped = queries.reshape(requests, span_rows, heads_here, cached_width)
     keys_own = jnp.concatenate([cache[: requests - 2], span_latent[: requests - 2]], axis=1)
     keys_moved = jnp.concatenate([moved, span_latent[requests - 2 :]], axis=1)
@@ -124,15 +226,13 @@
     values = jnp.einsum("thc,hcv->thv", latent_out, uv_weight, preferred_element_type=f32)
     values = values.astype(bf16).reshape(tok_rows, heads_here * value_width)
 
-    values_x = lax.all_gather(values, "dx", axis=0)
-    half = ny // 2
-    out_cols = out_cols.reshape((half, 2) + out_weight.shape)
-    weight_mine = lax.dynamic_index_in_dim(out_cols, core, 1, keepdims=False)
-    weight_other = lax.dynamic_index_in_dim(out_cols, 1 - core, 1, keepdims=False)
-    sent = jnp.einsum("atk,bkc->abtc", values_x, weight_other, preferred_element_type=f32)
-    sent = lax.ppermute(sent.astype(bf16), "tp", core_swap)
-    kept = jnp.einsum("atk,bkc->abtc", values_x, weight_mine, preferred_element_type=f32)
-    shares = (kept + sent.astype(f32)).astype(bf16).reshape(nx * half, tok_rows, col)
+    values_x = lax.all_gather(values, "dx", axis=0).reshape(nx * tok_rows, -1)
+    core_at = jnp.reshape(core, (1,))
+    sent = lax.ppermute(project(1 - core_at, values_x, out_cols), "tp", core_swap)
+    shares = project(core_at, values_x, out_cols, sent).reshape(members // 2, tok_rows, col)
+    shares, down_cols, residual_t, slots_t, weight_in = lax.optimization_barrier(
+        (shares, down_cols, residual_t, slots_t, weight_in)
+    )
     shares = lax.all_to_all(shares, "ep", 0, 0, tiled=True)
     attended = jnp.sum(shares.astype(f32), axis=0)
     mixed_t = (residual_t.astype(f32) + attended).astype(bf16)
@@ -148,18 +248,7 @@
     rows_in = lax.all_gather(received, MEM, axis=0)
     rows_in = rows_in.reshape(nx, ny, ny * capacity, nx * col)
 
-    gain = norm_gain.astype(f32)[:, None]
-    weight_in = jnp.concatenate([gate_weight[0], up_weight[0]], axis=1)
-    weight_in = (weight_in.astype(f32) * gain).astype(bf16)
-    weight_in = weight_in.reshape(nx, ny, col, -1).transpose(1, 0, 2, 3)
-    weight_in = weight_in.reshape(ny, nx * col, -1)
-    widened = rows_in.astype(f32)
-    mean_square = jnp.sum(widened * widened, axis=(1, 3)) / model_width
-    factor = lax.rsqrt(mean_square + norm_eps)[..., None]
-    proj = jnp.einsum("abrk,bkf->arf", rows_in, weight_in, preferred_element_type=f32) * factor
-    ff = gate_weight.shape[2]
-    hidden = (jax.nn.silu(proj[..., :ff]) * proj[..., ff:]).astype(bf16)
-    hidden = hidden.reshape(rank_count * capacity, ff)
+    hidden = hidden_of(rows_in, weight_in, float(model_width))
     hidden_all = lax.all_gather(hidden, MEM, axis=0)
     expert_out = jnp.einsum("mrf,mfc->rc", hidden_all, down_cols, preferred_element_type=f32)
     expert_out = expert_out.astype(bf16).reshape(rank_count, capacity, col)

time: 323 us -> 339 us (1.050)
  blocking collectives: 69.7 us -> 99.4 us
  waiting for transfers between devices: 136 us -> 112 us
  starting transfers between devices: 31.3 us -> 40 us
  matrix products: 21.3 us -> 14.3 us
  Pallas kernels: 0 us -> 5.58 us
  local copies, waits for them, and re-layouts: 34.1 us -> 39 us
    all_gather x1, blocking collectives: 22.5 us -> 52.6 us  [per_device(): moved = lax.all_gather(chosen, MEM, axis=1, tiled=True)]
    all_gather x1, waiting for transfers between devices: 64.4 us -> 38.7 us  [per_device(): rows_in = lax.all_gather(received, MEM, axis=0)]
    unnamed x40 -> x46, local copies, waits for them, and re-layouts: 8.93 us -> 20 us
    dot_general x3 -> x0, matrix products: 6.63 us -> none  [the longest x1 5.26 us: per_device(): jnp.einsum('abrk,bkf->arf', rows_in, weight_in, preferred_element_type=f32)]
    dynamic_slice x1 -> x0, local copies, waits for them, and re-layouts: 5.83 us -> none  [per_device(): weight_mine = lax.dynamic_index_in_dim(out_cols, core, 1, keepdims=False)]
    pallas_call x0 -> x3, Pallas kernels: none -> 5.58 us  [the longest x1 3.57 us: hidden_of(): pl.pallas_call(functools.partial(hidden_kernel, width), out_shape=jax.Sha...]
    reshape x1 -> x0, local copies, waits for them, and re-layouts: 5.48 us -> none  [per_device(): out_cols = out_cols.reshape((half, 2) + out_weight.shape)]
    all_to_all x1, starting transfers between devices: 3.55 us -> 8.92 us  [per_device(): shares = lax.all_to_all(shares, 'ep', 0, 0, tiled=True)]
  transfers between devices with their start and end apart: 11 -> 11, of which waited for: 5 -> 4; matrix products, arithmetic and copies ran while one was open for 13% -> 12% of each run, Pallas kernels for 0% -> 1%
where the time goes in v2:
time: 339 us; the launch traced here: 337 us
  waiting for transfers between devices  112 us (33%)
  blocking collectives  99.4 us (29%)
  starting transfers between devices  40 us (12%)
  local copies, waits for them, and re-layouts  39 us (12%)
  between operations  18.7 us (6%)
  matrix products  14.3 us (4%)
  other arithmetic  8.65 us (3%)
  Pallas kernels  5.58 us (2%)
    all_gather x1, blocking collectives, per_device(): moved = lax.all_gather(chosen, MEM, axis=1, tiled=True)  52.6 us
    all_gather x1, waiting for transfers between devices, per_device(): rows_in = lax.all_gather(received, MEM, axis=0)  38.7 us
    all_gather x1, waiting for transfers between devices, per_device(): hidden_all = lax.all_gather(hidden, MEM, axis=0)  37.7 us
    all_to_all x1, waiting for transfers between devices, per_device(): shares = lax.all_to_all(shares, 'ep', 0, 0, tiled=True)  26.3 us
    unnamed x46, local copies, waits for them, and re-layouts  20 us
    all_to_all x1, blocking collectives, per_device(): lax.all_to_all(total.reshape(members, tok_rows // members, col), MEM, 0,...  18.9 us
    all_to_all x1, blocking collectives, per_device(): received = lax.all_to_all(outgoing, DP, 0, 0, tiled=True)  15.7 us
    all_gather x1, blocking collectives, per_device(): values_x = lax.all_gather(values, 'dx', axis=0).reshape(nx * tok_rows, -1)  12.2 us
  transfers between devices with their start and end apart: 11, of which 4 were waited for; matrix products, arithmetic and copies ran while one was open for 12% of the time, Pallas kernels for 1%

profile of v2, /device:TPU:1, one launch (start us, length us, event | category | flops | bytes accessed | tf_op | source)
XLA Modules:
  0.0 337.5 jit_solution(4157877374869752211)
XLA Ops:
  6.5 2.3 fusion.59
  10.0 7.6 %all-to-all-start = ((bf16[16,2,16,576]{3,2,1,0:T(8,128)(2,1)}), bf16[16,2,16,576]{3,2,1,0:T(8,128)(2,1)S(1)}, u32[]{:S(2)}, u32[]{:S(2)}) async-start(bf16[16,2,16,576]{3,2,1,0:T(8,128)(2,1)} %broadcast_in_dim.31), calls=%async_computation | async-start | bytes 1310720 | tf_op jit(solution)/shard_map/all_to_all | solution.py:180
  19.3 2.2 collective-permute-start.1
  30.7 2.1 copy.179
  36.6 4.0 %copy.155 = bf16[1,128,7168]{1,2,0:T(8,128)(2,1)} copy(bf16[1,128,7168]{2,1,0:T(8,128)(2,1)} %param.27) | data formatting | bytes 3670016 | tf_op args[13]
  42.0 2.1 fusion.10
  44.1 11.2 %all-to-all-start.1 = ((bf16[16,128,448]{1,2,0:T(8,128)(2,1)}), bf16[16,128,448]{1,2,0:T(8,128)(2,1)}, u32[]{:S(2)}, u32[]{:S(2)}) async-start(bf16[16,128,448]{1,2,0:T(8,128)(2,1)} %bitcast.128), calls=%async_computation.1 | async-start | bytes 3670016 | tf_op jit(solution)/shard_map/all_to_all | solution.py:195
  58.8 52.6 %all_gather.21 = bf16[2,256,576]{2,1,0:T(8,128)(2,1)S(1)} all-gather(bf16[2,16,576]{2,1,0:T(8,128)(2,1)S(1)} %pad_maximum_fusion.4), channel_id=1, replica_groups=mesh['dx'=4,'dy'=4,'ep'=8,'tp'=2] {'ep','tp'}, dimensions={1}, use_global_device_ids=true | all-gather | bytes 626688 | tf_op jit(solution)/shard_map/all_gather | solution.py:189
  111.3 2.2 fusion.64
  117.7 12.2 %all_gather.22 = bf16[4,128,512]{2,1,0:T(8,128)(2,1)S(1)} all-gather(bf16[1,128,512]{2,1,0:T(8,128)(2,1)S(1)} %copy.151), channel_id=1, replica_groups=mesh['dx'=4,'dy'=4,'ep'=8,'tp'=2] {'dx'}, dimensions={0}, use_global_device_ids=true | all-gather | bytes 655360 | tf_op jit(solution)/shard_map/all_gather | solution.py:229
  129.9 3.8 %copy.152 = bf16[2048,448]{1,0:T(8,128)(2,1)} copy(bf16[2048,448]{0,1:T(8,128)(2,1)} %all-gather.8.cloned.1.call-done) | data formatting | bytes 3670016 | tf_op jit(solution)/shard_map/all_gather | solution.py:194
  141.6 3.9 %multiply_convert_fusion = bf16[4,4,448,256]{3,2,0,1:T(8,128)(2,1)} fusion(f32[4,4,448]{2,0,1:T(4,128)S(1)} %copy.163, bf16[4,4,448,128]{3,2,1,0:T(8,128)(2,1)} %bitcast.130, bf16[4,4,448,128]{3,2,1,0:T(8,128)(2,1)} %bitcast.131), kind=kLoop, calls=%fused_computation.2 | loop fusion | flops 12845056 | bytes 7368704 | tf_op jit(solution)/shard_map/convert_element_type | solution.py:207
  152.0 8.9 %all-to-all-start.2 = ((bf16[8,128,448]{1,2,0:T(8,128)(2,1)}), bf16[8,128,448]{1,2,0:T(8,128)(2,1)S(1)}, u32[]{:S(2)}, u32[]{:S(2)}) async-start(bf16[8,128,448]{1,2,0:T(8,128)(2,1)} %copy.164), calls=%async_computation.2 | async-start | bytes 1835008 | tf_op jit(solution)/shard_map/all_to_all | solution.py:236
  161.0 26.3 %all-to-all-done.2 = bf16[8,128,448]{1,2,0:T(8,128)(2,1)S(1)} async-done(((bf16[8,128,448]{1,2,0:T(8,128)(2,1)}), bf16[8,128,448]{1,2,0:T(8,128)(2,1)S(1)}, u32[]{:S(2)}, u32[]{:S(2)}) %all-to-all-start.2) | async-done | bytes 917536 | tf_op jit(solution)/shard_map/all_to_all | solution.py:236
  188.8 15.7 %all_to_all.30 = bf16[16,24,448]{2,1,0:T(8,128)(2,1)S(1)} all-to-all(bf16[16,24,448]{2,1,0:T(8,128)(2,1)S(1)} %bitcast.132), channel_id=1, replica_groups=mesh['dx'=4,'dy'=4,'ep'=8,'tp'=2] {'dx','dy'}, dimensions={0} | all-to-all | bytes 688128 | tf_op jit(solution)/shard_map/all_to_all | solution.py:245
  206.3 38.7 %all-gather.6.cloned.1.call-done = bf16[16,96,1792]{2,1,0:T(8,128)(2,1)} async-done(((bf16[1,96,1792]{2,1,0:T(8,128)(2,1)}), bf16[16,96,1792]{2,1,0:T(8,128)(2,1)}) %all-gather.6.cloned.1.call-update) | async-done | bytes 5505040 | tf_op jit(solution)/shard_map/all_gather | solution.py:248
  244.9 2.0 copy-done.3
  247.0 2.6 copy-done.4
  249.5 3.6 %shard_map.138 = bf16[384,128]{1,0:T(8,128)(2,1)} custom-call(bf16[4,4,96,1792]{3,2,1,0:T(8,128)(2,1)S(1)} %bitcast.124, bf16[4,1792,256]{2,1,0:T(8,128)(2,1)S(1)} %bitcast.123), custom_call_target="tpu_custom_call" | custom-call | flops 1409286144 | bytes 9175040 | tf_op jit(solution)/shard_map/pallas_call | solution.py:119
  253.1 37.7 %all-gather.10.cloned.1.call-done = bf16[6144,128]{1,0:T(8,128)(2,1)} async-done(((bf16[384,128]{1,0:T(8,128)(2,1)}), bf16[6144,128]{1,0:T(8,128)(2,1)}) %all-gather.10.cloned.1.call-update) | async-done | bytes 1572880 | tf_op jit(solution)/shard_map/all_gather | solution.py:252
  290.8 3.1 fusion.4
  294.9 6.5 %all-to-all-start.4 = ((bf16[16,24,448]{2,1,0:T(8,128)(2,1)}), bf16[16,24,448]{2,1,0:T(8,128)(2,1)S(1)}, u32[]{:S(2)}, u32[]{:S(2)}) async-start(bf16[16,24,448]{2,1,0:T(8,128)(2,1)} %bitcast.38), calls=%async_computation.4 | async-start | bytes 786432 | tf_op jit(solution)/shard_map/all_to_all | solution.py:256
  302.2 8.5 %all-to-all-done.4 = bf16[16,24,448]{2,1,0:T(8,128)(2,1)S(1)} async-done(((bf16[16,24,448]{2,1,0:T(8,128)(2,1)}), bf16[16,24,448]{2,1,0:T(8,128)(2,1)S(1)}, u32[]{:S(2)}, u32[]{:S(2)}) %all-to-all-start.4) | async-done | bytes 344096 | tf_op jit(solution)/shard_map/all_to_all | solution.py:256
  311.2 18.9 %all_to_all.31 = bf16[16,8,448]{2,1,0:T(8,128)(2,1)S(1)} all-to-all(bf16[16,8,448]{2,1,0:T(8,128)(2,1)S(1)} %bitcast.136), channel_id=1, replica_groups=mesh['dx'=4,'dy'=4,'ep'=8,'tp'=2] {'ep','tp'}, dimensions={0} | all-to-all | bytes 229376 | tf_op jit(solution)/shard_map/all_to_all | solution.py:264
  (117 shorter events, 40.1 us)
Async XLA Ops:
  6.5 11.9 %copy-start = (bf16[128,7168]{1,0:T(8,128)(2,1)S(1)}, bf16[128,7168]{1,0:T(8,128)(2,1)}, u32[]{:S(2)}) copy-start(bf16[128,7168]{1,0:T(8,128)(2,1)} %param.21) | copy-start | bytes 5505028
  8.8 12.7 %copy-start.18 = (s32[2,16]{1,0:T(2,128)S(1)}, s32[2,16]{1,0:T(2,128)}, u32[]{:S(2)}) copy-start(s32[2,16]{1,0:T(2,128)} %param.18) | copy-start | bytes 388
  8.8 14.7 %copy-start.10 = (bf16[4,32,576]{2,1,0:T(8,128)(2,1)S(1)}, bf16[4,32,576]{2,1,0:T(8,128)(2,1)}, u32[]{:S(2)}) copy-start(bf16[4,32,576]{2,1,0:T(8,128)(2,1)} %param.16) | copy-start | bytes 442372
  9.0 15.2 %copy-start.6 = (bf16[128,4,576]{0,2,1:T(8,128)(2,1)S(1)}, bf16[128,4,576]{0,2,1:T(8,128)(2,1)}, u32[]{:S(2)}) copy-start(bf16[128,4,576]{0,2,1:T(8,128)(2,1)} %param.14) | copy-start | bytes 1769476
  10.0 34.1 %all-to-all-start = ((bf16[16,2,16,576]{3,2,1,0:T(8,128)(2,1)}), bf16[16,2,16,576]{3,2,1,0:T(8,128)(2,1)S(1)}, u32[]{:S(2)}, u32[]{:S(2)}) async-start(bf16[16,2,16,576]{3,2,1,0:T(8,128)(2,1)} %broadcast_in_dim.31), calls=%async_computation | async-start | bytes 1310720 | tf_op jit(solution)/shard_map/all_to_all | solution.py:180
  17.6 7.8 %copy-start.17 = (s32[64]{0:T(128)S(1)}, s32[64]{0:T(128)}, u32[]{:S(2)}) copy-start(s32[64]{0:T(128)} %param.17) | copy-start | bytes 772
  17.6 112.2 %all-gather.8.cloned.1.call-start = ((), (), s32[]{:S(2)}) async-start(), calls=%async_computation.7 | async-start | bytes 2293760 | tf_op jit(solution)/shard_map/all_gather | solution.py:194
  19.3 131.4 %collective-permute-start.1 = (bf16[128,448]{0,1:T(8,128)(2,1)}, bf16[128,448]{0,1:T(8,128)(2,1)}, u32[]{:S(2)}, u32[]{:S(2)}) collective-permute-start(bf16[128,448]{0,1:T(8,128)(2,1)} %copy.182), channel_id=1, source_target_pairs={{0,0},{1,1},{2,2},{3,3},{4,64},{5,65},{6,66},{7,67},{8,128},{9,129... | collective-permute-start | bytes 344072 | tf_op jit(solution)/shard_map/ppermute | solution.py:198
  24.2 31.2 %copy-start.12 = (bf16[2,32,576]{2,1,0:T(8,128)(2,1)}, bf16[2,32,576]{2,1,0:T(8,128)(2,1)S(1)}, u32[]{:S(2)}) copy-start(bf16[2,32,576]{2,1,0:T(8,128)(2,1)S(1)} %get-tuple-element.23) | copy-start | bytes 221188
  25.4 9.5 %copy-start.7 = (bf16[64,4,576]{0,2,1:T(8,128)(2,1)S(1)}, bf16[64,4,576]{0,2,1:T(8,128)(2,1)}, u32[]{:S(2)}) copy-start(bf16[64,4,576]{0,2,1:T(8,128)(2,1)} %get-tuple-element.22) | copy-start | bytes 884740
  25.4 10.4 %copy-start.14 = (s32[128,2]{0,1:T(2,128)S(1)}, s32[128,2]{0,1:T(2,128)}, u32[]{:S(2)}) copy-start(s32[128,2]{0,1:T(2,128)} %param.23) | copy-start | bytes 3076
  36.6 5.3 %copy-start.8 = (bf16[2,256,576]{2,1,0:T(8,128)(2,1)S(1)}, bf16[2,256,576]{2,1,0:T(8,128)(2,1)}, u32[]{:S(2)}) copy-start(bf16[2,256,576]{2,1,0:T(8,128)(2,1)} %copy.179) | copy-start | bytes 1769476
  44.1 106.6 %all-to-all-start.1 = ((bf16[16,128,448]{1,2,0:T(8,128)(2,1)}), bf16[16,128,448]{1,2,0:T(8,128)(2,1)}, u32[]{:S(2)}, u32[]{:S(2)}) async-start(bf16[16,128,448]{1,2,0:T(8,128)(2,1)} %bitcast.128), calls=%async_computation.1 | async-start | bytes 3670016 | tf_op jit(solution)/shard_map/all_to_all | solution.py:195
  58.7 52.7 %copy-start.11 = (bf16[2,32,576]{2,1,0:T(8,128)(2,1)S(1)}, bf16[2,32,576]{2,1,0:T(8,128)(2,1)}, u32[]{:S(2)}) copy-start(bf16[2,32,576]{2,1,0:T(8,128)(2,1)} %get-tuple-element.24) | copy-start | bytes 221188
  136.2 4.6 %copy-start.15 = (s32[128,2]{0,1:T(2,128)S(1)}, s32[128,2]{0,1:T(2,128)}, u32[]{:S(2)}) copy-start(s32[128,2]{0,1:T(2,128)} %param.23) | copy-start | bytes 3076
  136.2 5.2 %copy-start.13 = (bf16[7168]{0:T(1024)(128)(2,1)S(1)}, bf16[7168]{0:T(1024)(128)(2,1)}, u32[]{:S(2)}) copy-start(bf16[7168]{0:T(1024)(128)(2,1)} %param.22) | copy-start | bytes 43012
  137.6 8.0 %collective-permute-start = (bf16[4,2,128,448]{2,3,1,0:T(8,128)(2,1)}, bf16[4,2,128,448]{2,3,1,0:T(8,128)(2,1)S(1)}, u32[]{:S(2)}, u32[]{:S(2)}) collective-permute-start(bf16[4,2,128,448]{2,3,1,0:T(8,128)(2,1)} %copy.153), channel_id=1, source_target_pairs={{0,1},{1,0},{2,3},{3,2},{4,5},{5,4},{6,7},{7,6},{8,9},{9,8},{10,11... | collective-permute-start | bytes 2752520 | tf_op jit(solution)/shard_map/ppermute | solution.py:231
  140.8 9.9 %collective-permute-start.2 = (s32[2,128]{1,0:T(2,128)S(1)}, s32[2,128]{1,0:T(2,128)S(1)}, u32[]{:S(2)}, u32[]{:S(2)}) collective-permute-start(s32[2,128]{1,0:T(2,128)S(1)} %add_bitcast_fusion.1), channel_id=1, source_target_pairs={{0,0},{1,1},{2,2},{3,3},{4,64},{5,65},{6,66},{7,67},{8,128},{9,129... | collective-permute-start | bytes 3080 | tf_op jit(solution)/shard_map/ppermute | solution.py:203
  152.0 35.3 %all-to-all-start.2 = ((bf16[8,128,448]{1,2,0:T(8,128)(2,1)}), bf16[8,128,448]{1,2,0:T(8,128)(2,1)S(1)}, u32[]{:S(2)}, u32[]{:S(2)}) async-start(bf16[8,128,448]{1,2,0:T(8,128)(2,1)} %copy.164), calls=%async_computation.2 | async-start | bytes 1835008 | tf_op jit(solution)/shard_map/all_to_all | solution.py:236
  160.9 84.0 %all-gather.6.cloned.1.call-start = ((), (), s32[]{:S(2)}) async-start(), calls=%async_computation.6 | async-start | bytes 5849088 | tf_op jit(solution)/shard_map/all_gather | solution.py:248
  206.1 84.8 %all-gather.10.cloned.1.call-start = ((), (), s32[]{:S(2)}) async-start(), calls=%async_computation.8 | async-start | bytes 1671168 | tf_op jit(solution)/shard_map/all_gather | solution.py:252
  290.8 10.6 %copy-start.19 = (bf16[128,2]{0,1:T(2,128)(2,1)S(1)}, bf16[128,2]{0,1:T(2,128)(2,1)}, u32[]{:S(2)}) copy-start(bf16[128,2]{0,1:T(2,128)(2,1)} %param.24) | copy-start | bytes 1540
  294.9 15.9 %all-to-all-start.4 = ((bf16[16,24,448]{2,1,0:T(8,128)(2,1)}), bf16[16,24,448]{2,1,0:T(8,128)(2,1)S(1)}, u32[]{:S(2)}, u32[]{:S(2)}) async-start(bf16[16,24,448]{2,1,0:T(8,128)(2,1)} %bitcast.38), calls=%async_computation.4 | async-start | bytes 786432 | tf_op jit(solution)/shard_map/all_to_all | solution.py:256
  301.6 9.5 %collective-permute-start.3 = (bf16[128,448]{0,1:T(8,128)(2,1)S(1)}, bf16[128,448]{0,1:T(8,128)(2,1)S(1)}, u32[]{:S(2)}, u32[]{:S(2)}) collective-permute-start(bf16[128,448]{0,1:T(8,128)(2,1)S(1)} %add_convert_fusion.1), channel_id=1, source_target_pairs={{0,0},{1,1},{2,2},{3,3},{4,64},{5,65},{6,66},{7,67},{8,128},{9,129... | collective-permute-start | bytes 344072 | tf_op jit(solution)/shard_map/ppermute | solution.py:239
  (7 other events, 13.3 us)
Sparse Core Ops, SparseCore 0:
  20.3 34.6 all-gather.7
  206.2 38.7 all-gather.5
  253.3 37.5 all-gather.9

commit v3 on v1

v3 whole, which is shorter than its diff:
```python
import functools

import jax
import jax.numpy as jnp
from jax import lax
from jax.experimental import pallas as pl
from jax.experimental.pallas import tpu as pltpu
from jax.sharding import Mesh, PartitionSpec as P

score_scale = 192.0 ** (-0.5)
norm_eps = 1e-06
DP = ("dx", "dy")
MEM = ("ep", "tp")
SWAP = ("dx", "ep", "tp")
bf16 = jnp.bfloat16
f32 = jnp.float32
VMEM_LIMIT = 56 << 20
NT = (((1,), (1,)), ((), ()))


def params():
    return pltpu.CompilerParams(vmem_limit_bytes=VMEM_LIMIT)


def cost(flops, nbytes):
    return pl.CostEstimate(flops=flops, bytes_accessed=nbytes, transcendentals=0)


def attend_kernel(lengths_ref, query_ref, prefix_ref, span_ref, uv_ref, out_ref):
    step = pl.program_id(0)
    length = lengths_ref[step]
    span_rows, heads, width = query_ref.shape
    latent, value = uv_ref.shape[1], uv_ref.shape[2]
    span = span_ref[0]
    prefix = prefix_ref[...].reshape(-1, width)
    prefix_rows = prefix.shape[0]
    rows = jnp.concatenate([query_ref[:, h, :] for h in range(heads)], axis=0)
    first = lax.dot_general(rows, prefix, NT, preferred_element_type=f32) * score_scale
    second = lax.dot_general(rows, span, NT, preferred_element_type=f32) * score_scale
    total = heads * span_rows
    key = lax.broadcasted_iota(jnp.int32, (total, prefix_rows), 1)
    first = jnp.where(key < length, first, -jnp.inf)
    token = lax.rem(lax.broadcasted_iota(jnp.int32, (total, span_rows), 0), span_rows)
    late = lax.broadcasted_iota(jnp.int32, (total, span_rows), 1)
    second = jnp.where(late <= token, second, -jnp.inf)
    highest = jnp.maximum(
        jnp.max(first, axis=1, keepdims=True), jnp.max(second, axis=1, keepdims=True)
    )
    first = jnp.exp(first - highest)
    second = jnp.exp(second - highest)
    norm = jnp.sum(first, axis=1, keepdims=True) + jnp.sum(second, axis=1, keepdims=True)
    out = jnp.dot((first / norm).astype(bf16), prefix[:, :latent], preferred_element_type=f32)
    out += jnp.dot((second / norm).astype(bf16), span[:, :latent], preferred_element_type=f32)
    out = out.astype(bf16)
    for h in range(heads):
        part = jnp.dot(
            out[h * span_rows : (h + 1) * span_rows], uv_ref[h], preferred_element_type=f32
        )
        out_ref[:, h * value : (h + 1) * value] = part.astype(bf16)


def attend(lengths, queries, prefix, prefix_spec, span, uv_weight, first_request, count):
    span_rows, width = span.shape[1], span.shape[2]
    heads = queries.shape[1]
    latent, value = uv_weight.shape[1], uv_weight.shape[2]
    keys = 288
    return pl.pallas_call(
        attend_kernel,
        out_shape=jax.ShapeDtypeStruct((count * span_rows, heads * value), bf16),
        grid_spec=pltpu.PrefetchScalarGridSpec(
            num_scalar_prefetch=1,
            grid=(count,),
            in_specs=[
                pl.BlockSpec((span_rows, heads, width), lambda j, n: (first_request + j, 0, 0)),
                prefix_spec,
                pl.BlockSpec((1, span_rows, width), lambda j, n: (first_request + j, 0, 0)),
                pl.BlockSpec((heads, latent, value), lambda j, n: (0, 0, 0)),
            ],
            out_specs=pl.BlockSpec((span_rows, heads * value), lambda j, n: (j, 0)),
        ),
        compiler_params=params(),
        cost_estimate=cost(
            2 * count * span_rows * heads * (keys * (width + latent) + latent * value),
            2 * count * (span_rows * heads * width + keys * width) + 2 * heads * latent * value,
        ),
    )(lengths, queries, prefix, span, uv_weight)


def share_kernel(core_ref, values_ref, weight_ref, *refs):
    out_ref = refs[-1]
    nx, _, cols, rows = out_ref.shape
    contract = (((0,), (1,)), ((), ()))
    for a in range(nx):
        piece = lax.dot_general(
            weight_ref[0], values_ref[a], contract, preferred_element_type=f32
        )
        if len(refs) == 2:
            piece += refs[0][a, 0].astype(f32)
        out_ref[a, 0] = piece.astype(bf16)


def project(core, values, weights, *other):
    nx, rows, depth = values.shape
    blocks, _, cols = weights.shape
    half = blocks // 2
    piece = pl.BlockSpec((nx, 1, cols, rows), lambda i, c: (0, i, 0, 0))
    return pl.pallas_call(
        share_kernel,
        out_shape=jax.ShapeDtypeStruct((nx, half, cols, rows), bf16),
        grid_spec=pltpu.PrefetchScalarGridSpec(
            num_scalar_prefetch=1,
            grid=(half,),
            in_specs=[
                pl.BlockSpec((nx, rows, depth), lambda i, c: (0, 0, 0)),
                pl.BlockSpec((1, depth, cols), lambda i, c: (2 * i + c[0], 0, 0)),
            ]
            + [piece] * len(other),
            out_specs=piece,
        ),
        compiler_params=params(),
        cost_estimate=cost(
            2 * nx * rows * depth * cols * half,
            2 * (nx * rows * depth + half * depth * cols + half * nx * rows * cols),
        ),
    )(core, values, weights, *other)


def hidden_kernel(width, rows_ref, gain_ref, gate_ref, up_ref, out_ref, total, squares):
    step = pl.program_id(0)
    groups, _, rows, depth = rows_ref.shape
    block = rows_ref[...].reshape(groups * rows, depth)
    widened = block.astype(f32)
    square = jnp.sum(widened * widened, axis=1, keepdims=True)
    scaled = (widened * gain_ref[0]).astype(bf16)
    gate = gate_ref[...].reshape(depth, -1)
    up = up_ref[...].reshape(depth, -1)
    weight = jnp.concatenate([gate, up], axis=1)
    product = jnp.dot(scaled, weight, preferred_element_type=f32)

    @pl.when(step == 0)
    def _():
        total[...] = product
        squares[...] = square

    @pl.when(step > 0)
    def _():
        total[...] += product
        squares[...] += square

    @pl.when(step == pl.num_programs(0) - 1)
    def _():
        factor = lax.rsqrt(squares[...] / width + norm_eps)
        ff = out_ref.shape[1]
        gate = total[:, :ff] * factor
        up = total[:, ff:] * factor
        out_ref[...] = (gate / (1.0 + jnp.exp(-gate)) * up).astype(bf16)


def hidden_of(rows_in, gain, gate_weight, up_weight, width):
    nx, ny, rows, depth = rows_in.shape
    ff = gate_weight.shape[3]
    weight_spec = pl.BlockSpec((nx, 1, depth // nx, ff), lambda i: (0, i, 0, 0))
    return pl.pallas_call(
        functools.partial(hidden_kernel, width),
        out_shape=jax.ShapeDtypeStruct((nx * rows, ff), bf16),
        grid=(ny,),
        in_specs=[
            pl.BlockSpec((nx, 1, rows, depth), lambda i: (0, i, 0, 0)),
            pl.BlockSpec((1, 1, depth), lambda i: (i, 0, 0)),
            weight_spec,
            weight_spec,
        ],
        out_specs=pl.BlockSpec((nx * rows, ff), lambda i: (0, 0)),
        scratch_shapes=[pltpu.VMEM((nx * rows, 2 * ff), f32), pltpu.VMEM((nx * rows, 1), f32)],
        compiler_params=params(),
        cost_estimate=cost(
            4 * nx * ny * rows * depth * ff, 2 * (nx * ny * rows * depth + 2 * ny * depth * ff)
        ),
    )(rows_in, gain, gate_weight, up_weight)


def places_of(route_rows, experts):
    flat_routes = route_rows.reshape(-1)
    hits = (flat_routes[:, None] == jnp.arange(experts, dtype=jnp.int32)[None, :]).astype(jnp.int32)
    earlier = jnp.cumsum(hits, axis=0) - hits
    return jnp.sum(earlier * hits, axis=1).reshape(route_rows.shape)


def per_device(
    queries,
    cache,
    span_latent,
    prefix_len,
    destination,
    uv_weight,
    out_weight,
    residual,
    norm_gain,
    routes,
    route_weight,
    gate_weight,
    up_weight,
    down_weight,
):
    requests, prefix_rows, cached_width = cache.shape
    tok_rows = queries.shape[0]
    model_width = residual.shape[1]
    top_k = routes.shape[1]
    ff = gate_weight.shape[2]
    nx, ny = lax.axis_size("dx"), lax.axis_size("dy")
    nz = lax.axis_size("ep")
    rank_count = nx * ny
    members = lax.axis_size(MEM)
    my_rank = lax.axis_index(DP)
    member = lax.axis_index(MEM)
    layer = lax.axis_index("ep")
    core = lax.axis_index("tp")
    col = model_width // members
    capacity = max(2, 3 * tok_rows * top_k // (2 * rank_count))
    swap = [
        (x * members + a * ny + b, a * members + x * ny + b)
        for x in range(nx)
        for a in range(nx)
        for b in range(ny)
    ]

    def other_core(array):
        return lax.ppermute(array, "tp", [(0, 1), (1, 0)])

    def along(array, hops):
        return lax.ppermute(array, "ep", [(z, (z + hops) % nz) for z in range(nz)])

    ranks = jnp.arange(rank_count, dtype=jnp.int32)
    source_first = jnp.sum(ranks * (destination[0] == my_rank).astype(jnp.int32))
    source_second = jnp.sum(ranks * (destination[1] == my_rank).astype(jnp.int32))
    part = prefix_rows // members
    moving = lax.dynamic_slice_in_dim(cache[requests - 2 :], member * part, part, 1)
    arrived = lax.all_to_all(
        jnp.broadcast_to(moving[None], (rank_count,) + moving.shape), DP, 0, 0, tiled=True
    )
    chosen = jnp.stack(
        [
            lax.dynamic_index_in_dim(arrived[:, 0], source_first, 0, keepdims=False),
            lax.dynamic_index_in_dim(arrived[:, 1], source_second, 0, keepdims=False),
        ]
    )
    moved = lax.all_gather(chosen, MEM, axis=0)
    own_len = lax.dynamic_slice_in_dim(prefix_len, my_rank * requests, requests - 2)
    moved_len = jnp.concatenate(
        [
            lax.dynamic_slice_in_dim(prefix_len, source_first * requests + requests - 2, 1),
            lax.dynamic_slice_in_dim(prefix_len, source_second * requests + requests - 1, 1),
        ]
    )

    out_cols = lax.all_gather(out_weight, "dy", axis=0)
    down_t = down_weight[0].T.reshape(nz, 2, col, ff)
    down_mine = lax.dynamic_index_in_dim(down_t, core, 1, keepdims=False)
    down_other = other_core(lax.dynamic_index_in_dim(down_t, 1 - core, 1, keepdims=False))
    down_pair = jnp.stack([down_mine, down_other], axis=1)

    def down_for(hops):
        piece = lax.dynamic_index_in_dim(down_pair, lax.rem(layer + hops, nz), 0, keepdims=False)
        return along(piece, hops) if hops else piece

    hop_order = list(range(nz))
    down_parts = [down_for(hops) for hops in hop_order]
    places = places_of(routes, rank_count)
    packed = jnp.concatenate(
        [
            lax.dynamic_slice_in_dim(residual, member * col, col, 1).T,
            routes.T.astype(bf16),
            places.T.astype(bf16),
            jnp.zeros((16 - 2 * top_k, tok_rows), bf16),
        ],
        axis=0,
    )
    packed_t = lax.ppermute(packed, SWAP, swap)

    part_rows = cache.shape[1]
    values_own = attend(
        own_len,
        queries,
        cache,
        pl.BlockSpec((1, part_rows, cached_width), lambda j, n: (j, 0, 0)),
        span_latent,
        uv_weight,
        0,
        requests - 2,
    )
    values_moved = attend(
        moved_len,
        queries,
        moved,
        pl.BlockSpec((members, 1, part, cached_width), lambda j, n: (0, j, 0, 0)),
        span_latent,
        uv_weight,
        requests - 2,
        2,
    )
    values = jnp.concatenate([values_own, values_moved], axis=0)

    values_x = lax.all_gather(values, "dx", axis=0)
    core_at = jnp.reshape(core, (1,))
    sent = other_core(project(1 - core_at, values_x, out_cols))
    shares = project(core_at, values_x, out_cols, sent).reshape(nz, col, tok_rows)
    shares, down_parts, packed_t = lax.optimization_barrier((shares, down_parts, packed_t))
    shares = lax.all_to_all(shares, "ep", 0, 0, tiled=True)
    attended = jnp.sum(shares.astype(f32), axis=0)
    mixed_t = (packed_t[:col].astype(f32) + attended).astype(bf16)
    mixed = lax.ppermute(mixed_t, SWAP, swap)

    slot_index = jnp.arange(rank_count * capacity, dtype=jnp.int32)
    routes_t = packed_t[col : col + top_k].astype(jnp.int32)
    places_t = packed_t[col + top_k : col + 2 * top_k].astype(jnp.int32)
    slots_t = routes_t * capacity + places_t
    placer = jnp.any(slot_index[:, None, None] == slots_t[None], axis=1).astype(bf16)
    outgoing = lax.dot_general(placer, mixed_t, NT, preferred_element_type=f32).astype(bf16)
    outgoing = outgoing.reshape(rank_count, capacity, col)
    received = lax.all_to_all(outgoing, DP, 0, 0, tiled=True)
    received = received.reshape(nx, ny, capacity, col).transpose(1, 2, 0, 3)
    received = received.reshape(ny * capacity, nx * col)
    rows_in = lax.all_gather(received, MEM, axis=0)
    rows_in, mixed = lax.optimization_barrier((rows_in, mixed))
    rows_in = rows_in.reshape(nx, ny, ny * capacity, nx * col)
    gain = norm_gain.astype(f32).reshape(nx, ny, col).transpose(1, 0, 2).reshape(ny, 1, nx * col)
    hidden = hidden_of(
        rows_in,
        gain,
        gate_weight.reshape(nx, ny, col, ff),
        up_weight.reshape(nx, ny, col, ff),
        float(model_width),
    )

    half = hidden.shape[0] // 2
    blocks = {0: hidden}
    up_way, down_way = hidden, hidden
    for hops in range(1, nz // 2):
        up_way, down_way = along(up_way, 1), along(down_way, -1)
        blocks[hops], blocks[nz - hops] = up_way, down_way
    blocks[nz // 2] = jnp.concatenate([along(up_way[:half], 1), along(down_way[half:], -1)], axis=0)
    hidden_all = jnp.stack([jnp.stack([blocks[h], other_core(blocks[h])]) for h in hop_order])
    down_all = jnp.stack(down_parts)
    expert_out = jnp.einsum("dsrf,dscf->rc", hidden_all, down_all, preferred_element_type=f32)
    expert_out = expert_out.astype(bf16).reshape(rank_count, capacity, col)

    returned = lax.all_to_all(expert_out, DP, 0, 0, tiled=True)
    returned = returned.reshape(rank_count * capacity, col)
    slots = (routes * capacity + places).T
    matches = slots[:, :, None] == slot_index[None, None, :]
    combiner = jnp.sum(
        jnp.where(matches, route_weight.T[:, :, None], jnp.zeros((), route_weight.dtype)), axis=0
    )
    moe = jnp.dot(combiner, returned, preferred_element_type=f32)
    total = (mixed.T.astype(f32) + moe).astype(bf16)
    total = lax.all_to_all(total.reshape(members, tok_rows // members, col), MEM, 0, 0, tiled=True)
    return total.transpose(1, 0, 2).reshape(tok_rows // members, model_width)


def solution(mesh):
    dp, ep, tp = mesh.devices.shape
    nx = 1
    while nx * nx < dp:
        nx *= 2
    grid = Mesh(mesh.devices.reshape(nx, dp // nx, ep, tp), DP + MEM)
    in_specs = (
        P(DP, MEM, None),
        P(DP, None, None),
        P(DP, None, None),
        P(),
        P(),
        P(MEM, None, None),
        P(MEM, DP),
        P(DP, None),
        P(),
        P(DP, None),
        P(DP, None),
        P(DP, None, MEM),
        P(DP, None, MEM),
        P(DP, MEM, None),
    )
    out_specs = P(DP + MEM, None)
    return jax.shard_map(
        per_device, mesh=grid, in_specs=in_specs, out_specs=out_specs, check_vma=False
    )
```

time: 323 us -> 332 us (1.028)
  starting transfers between devices: 31.3 us -> 73.2 us
  waiting for transfers between devices: 136 us -> 102 us
  Pallas kernels: 0 us -> 23 us
  matrix products: 21.3 us -> 1.7 us
  local copies, waits for them, and re-layouts: 34.1 us -> 29.2 us
    ppermute x4 -> x27, starting transfers between devices: 4.67 us -> 58.1 us  [the longest x15 43.2 us: along(): return lax.ppermute(array, 'ep', [(z, (z + hops) % nz) for z in range(nz)])]
    all_gather x1 -> x0, waiting for transfers between devices: 37 us -> none  [per_device(): hidden_all = lax.all_gather(hidden, MEM, axis=0)]
    ppermute x4 -> x27, waiting for transfers between devices: 2.11 us -> 29.4 us  [the longest x15 28.4 us: along(): return lax.ppermute(array, 'ep', [(z, (z + hops) % nz) for z in range(nz)])]
    all_gather x1, waiting for transfers between devices: 64.4 us -> 39.1 us  [per_device(): rows_in = lax.all_gather(received, MEM, axis=0)]
    pallas_call x0 -> x5, Pallas kernels: none -> 23 us  [the longest x2 9.32 us: attend(): pl.pallas_call(attend_kernel, out_shape=jax.ShapeDtypeStruct((count * spa...]
    dot_general x10 -> x2, matrix products: 18 us -> 1.4 us  [the longest x1 1.12 us: per_device(): jnp.einsum('dsrf,dscf->rc', hidden_all, down_all, preferred_element_type=...]
    all_to_all x1 -> x0, starting transfers between devices: 8.81 us -> none  [per_device(): lax.all_to_all(down_weight[0].reshape(-1, members, col).transpose(1, 0, 2...]
    unnamed x40 -> x55, local copies, waits for them, and re-layouts: 8.93 us -> 14.1 us
  transfers between devices with their start and end apart: 11 -> 32, of which waited for: 5 -> 10; matrix products, arithmetic and copies ran while one was open for 13% -> 10% of each run, Pallas kernels for 0% -> 5%
where the time goes in v3:
time: 332 us; the launch traced here: 330 us
  waiting for transfers between devices  102 us (31%)
  starting transfers between devices  73.2 us (22%)
  blocking collectives  69.8 us (21%)
  local copies, waits for them, and re-layouts  29.2 us (9%)
  Pallas kernels  23 us (7%)
  between operations  19.5 us (6%)
  other arithmetic  11.7 us (4%)
    ppermute x15, starting transfers between devices, along(): return lax.ppermute(array, 'ep', [(z, (z + hops) % nz) for z in range(nz)])  43.2 us
    all_gather x1, waiting for transfers between devices, per_device(): rows_in = lax.all_gather(received, MEM, axis=0)  39.1 us
    ppermute x15, waiting for transfers between devices, along(): return lax.ppermute(array, 'ep', [(z, (z + hops) % nz) for z in range(nz)])  28.4 us
    all_to_all x1, waiting for transfers between devices, per_device(): shares = lax.all_to_all(shares, 'ep', 0, 0, tiled=True)  23.9 us
    all_gather x1, blocking collectives, per_device(): moved = lax.all_gather(chosen, MEM, axis=0)  23.1 us
    all_to_all x1, blocking collectives, per_device(): received = lax.all_to_all(outgoing, DP, 0, 0, tiled=True)  19.7 us
    all_to_all x1, blocking collectives, per_device(): lax.all_to_all(total.reshape(members, tok_rows // members, col), MEM, 0,...  15.3 us
    unnamed x55, local copies, waits for them, and re-layouts  14.1 us
  transfers between devices with their start and end apart: 32, of which 10 were waited for; matrix products, arithmetic and copies ran while one was open for 10% of the time, Pallas kernels for 5%

profile of v3, /device:TPU:1, one launch (start us, length us, event | category | flops | bytes accessed | tf_op | source)
XLA Modules:
  0.0 330.3 jit_solution(3182518771976470759)
XLA Ops:
  9.3 7.6 %all-to-all-start = ((bf16[16,2,16,576]{3,2,1,0:T(8,128)(2,1)}), bf16[16,2,16,576]{3,2,1,0:T(8,128)(2,1)S(1)}, u32[]{:S(2)}, u32[]{:S(2)}) async-start(bf16[16,2,16,576]{3,2,1,0:T(8,128)(2,1)} %broadcast_in_dim.12), calls=%async_computation | async-start | bytes 1310720 | tf_op jit(solution)/shard_map/all_to_all | solution.py:238
  16.9 3.9 %copy.109 = bf16[1,128,7168]{1,2,0:T(8,128)(2,1)} copy(bf16[1,128,7168]{2,1,0:T(8,128)(2,1)} %param.27) | data formatting | bytes 3670016 | tf_op args[13]
  38.4 4.7 %shard_map.136 = bf16[64,512]{1,0:T(8,128)(2,1)} custom-call(s32[2]{0:T(128)} %dynamic_slice.58.lengths_ref, bf16[128,4,576]{2,1,0:T(4,128)(2,1)} %copy.104.query_ref, bf16[4,256,576]{2,1,0:T(8,128)(2,1)} %copy.105.prefix_ref, bf16[4,32,576]{2,1,0:T(8,128)(2,1)} %span_ref.3, bf16[4,512,128]{2,1,0:T(8,128)(2,1)} %uv_ref.3), custom_call_target="tpu_custom_call" | custom-call | flops 193986560 | bytes 1482752 | tf_op jit(solution)/shard_map/pallas_call | solution.py:67
  45.1 23.1 %all-gather = bf16[32,16,576]{2,1,0:T(8,128)(2,1)} all-gather(bf16[2,16,576]{2,1,0:T(8,128)(2,1)S(1)} %pad_maximum_fusion.1), channel_id=2, replica_groups=mesh['dx'=4,'dy'=4,'ep'=8,'tp'=2] {'ep','tp'}, dimensions={0}, use_global_device_ids=true | all-gather | bytes 626688 | tf_op jit(solution)/shard_map/all_gather | solution.py:247
  68.2 4.6 %shard_map.137 = bf16[64,512]{1,0:T(8,128)(2,1)} custom-call(s32[2]{0:T(128)} %pad_add_fusion.lengths_ref, bf16[128,4,576]{2,1,0:T(4,128)(2,1)} %copy.104.query_ref, bf16[16,2,16,576]{3,2,1,0:T(8,128)(2,1)} %bitcast.167, bf16[4,32,576]{2,1,0:T(8,128)(2,1)} %span_ref.3, bf16[4,512,128]{2,1,0:T(8,128)(2,1)} %uv_ref.3), custom_call_target="tpu_custom_call" | custom-call | flops 193986560 | bytes 1482752 | tf_op jit(solution)/shard_map/pallas_call | solution.py:67
  73.7 11.8 %all-gather.1 = bf16[512,512]{1,0:T(8,128)(2,1)} all-gather(bf16[128,512]{1,0:T(8,128)(2,1)S(1)} %pad_maximum_fusion), channel_id=3, replica_groups=mesh['dx'=4,'dy'=4,'ep'=8,'tp'=2] {'dx'}, dimensions={0}, use_global_device_ids=true | all-gather | bytes 655360 | tf_op jit(solution)/shard_map/all_gather | solution.py:303
  85.5 3.8 %copy.108 = bf16[2048,448]{1,0:T(8,128)(2,1)} copy(bf16[2048,448]{0,1:T(8,128)(2,1)} %all-gather.8.cloned.1.call-done) | data formatting | bytes 3670016 | tf_op jit(solution)/shard_map/all_gather | solution.py:256
  89.3 3.7 %shard_map.138 = bf16[4,2,448,128]{3,2,1,0:T(8,128)(2,1)} custom-call(s32[1]{0:T(128)S(6)} %sub.17.core_ref, bf16[4,128,512]{2,1,0:T(8,128)(2,1)} %bitcast.164, bf16[4,512,448]{2,1,0:T(8,128)(2,1)} %bitcast.160), custom_call_target="tpu_custom_call" | custom-call | flops 469762048 | bytes 2359296 | tf_op jit(solution)/shard_map/pallas_call | solution.py:107
  102.6 4.8 %collective-permute-start.4 = (bf16[2,448,128]{2,1,0:T(8,128)(2,1)}, bf16[2,448,128]{2,1,0:T(8,128)(2,1)S(1)}, u32[]{:S(2)}, u32[]{:S(2)}) collective-permute-start(bf16[2,448,128]{2,1,0:T(8,128)(2,1)} %get-tuple-element.35), channel_id=1, source_target_pairs={{0,6},{2,8},{4,10},{6,12},{8,14},{10,0},{12,2},{14,4},{1,7},{3,9},... | collective-permute-start | bytes 688136 | tf_op jit(solution)/shard_map/ppermute | solution.py:231
  108.3 13.8 %collective-permute-start.5 = (bf16[2,448,128]{2,1,0:T(8,128)(2,1)S(1)}, bf16[2,448,128]{2,1,0:T(8,128)(2,1)S(1)}, u32[]{:S(2)}, u32[]{:S(2)}) collective-permute-start(bf16[2,448,128]{2,1,0:T(8,128)(2,1)S(1)} %get-tuple-element.36), channel_id=1, source_target_pairs={{0,8},{2,10},{4,12},{6,14},{8,0},{10,2},{12,4},{14,6},{1,9},{3,11}... | collective-permute-start | bytes 688136 | tf_op jit(solution)/shard_map/ppermute | solution.py:231
  122.2 10.9 %collective-permute-start.8 = (bf16[2,448,128]{2,1,0:T(8,128)(2,1)S(1)}, bf16[2,448,128]{2,1,0:T(8,128)(2,1)S(1)}, u32[]{:S(2)}, u32[]{:S(2)}) collective-permute-start(bf16[2,448,128]{2,1,0:T(8,128)(2,1)S(1)} %get-tuple-element.31), channel_id=1, source_target_pairs={{0,14},{2,0},{4,2},{6,4},{8,6},{10,8},{12,10},{14,12},{1,15},{3,1}... | collective-permute-start | bytes 688136 | tf_op jit(solution)/shard_map/ppermute | solution.py:231
  134.3 3.8 %shard_map.139 = bf16[4,2,448,128]{3,2,1,0:T(8,128)(2,1)} custom-call(s32[1]{0:T(128)} %bitcast.core_ref, bf16[4,128,512]{2,1,0:T(8,128)(2,1)} %bitcast.165, bf16[4,512,448]{2,1,0:T(8,128)(2,1)} %bitcast.161, bf16[4,2,448,128]{3,2,1,0:T(8,128)(2,1)} %collective-permute-done.refs_0_), custom_call_target="tpu_custom_call" | custom-call | flops 469762048 | bytes 2359296 | tf_op jit(solution)/shard_map/pallas_call | solution.py:107
  138.2 6.6 %collective-permute-done.5 = bf16[2,448,128]{2,1,0:T(8,128)(2,1)S(1)} collective-permute-done((bf16[2,448,128]{2,1,0:T(8,128)(2,1)S(1)}, bf16[2,448,128]{2,1,0:T(8,128)(2,1)S(1)}, u32[]{:S(2)}, u32[]{:S(2)}) %collective-permute-start.5) | collective-permute-done | bytes 229408 | tf_op jit(solution)/shard_map/ppermute | solution.py:231
  147.0 11.0 %collective-permute-done.6 = bf16[2,448,128]{2,1,0:T(8,128)(2,1)S(1)} collective-permute-done((bf16[2,448,128]{2,1,0:T(8,128)(2,1)S(1)}, bf16[2,448,128]{2,1,0:T(8,128)(2,1)S(1)}, u32[]{:S(2)}, u32[]{:S(2)}) %collective-permute-start.6) | collective-permute-done | bytes 229408 | tf_op jit(solution)/shard_map/ppermute | solution.py:231
  158.0 6.6 %collective-permute-done.7 = bf16[2,448,128]{2,1,0:T(8,128)(2,1)S(1)} collective-permute-done((bf16[2,448,128]{2,1,0:T(8,128)(2,1)S(1)}, bf16[2,448,128]{2,1,0:T(8,128)(2,1)S(1)}, u32[]{:S(2)}, u32[]{:S(2)}) %collective-permute-start.7) | collective-permute-done | bytes 229408 | tf_op jit(solution)/shard_map/ppermute | solution.py:231
  165.3 3.9 %all-to-all-start.1 = ((bf16[8,448,128]{2,1,0:T(8,128)(2,1)}), bf16[8,448,128]{2,1,0:T(8,128)(2,1)S(1)}, u32[]{:S(2)}, u32[]{:S(2)}) async-start(bf16[8,448,128]{2,1,0:T(8,128)(2,1)} %bitcast.166), calls=%async_computation.1 | async-start | bytes 1835008 | tf_op jit(solution)/shard_map/all_to_all | solution.py:308
  170.0 23.9 %all-to-all-done.1 = bf16[8,448,128]{2,1,0:T(8,128)(2,1)S(1)} async-done(((bf16[8,448,128]{2,1,0:T(8,128)(2,1)}), bf16[8,448,128]{2,1,0:T(8,128)(2,1)S(1)}, u32[]{:S(2)}, u32[]{:S(2)}) %all-to-all-start.1) | async-done | bytes 917536 | tf_op jit(solution)/shard_map/all_to_all | solution.py:308
  195.5 19.7 %all_to_all.25 = bf16[16,24,448]{2,1,0:T(8,128)(2,1)S(1)} all-to-all(bf16[16,24,448]{2,1,0:T(8,128)(2,1)S(1)} %bitcast.170), channel_id=1, replica_groups=mesh['dx'=4,'dy'=4,'ep'=8,'tp'=2] {'dx','dy'}, dimensions={0} | all-to-all | bytes 688128 | tf_op jit(solution)/shard_map/all_to_all | solution.py:320
  221.6 39.1 %all-gather.6.cloned.1.call-done = bf16[16,96,1792]{2,1,0:T(8,128)(2,1)} async-done(((bf16[1,96,1792]{2,1,0:T(8,128)(2,1)}), bf16[16,96,1792]{2,1,0:T(8,128)(2,1)}) %all-gather.6.cloned.1.call-update) | async-done | bytes 5505040 | tf_op jit(solution)/shard_map/all_gather | solution.py:323
  260.7 6.2 %shard_map.140 = bf16[384,128]{1,0:T(8,128)(2,1)} custom-call(bf16[4,4,96,1792]{3,2,1,0:T(8,128)(2,1)} %bitcast.163, f32[4,1,1792]{2,1,0:T(1,128)} %reshape.93.gain_ref, bf16[4,4,448,128]{3,2,1,0:T(8,128)(2,1)} %bitcast.168, bf16[4,4,448,128]{3,2,1,0:T(8,128)(2,1)} %bitcast.169), custom_call_target="tpu_custom_call" | custom-call | flops 1409286144 | bytes 9175040 | tf_op jit(solution)/shard_map/pallas_call | solution.py:163
  284.0 3.0 collective-permute-start.22
  294.2 3.6 %all-to-all-start.3 = ((bf16[16,24,448]{2,1,0:T(8,128)(2,1)}), bf16[16,24,448]{2,1,0:T(8,128)(2,1)S(1)}, u32[]{:S(2)}, u32[]{:S(2)}) async-start(bf16[16,24,448]{2,1,0:T(8,128)(2,1)} %bitcast.72), calls=%async_computation.3 | async-start | bytes 786432 | tf_op jit(solution)/shard_map/all_to_all | solution.py:347
  297.9 9.0 %all-to-all-done.3 = bf16[16,24,448]{2,1,0:T(8,128)(2,1)S(1)} async-done(((bf16[16,24,448]{2,1,0:T(8,128)(2,1)}), bf16[16,24,448]{2,1,0:T(8,128)(2,1)S(1)}, u32[]{:S(2)}, u32[]{:S(2)}) %all-to-all-start.3) | async-done | bytes 344096 | tf_op jit(solution)/shard_map/all_to_all | solution.py:347
  307.4 15.3 %all_to_all.26 = bf16[16,8,448]{2,1,0:T(8,128)(2,1)S(1)} all-to-all(bf16[16,8,448]{2,1,0:T(8,128)(2,1)S(1)} %bitcast.173), channel_id=1, replica_groups=mesh['dx'=4,'dy'=4,'ep'=8,'tp'=2] {'ep','tp'}, dimensions={0} | all-to-all | bytes 229376 | tf_op jit(solution)/shard_map/all_to_all | solution.py:356
  (169 shorter events, 66.5 us)
Async XLA Ops:
  6.5 79.0 %all-gather.8.cloned.1.call-start = ((), (), s32[]{:S(2)}) async-start(), calls=%async_computation.6 | async-start | bytes 2293760 | tf_op jit(solution)/shard_map/all_gather | solution.py:256
  9.3 35.7 %all-to-all-start = ((bf16[16,2,16,576]{3,2,1,0:T(8,128)(2,1)}), bf16[16,2,16,576]{3,2,1,0:T(8,128)(2,1)S(1)}, u32[]{:S(2)}, u32[]{:S(2)}) async-start(bf16[16,2,16,576]{3,2,1,0:T(8,128)(2,1)} %broadcast_in_dim.12), calls=%async_computation | async-start | bytes 1310720 | tf_op jit(solution)/shard_map/all_to_all | solution.py:238
  23.4 73.5 %collective-permute-start.1 = (bf16[8,448,128]{2,1,0:T(8,128)(2,1)}, bf16[8,448,128]{2,1,0:T(8,128)(2,1)}, u32[]{:S(2)}, u32[]{:S(2)}) collective-permute-start(bf16[8,448,128]{2,1,0:T(8,128)(2,1)} %get-tuple-element.40), channel_id=1, source_target_pairs={{0,1},{1,0},{2,3},{3,2},{4,5},{5,4},{6,7},{7,6},{8,9},{9,8},{10,11... | collective-permute-start | bytes 2752520 | tf_op jit(solution)/shard_map/ppermute | solution.py:228
  93.0 40.1 %collective-permute-start = (bf16[4,2,448,128]{3,2,1,0:T(8,128)(2,1)}, bf16[4,2,448,128]{3,2,1,0:T(8,128)(2,1)}, u32[]{:S(2)}, u32[]{:S(2)}) collective-permute-start(bf16[4,2,448,128]{3,2,1,0:T(8,128)(2,1)} %shard_map.138), channel_id=1, source_target_pairs={{0,1},{1,0},{2,3},{3,2},{4,5},{5,4},{6,7},{7,6},{8,9},{9,8},{10,11... | collective-permute-start | bytes 2752520 | tf_op jit(solution)/shard_map/ppermute | solution.py:228
  99.0 23.2 %collective-permute-start.2 = (bf16[2,448,128]{2,1,0:T(8,128)(2,1)}, bf16[2,448,128]{2,1,0:T(8,128)(2,1)}, u32[]{:S(2)}, u32[]{:S(2)}) collective-permute-start(bf16[2,448,128]{2,1,0:T(8,128)(2,1)} %get-tuple-element.33), channel_id=1, source_target_pairs={{0,2},{2,4},{4,6},{6,8},{8,10},{10,12},{12,14},{14,0},{1,3},{3,5},... | collective-permute-start | bytes 688136 | tf_op jit(solution)/shard_map/ppermute | solution.py:231
  99.0 34.1 %collective-permute-start.3 = (bf16[2,448,128]{2,1,0:T(8,128)(2,1)}, bf16[2,448,128]{2,1,0:T(8,128)(2,1)}, u32[]{:S(2)}, u32[]{:S(2)}) collective-permute-start(bf16[2,448,128]{2,1,0:T(8,128)(2,1)} %get-tuple-element.34), channel_id=1, source_target_pairs={{0,4},{2,6},{4,8},{6,10},{8,12},{10,14},{12,0},{14,2},{1,5},{3,7},... | collective-permute-start | bytes 688136 | tf_op jit(solution)/shard_map/ppermute | solution.py:231
  100.4 7.9 %collective-permute-start.9 = (bf16[464,128]{1,0:T(8,128)(2,1)}, bf16[464,128]{1,0:T(8,128)(2,1)}, u32[]{:S(2)}, u32[]{:S(2)}) collective-permute-start(bf16[464,128]{1,0:T(8,128)(2,1)} %maximum_maximum_fusion), channel_id=1, source_target_pairs={{0,0},{1,1},{2,2},{3,3},{4,64},{5,65},{6,66},{7,67},{8,128},{9,129... | collective-permute-start | bytes 356360 | tf_op jit(solution)/shard_map/ppermute | solution.py:278
  102.6 35.6 %collective-permute-start.4 = (bf16[2,448,128]{2,1,0:T(8,128)(2,1)}, bf16[2,448,128]{2,1,0:T(8,128)(2,1)S(1)}, u32[]{:S(2)}, u32[]{:S(2)}) collective-permute-start(bf16[2,448,128]{2,1,0:T(8,128)(2,1)} %get-tuple-element.35), channel_id=1, source_target_pairs={{0,6},{2,8},{4,10},{6,12},{8,14},{10,0},{12,2},{14,4},{1,7},{3,9},... | collective-permute-start | bytes 688136 | tf_op jit(solution)/shard_map/ppermute | solution.py:231
  108.3 36.5 %collective-permute-start.5 = (bf16[2,448,128]{2,1,0:T(8,128)(2,1)S(1)}, bf16[2,448,128]{2,1,0:T(8,128)(2,1)S(1)}, u32[]{:S(2)}, u32[]{:S(2)}) collective-permute-start(bf16[2,448,128]{2,1,0:T(8,128)(2,1)S(1)} %get-tuple-element.36), channel_id=1, source_target_pairs={{0,8},{2,10},{4,12},{6,14},{8,0},{10,2},{12,4},{14,6},{1,9},{3,11}... | collective-permute-start | bytes 688136 | tf_op jit(solution)/shard_map/ppermute | solution.py:231
  122.2 24.1 %collective-permute-start.8 = (bf16[2,448,128]{2,1,0:T(8,128)(2,1)S(1)}, bf16[2,448,128]{2,1,0:T(8,128)(2,1)S(1)}, u32[]{:S(2)}, u32[]{:S(2)}) collective-permute-start(bf16[2,448,128]{2,1,0:T(8,128)(2,1)S(1)} %get-tuple-element.31), channel_id=1, source_target_pairs={{0,14},{2,0},{4,2},{6,4},{8,6},{10,8},{12,10},{14,12},{1,15},{3,1}... | collective-permute-start | bytes 688136 | tf_op jit(solution)/shard_map/ppermute | solution.py:231
  133.1 24.9 %collective-permute-start.6 = (bf16[2,448,128]{2,1,0:T(8,128)(2,1)S(1)}, bf16[2,448,128]{2,1,0:T(8,128)(2,1)S(1)}, u32[]{:S(2)}, u32[]{:S(2)}) collective-permute-start(bf16[2,448,128]{2,1,0:T(8,128)(2,1)S(1)} %get-tuple-element.38), channel_id=1, source_target_pairs={{0,10},{2,12},{4,14},{6,0},{8,2},{10,4},{12,6},{14,8},{1,11},{3,13... | collective-permute-start | bytes 688136 | tf_op jit(solution)/shard_map/ppermute | solution.py:231
  133.1 31.5 %collective-permute-start.7 = (bf16[2,448,128]{2,1,0:T(8,128)(2,1)S(1)}, bf16[2,448,128]{2,1,0:T(8,128)(2,1)S(1)}, u32[]{:S(2)}, u32[]{:S(2)}) collective-permute-start(bf16[2,448,128]{2,1,0:T(8,128)(2,1)S(1)} %get-tuple-element.37), channel_id=1, source_target_pairs={{0,12},{2,14},{4,0},{6,2},{8,4},{10,6},{12,8},{14,10},{1,13},{3,15... | collective-permute-start | bytes 688136 | tf_op jit(solution)/shard_map/ppermute | solution.py:231
  165.3 28.7 %all-to-all-start.1 = ((bf16[8,448,128]{2,1,0:T(8,128)(2,1)}), bf16[8,448,128]{2,1,0:T(8,128)(2,1)S(1)}, u32[]{:S(2)}, u32[]{:S(2)}) async-start(bf16[8,448,128]{2,1,0:T(8,128)(2,1)} %bitcast.166), calls=%async_computation.1 | async-start | bytes 1835008 | tf_op jit(solution)/shard_map/all_to_all | solution.py:308
  169.2 91.5 %all-gather.6.cloned.1.call-start = ((), (), s32[]{:S(2)}) async-start(), calls=%async_computation.5 | async-start | bytes 5849088 | tf_op jit(solution)/shard_map/all_gather | solution.py:323
  267.8 5.7 %collective-permute-start.19 = (bf16[384,128]{1,0:T(8,128)(2,1)}, bf16[384,128]{1,0:T(8,128)(2,1)S(1)}, u32[]{:S(2)}, u32[]{:S(2)}) collective-permute-start(bf16[384,128]{1,0:T(8,128)(2,1)} %shard_map.140), channel_id=1, source_target_pairs={{0,14},{2,0},{4,2},{6,4},{8,6},{10,8},{12,10},{14,12},{1,15},{3,1}... | collective-permute-start | bytes 294920 | tf_op jit(solution)/shard_map/ppermute | solution.py:231
  269.6 7.2 %collective-permute-start.11 = (bf16[384,128]{1,0:T(8,128)(2,1)}, bf16[384,128]{1,0:T(8,128)(2,1)S(1)}, u32[]{:S(2)}, u32[]{:S(2)}) collective-permute-start(bf16[384,128]{1,0:T(8,128)(2,1)} %shard_map.140), channel_id=1, source_target_pairs={{0,1},{1,0},{2,3},{3,2},{4,5},{5,4},{6,7},{7,6},{8,9},{9,8},{10,11... | collective-permute-start | bytes 294920 | tf_op jit(solution)/shard_map/ppermute | solution.py:228
  272.5 9.9 %collective-permute-start.13 = (bf16[384,128]{1,0:T(8,128)(2,1)S(1)}, bf16[384,128]{1,0:T(8,128)(2,1)S(1)}, u32[]{:S(2)}, u32[]{:S(2)}) collective-permute-start(bf16[384,128]{1,0:T(8,128)(2,1)S(1)} %collective-permute-done.12), channel_id=1, source_target_pairs={{0,1},{1,0},{2,3},{3,2},{4,5},{5,4},{6,7},{7,6},{8,9},{9,8},{10,11... | collective-permute-start | bytes 294920 | tf_op jit(solution)/shard_map/ppermute | solution.py:228
  273.6 5.8 %collective-permute-start.20 = (bf16[384,128]{1,0:T(8,128)(2,1)S(1)}, bf16[384,128]{1,0:T(8,128)(2,1)S(1)}, u32[]{:S(2)}, u32[]{:S(2)}) collective-permute-start(bf16[384,128]{1,0:T(8,128)(2,1)S(1)} %collective-permute-done.19), channel_id=1, source_target_pairs={{0,14},{2,0},{4,2},{6,4},{8,6},{10,8},{12,10},{14,12},{1,15},{3,1}... | collective-permute-start | bytes 294920 | tf_op jit(solution)/shard_map/ppermute | solution.py:231
  276.5 15.5 %collective-permute-start.26 = (bf16[384,128]{1,0:T(8,128)(2,1)S(1)}, bf16[384,128]{1,0:T(8,128)(2,1)S(1)}, u32[]{:S(2)}, u32[]{:S(2)}) collective-permute-start(bf16[384,128]{1,0:T(8,128)(2,1)S(1)} %collective-permute-done.19), channel_id=1, source_target_pairs={{0,1},{1,0},{2,3},{3,2},{4,5},{5,4},{6,7},{7,6},{8,9},{9,8},{10,11... | collective-permute-start | bytes 294920 | tf_op jit(solution)/shard_map/ppermute | solution.py:228
  277.8 9.2 %collective-permute-start.15 = (bf16[384,128]{1,0:T(8,128)(2,1)S(1)}, bf16[384,128]{1,0:T(8,128)(2,1)S(1)}, u32[]{:S(2)}, u32[]{:S(2)}) collective-permute-start(bf16[384,128]{1,0:T(8,128)(2,1)S(1)} %collective-permute-done.14), channel_id=1, source_target_pairs={{0,1},{1,0},{2,3},{3,2},{4,5},{5,4},{6,7},{7,6},{8,9},{9,8},{10,11... | collective-permute-start | bytes 294920 | tf_op jit(solution)/shard_map/ppermute | solution.py:228
  282.3 9.7 %collective-permute-start.25 = (bf16[384,128]{1,0:T(8,128)(2,1)S(1)}, bf16[384,128]{1,0:T(8,128)(2,1)S(1)}, u32[]{:S(2)}, u32[]{:S(2)}) collective-permute-start(bf16[384,128]{1,0:T(8,128)(2,1)S(1)} %collective-permute-done.20), channel_id=1, source_target_pairs={{0,1},{1,0},{2,3},{3,2},{4,5},{5,4},{6,7},{7,6},{8,9},{9,8},{10,11... | collective-permute-start | bytes 294920 | tf_op jit(solution)/shard_map/ppermute | solution.py:228
  283.3 5.9 %collective-permute-start.18 = (bf16[192,128]{1,0:T(8,128)(2,1)S(1)}, bf16[192,128]{1,0:T(8,128)(2,1)S(1)}, u32[]{:S(2)}, u32[]{:S(2)}) collective-permute-start(bf16[192,128]{1,0:T(8,128)(2,1)S(1)} %slice.51), channel_id=1, source_target_pairs={{0,2},{2,4},{4,6},{6,8},{8,10},{10,12},{12,14},{14,0},{1,3},{3,5},... | collective-permute-start | bytes 147464 | tf_op jit(solution)/shard_map/ppermute | solution.py:231
  284.0 6.5 %collective-permute-start.22 = (bf16[192,128]{1,0:T(8,128)(2,1)S(1)}, bf16[192,128]{1,0:T(8,128)(2,1)S(1)}, u32[]{:S(2)}, u32[]{:S(2)}) collective-permute-start(bf16[192,128]{1,0:T(8,128)(2,1)S(1)} %slice.52), channel_id=1, source_target_pairs={{0,14},{2,0},{4,2},{6,4},{8,6},{10,8},{12,10},{14,12},{1,15},{3,1}... | collective-permute-start | bytes 147464 | tf_op jit(solution)/shard_map/ppermute | solution.py:231
  294.2 12.7 %all-to-all-start.3 = ((bf16[16,24,448]{2,1,0:T(8,128)(2,1)}), bf16[16,24,448]{2,1,0:T(8,128)(2,1)S(1)}, u32[]{:S(2)}, u32[]{:S(2)}) async-start(bf16[16,24,448]{2,1,0:T(8,128)(2,1)} %bitcast.72), calls=%async_computation.3 | async-start | bytes 786432 | tf_op jit(solution)/shard_map/all_to_all | solution.py:347
  (30 other events, 232.0 us)
Sparse Core Ops, SparseCore 0:
  9.2 35.8 all-gather.7
  216.8 43.8 all-gather.5

commit v4 on v3

--- a/solution.py
+++ b/solution.py
@@ -15,6 +15,7 @@
 bf16 = jnp.bfloat16
 f32 = jnp.float32
 VMEM_LIMIT = 56 << 20
+NN = (((1,), (0,)), ((), ()))
 NT = (((1,), (1,)), ((), ()))
 
 
@@ -26,22 +27,16 @@
     return pl.CostEstimate(flops=flops, bytes_accessed=nbytes, transcendentals=0)
 
 
-def attend_kernel(lengths_ref, query_ref, prefix_ref, span_ref, uv_ref, out_ref):
-    step = pl.program_id(0)
-    length = lengths_ref[step]
-    span_rows, heads, width = query_ref.shape
-    latent, value = uv_ref.shape[1], uv_ref.shape[2]
-    span = span_ref[0]
-    prefix = prefix_ref[...].reshape(-1, width)
-    prefix_rows = prefix.shape[0]
-    rows = jnp.concatenate([query_ref[:, h, :] for h in range(heads)], axis=0)
-    first = lax.dot_general(rows, prefix, NT, preferred_element_type=f32) * score_scale
+def attend_one(rows, length, prefix, prefix_dims, span, uv_ref, latent, store):
+    total, span_rows = rows.shape[0], span.shape[0]
+    keys_first = prefix_dims is NT
+    cached = prefix[:, :latent] if keys_first else prefix[:latent]
+    first = lax.dot_general(rows, prefix, prefix_dims, preferred_element_type=f32) * score_scale
     second = lax.dot_general(rows, span, NT, preferred_element_type=f32) * score_scale
-    total = heads * span_rows
-    key = lax.broadcasted_iota(jnp.int32, (total, prefix_rows), 1)
+    key = lax.broadcasted_iota(jnp.int32, first.shape, 1)
     first = jnp.where(key < length, first, -jnp.inf)
-    token = lax.rem(lax.broadcasted_iota(jnp.int32, (total, span_rows), 0), span_rows)
-    late = lax.broadcasted_iota(jnp.int32, (total, span_rows), 1)
+    token = lax.rem(lax.broadcasted_iota(jnp.int32, second.shape, 0), span_rows)
+    late = lax.broadcasted_iota(jnp.int32, second.shape, 1)
     second = jnp.where(late <= token, second, -jnp.inf)
     highest = jnp.maximum(
         jnp.max(first, axis=1, keepdims=True), jnp.max(second, axis=1, keepdims=True)
@@ -49,50 +44,74 @@
     first = jnp.exp(first - highest)
     second = jnp.exp(second - highest)
     norm = jnp.sum(first, axis=1, keepdims=True) + jnp.sum(second, axis=1, keepdims=True)
-    out = jnp.dot((first / norm).astype(bf16), prefix[:, :latent], preferred_element_type=f32)
-    out += jnp.dot((second / norm).astype(bf16), span[:, :latent], preferred_element_type=f32)
+    first = (first / norm).astype(bf16)
+    second = (second / norm).astype(bf16)
+    out = lax.dot_general(first, cached, NN if keys_first else NT, preferred_element_type=f32)
+    out += jnp.dot(second, span[:, :latent], preferred_element_type=f32)
     out = out.astype(bf16)
-    for h in range(heads):
+    for h in range(total // span_rows):
         part = jnp.dot(
             out[h * span_rows : (h + 1) * span_rows], uv_ref[h], preferred_element_type=f32
         )
-        out_ref[:, h * value : (h + 1) * value] = part.astype(bf16)
-
-
-def attend(lengths, queries, prefix, prefix_spec, span, uv_weight, first_request, count):
-    span_rows, width = span.shape[1], span.shape[2]
-    heads = queries.shape[1]
-    latent, value = uv_weight.shape[1], uv_weight.shape[2]
-    keys = 288
+        store(h, part.astype(bf16))
+
+
+def own_kernel(lengths_ref, query_ref, prefix_ref, span_ref, uv_ref, out_ref, rows_ref):
+    heads, latent, value = uv_ref.shape
+    span_rows = span_ref.shape[1]
+    here = prefix_ref.shape[0]
+    turned = [query_ref[h].T for h in range(heads)]
+    for j in range(here + rows_ref.shape[0]):
+        at = slice(j * span_rows, (j + 1) * span_rows)
+        rows = jnp.concatenate([turned[h][at] for h in range(heads)], axis=0)
+        if j >= here:
+            rows_ref[j - here] = rows
+            continue
+
+        def store(h, part):
+            out_ref[at, h * value : (h + 1) * value] = part
+
+        attend_one(rows, lengths_ref[j], prefix_ref[j], NN, span_ref[j], uv_ref, latent, store)
+
+
+def moved_kernel(lengths_ref, rows_ref, prefix_ref, span_ref, uv_ref, out_ref):
+    heads, latent, value = uv_ref.shape
+    here, _, width = rows_ref.shape
+    span_rows = span_ref.shape[1]
+    for j in range(here):
+        at = slice(j * span_rows, (j + 1) * span_rows)
+
+        def store(h, part):
+            out_ref[at, h * value : (h + 1) * value] = part
+
+        prefix = prefix_ref[:, j].reshape(-1, width)
+        attend_one(rows_ref[j], lengths_ref[j], prefix, NT, span_ref[j], uv_ref, latent, store)
+
+
+def attend_call(kernel, operands, specs, shapes):
+    flops = 2 * 2 * 128 * (288 * (576 + 512) + 512 * 128)
+    outs = [jax.ShapeDtypeStruct(shape, bf16) for shape in shapes]
     return pl.pallas_call(
-        attend_kernel,
-        out_shape=jax.ShapeDtypeStruct((count * span_rows, heads * value), bf16),
-        grid_spec=pltpu.PrefetchScalarGridSpec(
-            num_scalar_prefetch=1,
-            grid=(count,),
-            in_specs=[
-                pl.BlockSpec((span_rows, heads, width), lambda j, n: (first_request + j, 0, 0)),
-                prefix_spec,
-                pl.BlockSpec((1, span_rows, width), lambda j, n: (first_request + j, 0, 0)),
-                pl.BlockSpec((heads, latent, value), lambda j, n: (0, 0, 0)),
-            ],
-            out_specs=pl.BlockSpec((span_rows, heads * value), lambda j, n: (j, 0)),
-        ),
+        kernel,
+        out_shape=outs,
+        in_specs=[pl.BlockSpec(memory_space=pltpu.SMEM)] + specs,
+        out_specs=[whole(shape) for shape in shapes],
+        grid=(1,),
         compiler_params=params(),
-        cost_estimate=cost(
-            2 * count * span_rows * heads * (keys * (width + latent) + latent * value),
-            2 * count * (span_rows * heads * width + keys * width) + 2 * heads * latent * value,
-        ),
-    )(lengths, queries, prefix, span, uv_weight)
+        cost_estimate=cost(flops, 2 << 20),
+    )(*operands)
+
+
+def whole(shape, block=0):
+    return pl.BlockSpec(tuple(shape), lambda i: (block,) + (0,) * (len(shape) - 1))
 
 
 def share_kernel(core_ref, values_ref, weight_ref, *refs):
     out_ref = refs[-1]
     nx, _, cols, rows = out_ref.shape
-    contract = (((0,), (1,)), ((), ()))
     for a in range(nx):
         piece = lax.dot_general(
-            weight_ref[0], values_ref[a], contract, preferred_element_type=f32
+            weight_ref[0], values_ref[a], NT, preferred_element_type=f32
         )
         if len(refs) == 2:
             piece += refs[0][a, 0].astype(f32)
@@ -101,7 +120,7 @@
 
 def project(core, values, weights, *other):
     nx, rows, depth = values.shape
-    blocks, _, cols = weights.shape
+    blocks, cols, _ = weights.shape
     half = blocks // 2
     piece = pl.BlockSpec((nx, 1, cols, rows), lambda i, c: (0, i, 0, 0))
     return pl.pallas_call(
@@ -112,7 +131,7 @@
             grid=(half,),
             in_specs=[
                 pl.BlockSpec((nx, rows, depth), lambda i, c: (0, 0, 0)),
-                pl.BlockSpec((1, depth, cols), lambda i, c: (2 * i + c[0], 0, 0)),
+                pl.BlockSpec((1, cols, depth), lambda i, c: (2 * i + c[0], 0, 0)),
             ]
             + [piece] * len(other),
             out_specs=piece,
@@ -177,6 +196,64 @@
             4 * nx * ny * rows * depth * ff, 2 * (nx * ny * rows * depth + 2 * ny * depth * ff)
         ),
     )(rows_in, gain, gate_weight, up_weight)
+
+
+def slices_kernel(layer_ref, in_ref, *out_refs):
+    step = pl.program_id(0)
+    for hops, out_ref in enumerate(out_refs):
+
+        @pl.when(step == hops)
+        def _(out_ref=out_ref):
+            out_ref[...] = in_ref[...]
+
+
+def slices_of(layer, array, count):
+    rows, columns = array.shape
+    width = columns // count
+    return pl.pallas_call(
+        slices_kernel,
+        out_shape=[jax.ShapeDtypeStruct((rows, width), array.dtype)] * count,
+        grid_spec=pltpu.PrefetchScalarGridSpec(
+            num_scalar_prefetch=1,
+            grid=(count,),
+            in_specs=[pl.BlockSpec((rows, width), lambda i, z: (0, lax.rem(z[0] + i, count)))],
+            out_specs=[pl.BlockSpec((rows, width), lambda i, z: (0, 0))] * count,
+        ),
+        compiler_params=params(),
+        cost_estimate=cost(0, 4 * rows * columns),
+    )(layer, array)
+
+
+def down_kernel(core_ref, *refs):
+    count = (len(refs) - 2) // 2
+    kept_ref, sent_ref = refs[-2:]
+    total = None
+    for hidden_ref, weight_ref in zip(refs[:count], refs[count : 2 * count]):
+        product = jnp.dot(hidden_ref[...], weight_ref[...], preferred_element_type=f32)
+        total = product if total is None else total + product
+    col = kept_ref.shape[1]
+    low, high = total[:, :col], total[:, col:]
+    first = core_ref[0] == 0
+    kept_ref[...] = jnp.where(first, low, high)
+    sent_ref[...] = jnp.where(first, high, low).astype(bf16)
+
+
+def down_project(core, hidden, weights):
+    rows = hidden[0].shape[0]
+    cols = weights[0].shape[1] // 2
+    operands = list(hidden) + list(weights)
+    return pl.pallas_call(
+        down_kernel,
+        out_shape=[
+            jax.ShapeDtypeStruct((rows, cols), f32),
+            jax.ShapeDtypeStruct((rows, cols), bf16),
+        ],
+        grid=(1,),
+        in_specs=[pl.BlockSpec(memory_space=pltpu.SMEM)] + [whole(o.shape) for o in operands],
+        out_specs=[whole((rows, cols))] * 2,
+        compiler_params=params(),
+        cost_estimate=cost(4 * rows * cols * 1024, 5 << 20),
+    )(core, *operands)
 
 
 def places_of(route_rows, experts):
@@ -238,13 +315,6 @@
     arrived = lax.all_to_all(
         jnp.broadcast_to(moving[None], (rank_count,) + moving.shape), DP, 0, 0, tiled=True
     )
-    chosen = jnp.stack(
-        [
-            lax.dynamic_index_in_dim(arrived[:, 0], source_first, 0, keepdims=False),
-            lax.dynamic_index_in_dim(arrived[:, 1], source_second, 0, keepdims=False),
-        ]
-    )
-    moved = lax.all_gather(chosen, MEM, axis=0)
     own_len = lax.dynamic_slice_in_dim(prefix_len, my_rank * requests, requests - 2)
     moved_len = jnp.concatenate(
         [
@@ -253,18 +323,8 @@
         ]
     )
 
-    out_cols = lax.all_gather(out_weight, "dy", axis=0)
-    down_t = down_weight[0].T.reshape(nz, 2, col, ff)
-    down_mine = lax.dynamic_index_in_dim(down_t, core, 1, keepdims=False)
-    down_other = other_core(lax.dynamic_index_in_dim(down_t, 1 - core, 1, keepdims=False))
-    down_pair = jnp.stack([down_mine, down_other], axis=1)
-
-    def down_for(hops):
-        piece = lax.dynamic_index_in_dim(down_pair, lax.rem(layer + hops, nz), 0, keepdims=False)
-        return along(piece, hops) if hops else piece
-
-    hop_order = list(range(nz))
-    down_parts = [down_for(hops) for hops in hop_order]
+    out_cols = lax.all_gather(out_weight.T, "dy", axis=0)
+    slices = slices_of(jnp.reshape(layer, (1,)), down_weight[0], nz)
     places = places_of(routes, rank_count)
     packed = jnp.concatenate(
         [
@@ -277,38 +337,68 @@
     )
     packed_t = lax.ppermute(packed, SWAP, swap)
 
-    part_rows = cache.shape[1]
-    values_own = attend(
-        own_len,
-        queries,
-        cache,
-        pl.BlockSpec((1, part_rows, cached_width), lambda j, n: (j, 0, 0)),
-        span_latent,
-        uv_weight,
-        0,
-        requests - 2,
-    )
-    values_moved = attend(
-        moved_len,
-        queries,
-        moved,
-        pl.BlockSpec((members, 1, part, cached_width), lambda j, n: (0, j, 0, 0)),
-        span_latent,
-        uv_weight,
-        requests - 2,
-        2,
+    down = {0: slices[0], 3: along(slices[3], 3), nz - 3: along(slices[nz - 3], -3)}
+    arrived, down[3], down[nz - 3] = lax.optimization_barrier((arrived, down[3], down[nz - 3]))
+    chosen = jnp.stack(
+        [
+            lax.dynamic_index_in_dim(arrived[:, 0], source_first, 0, keepdims=False),
+            lax.dynamic_index_in_dim(arrived[:, 1], source_second, 0, keepdims=False),
+        ]
+    )
+    moved = lax.all_gather(chosen, MEM, axis=0)
+
+    heads, latent = queries.shape[1], uv_weight.shape[1]
+    value = uv_weight.shape[2]
+    here = requests - 2
+    span_rows = span_latent.shape[1]
+    values_shape = (2 * span_rows, heads * value)
+    turned = (queries.transpose(1, 2, 0), cache.transpose(0, 2, 1))
+    spans = (2, span_rows, cached_width)
+    values_own, query_rows = attend_call(
+        own_kernel,
+        (own_len, *turned, span_latent, uv_weight),
+        [
+            whole(turned[0].shape),
+            whole((here, cached_width, prefix_rows)),
+            whole(spans),
+            whole(uv_weight.shape),
+        ],
+        [values_shape, (2, heads * span_rows, cached_width)],
+    )
+    (values_moved,) = attend_call(
+        moved_kernel,
+        (moved_len, query_rows, moved, span_latent, uv_weight),
+        [whole(query_rows.shape), whole(moved.shape), whole(spans, 1), whole(uv_weight.shape)],
+        [values_shape],
     )
     values = jnp.concatenate([values_own, values_moved], axis=0)
+
+    middle = nz // 2
+    rows_half = ff // 2
+    second = [slices[middle], slices[1], slices[nz - 1]]
+    second, _ = lax.optimization_barrier((second, moved))
+    second = [
+        along(second[0][:rows_half], middle),
+        along(second[0][rows_half:], -middle),
+        along(second[1], 1),
+        along(second[2], -1),
+    ]
 
     values_x = lax.all_gather(values, "dx", axis=0)
     core_at = jnp.reshape(core, (1,))
     sent = other_core(project(1 - core_at, values_x, out_cols))
     shares = project(core_at, values_x, out_cols, sent).reshape(nz, col, tok_rows)
-    shares, down_parts, packed_t = lax.optimization_barrier((shares, down_parts, packed_t))
+    shares, second, packed_t = lax.optimization_barrier((shares, second, packed_t))
+    down[middle] = jnp.concatenate(second[:2], axis=0)
+    down[1], down[nz - 1] = second[2:]
     shares = lax.all_to_all(shares, "ep", 0, 0, tiled=True)
     attended = jnp.sum(shares.astype(f32), axis=0)
     mixed_t = (packed_t[:col].astype(f32) + attended).astype(bf16)
     mixed = lax.ppermute(mixed_t, SWAP, swap)
+
+    third = [slices[2], slices[nz - 2]]
+    third, mixed_t = lax.optimization_barrier((third, mixed_t))
+    third = [along(third[0], 2), along(third[1], -2)]
 
     slot_index = jnp.arange(rank_count * capacity, dtype=jnp.int32)
     routes_t = packed_t[col : col + top_k].astype(jnp.int32)
@@ -320,6 +410,8 @@
     received = lax.all_to_all(outgoing, DP, 0, 0, tiled=True)
     received = received.reshape(nx, ny, capacity, col).transpose(1, 2, 0, 3)
     received = received.reshape(ny * capacity, nx * col)
+    received, third = lax.optimization_barrier((received, third))
+    down[2], down[nz - 2] = third
     rows_in = lax.all_gather(received, MEM, axis=0)
     rows_in, mixed = lax.optimization_barrier((rows_in, mixed))
     rows_in = rows_in.reshape(nx, ny, ny * capacity, nx * col)
@@ -339,10 +431,10 @@
         up_way, down_way = along(up_way, 1), along(down_way, -1)
         blocks[hops], blocks[nz - hops] = up_way, down_way
     blocks[nz // 2] = jnp.concatenate([along(up_way[:half], 1), along(down_way[half:], -1)], axis=0)
-    hidden_all = jnp.stack([jnp.stack([blocks[h], other_core(blocks[h])]) for h in hop_order])
-    down_all = jnp.stack(down_parts)
-    expert_out = jnp.einsum("dsrf,dscf->rc", hidden_all, down_all, preferred_element_type=f32)
-    expert_out = expert_out.astype(bf16).reshape(rank_count, capacity, col)
+    order = range(nz)
+    kept, sent = down_project(core_at, [blocks[h] for h in order], [down[h] for h in order])
+    expert_out = (kept + other_core(sent).astype(f32)).astype(bf16)
+    expert_out = expert_out.reshape(rank_count, capacity, col)
 
     returned = lax.all_to_all(expert_out, DP, 0, 0, tiled=True)
     returned = returned.reshape(rank_count * capacity, col)

time: 332 us -> 296 us (0.89)
  local copies, waits for them, and re-layouts: 29.2 us -> 9.07 us
  blocking collectives: 69.8 us -> 51.1 us
  Pallas kernels: 23 us -> 30.3 us
  starting transfers between devices: 73.2 us -> 66.4 us
  waiting for transfers between devices: 102 us -> 108 us
    all_to_all x1 -> x0, blocking collectives: 19.7 us -> none  [per_device(): received = lax.all_to_all(outgoing, DP, 0, 0, tiled=True)]
    unnamed x55 -> x46, local copies, waits for them, and re-layouts: 14.1 us -> 0.63 us
    ppermute x15 -> x16, starting transfers between devices: 43.2 us -> 31.9 us  [along(): return lax.ppermute(array, 'ep', [(z, (z + hops) % nz) for z in range(nz)])]
    pallas_call x2 -> x4, Pallas kernels: 9.32 us -> 17.5 us  [the longest x2 7.39 us: attend_call(): pl.pallas_call(kernel, out_shape=outs, in_specs=[pl.BlockSpec(memory_spac...]
    all_to_all x0 -> x1, starting transfers between devices: none -> 8.16 us  [per_device(): received = lax.all_to_all(outgoing, DP, 0, 0, tiled=True)]
    all_gather x1, waiting for transfers between devices: 39.1 us -> 46.4 us  [per_device(): rows_in = lax.all_gather(received, MEM, axis=0)]
    ppermute x15 -> x16, waiting for transfers between devices: 28.4 us -> 22.1 us  [along(): return lax.ppermute(array, 'ep', [(z, (z + hops) % nz) for z in range(nz)])]
    all_to_all x0 -> x1, waiting for transfers between devices: none -> 5.34 us  [per_device(): received = lax.all_to_all(outgoing, DP, 0, 0, tiled=True)]
  transfers between devices with their start and end apart: 32 -> 26, of which waited for: 10 -> 13; matrix products, arithmetic and copies ran while one was open for 10% -> 4% of each run, Pallas kernels for 5% -> 6%
where the time goes in v4:
time: 296 us; the launch traced here: 295 us
  waiting for transfers between devices  108 us (36%)
  starting transfers between devices  66.4 us (22%)
  blocking collectives  51.1 us (17%)
  Pallas kernels  30.3 us (10%)
  between operations  19 us (6%)
  other arithmetic  9.66 us (3%)
  local copies, waits for them, and re-layouts  9.07 us (3%)
    all_gather x1, waiting for transfers between devices, per_device(): rows_in = lax.all_gather(received, MEM, axis=0)  46.4 us
    ppermute x16, starting transfers between devices, along(): return lax.ppermute(array, 'ep', [(z, (z + hops) % nz) for z in range(nz)])  31.9 us
    all_gather x1, blocking collectives, per_device(): moved = lax.all_gather(chosen, MEM, axis=0)  24.3 us
    all_to_all x1, waiting for transfers between devices, per_device(): shares = lax.all_to_all(shares, 'ep', 0, 0, tiled=True)  23.3 us
    ppermute x16, waiting for transfers between devices, along(): return lax.ppermute(array, 'ep', [(z, (z + hops) % nz) for z in range(nz)])  22.1 us
    all_to_all x1, blocking collectives, per_device(): lax.all_to_all(total.reshape(members, tok_rows // members, col), MEM, 0,...  15.3 us
    all_gather x1, blocking collectives, per_device(): values_x = lax.all_gather(values, 'dx', axis=0)  11.5 us
    all_to_all x1, waiting for transfers between devices, per_device(): returned = lax.all_to_all(expert_out, DP, 0, 0, tiled=True)  9.09 us
  transfers between devices with their start and end apart: 26, of which 13 were waited for; matrix products, arithmetic and copies ran while one was open for 4% of the time, Pallas kernels for 6%

profile of v4, /device:TPU:1, one launch (start us, length us, event | category | flops | bytes accessed | tf_op | source)
XLA Modules:
  0.0 294.6 jit_solution(13374616368077797103)
XLA Ops:
  9.4 7.6 %all-to-all-start = ((bf16[16,2,16,576]{3,2,1,0:T(8,128)(2,1)}), bf16[16,2,16,576]{3,2,1,0:T(8,128)(2,1)S(1)}, u32[]{:S(2)}, u32[]{:S(2)}) async-start(bf16[16,2,16,576]{3,2,1,0:T(8,128)(2,1)} %broadcast_in_dim.12), calls=%async_computation | async-start | bytes 1310720 | tf_op jit(solution)/shard_map/all_to_all | solution.py:315
  17.0 5.4 %shard_map.137 = (bf16[128,896]{1,0:T(8,128)(2,1)}, bf16[128,896]{1,0:T(8,128)(2,1)}, bf16[128,896]{1,0:T(8,128)(2,1)}, bf16[128,896]{1,0:T(8,128)(2,1)}, bf16[1...) custom-call(s32[1]{0:T(128)} %bitcast.5.layer_ref, ...), custom_call_target="tpu_custom_call" | custom-call | bytes 3670016 | tf_op jit(solution)/shard_map/pallas_call | solution.py:213
  22.4 4.3 %collective-permute-start = (bf16[128,896]{1,0:T(8,128)(2,1)}, bf16[128,896]{1,0:T(8,128)(2,1)S(1)}, u32[]{:S(2)}, u32[]{:S(2)}) collective-permute-start(bf16[128,896]{1,0:T(8,128)(2,1)} %get-tuple-element.39), channel_id=1, source_target_pairs={{0,6},{2,8},{4,10},{6,12},{8,14},{10,0},{12,2},{14,4},{1,7},{3,9},... | collective-permute-start | bytes 688136 | tf_op jit(solution)/shard_map/ppermute | solution.py:308
  34.0 3.8 %shard_map.136 = (bf16[64,512]{1,0:T(8,128)(2,1)}, bf16[2,128,576]{2,1,0:T(8,128)(2,1)}) custom-call(s32[2]{0:T(128)} %dynamic_slice.26.lengths_ref, bf16[4,576,128]{2,1,0:T(8,128)(2,1)} %bitcast.85, bf16[4,576,256]{2,1,0:T(8,128)(2,1)} %bitcast.77, bf16[4,32,576]{2,1,0:T(8,128)(2,1)} %span_ref.3, bf16[4,512,128]{2,1,0:T(8,128)(2,1)} %uv_ref.3), custom_call_target="tpu_custom_call" | custom-call | flops 193986560 | bytes 2097152 | tf_op jit(solution)/shard_map/pallas_call | solution.py:94
  42.1 24.3 %all-gather = bf16[32,16,576]{2,1,0:T(8,128)(2,1)} all-gather(bf16[2,16,576]{2,1,0:T(8,128)(2,1)S(1)} %pad_maximum_fusion.3), channel_id=2, replica_groups=mesh['dx'=4,'dy'=4,'ep'=8,'tp'=2] {'ep','tp'}, dimensions={0}, use_global_device_ids=true | all-gather | bytes 626688 | tf_op jit(solution)/shard_map/all_gather | solution.py:348
  66.4 3.6 %shard_map.138 = bf16[64,512]{1,0:T(8,128)(2,1)} custom-call(s32[2]{0:T(128)} %pad_add_fusion.lengths_ref, bf16[2,128,576]{2,1,0:T(8,128)(2,1)} %get-tuple-element.38.rows_ref, bf16[16,2,16,576]{3,2,1,0:T(8,128)(2,1)} %bitcast.78, bf16[4,32,576]{2,1,0:T(8,128)(2,1)} %span_ref.3, bf16[4,512,128]{2,1,0:T(8,128)(2,1)} %uv_ref.3), custom_call_target="tpu_custom_call" | custom-call | flops 193986560 | bytes 2097152 | tf_op jit(solution)/shard_map/pallas_call | solution.py:94
  70.9 11.5 %all-gather.1 = bf16[512,512]{1,0:T(8,128)(2,1)} all-gather(bf16[128,512]{1,0:T(8,128)(2,1)S(1)} %pad_maximum_fusion.1), channel_id=3, replica_groups=mesh['dx'=4,'dy'=4,'ep'=8,'tp'=2] {'dx'}, dimensions={0}, use_global_device_ids=true | all-gather | bytes 655360 | tf_op jit(solution)/shard_map/all_gather | solution.py:387
  91.0 5.5 %collective-permute-start.6 = (bf16[128,896]{1,0:T(8,128)(2,1)}, bf16[128,896]{1,0:T(8,128)(2,1)S(1)}, u32[]{:S(2)}, u32[]{:S(2)}) collective-permute-start(bf16[128,896]{1,0:T(8,128)(2,1)} %get-tuple-element.47), channel_id=1, source_target_pairs={{0,14},{2,0},{4,2},{6,4},{8,6},{10,8},{12,10},{14,12},{1,15},{3,1}... | collective-permute-start | bytes 688136 | tf_op jit(solution)/shard_map/ppermute | solution.py:308
  96.4 4.8 %collective-permute-start.3 = (bf16[64,896]{1,0:T(8,128)(2,1)S(1)}, bf16[64,896]{1,0:T(8,128)(2,1)S(1)}, u32[]{:S(2)}, u32[]{:S(2)}) collective-permute-start(bf16[64,896]{1,0:T(8,128)(2,1)S(1)} %get-tuple-element.74), channel_id=1, source_target_pairs={{0,8},{2,10},{4,12},{6,14},{8,0},{10,2},{12,4},{14,6},{1,9},{3,11}... | collective-permute-start | bytes 344072 | tf_op jit(solution)/shard_map/ppermute | solution.py:308
  102.2 3.4 %shard_map.140 = bf16[4,2,448,128]{3,2,1,0:T(8,128)(2,1)} custom-call(s32[1]{0:T(128)} %bitcast.core_ref, bf16[4,128,512]{2,1,0:T(8,128)(2,1)} %bitcast.75, bf16[4,448,512]{2,1,0:T(8,128)(2,1)} %bitcast.72, bf16[4,2,448,128]{3,2,1,0:T(8,128)(2,1)} %copy-done.1), custom_call_target="tpu_custom_call" | custom-call | flops 469762048 | bytes 2359296 | tf_op jit(solution)/shard_map/pallas_call | solution.py:126
  105.6 6.3 %collective-permute-done.3 = bf16[64,896]{1,0:T(8,128)(2,1)S(1)} collective-permute-done((bf16[64,896]{1,0:T(8,128)(2,1)S(1)}, bf16[64,896]{1,0:T(8,128)(2,1)S(1)}, u32[]{:S(2)}, u32[]{:S(2)}) %collective-permute-start.3) | collective-permute-done | bytes 114720 | tf_op jit(solution)/shard_map/ppermute | solution.py:308
  111.9 4.6 %collective-permute-done.4 = bf16[64,896]{1,0:T(8,128)(2,1)S(1)} collective-permute-done((bf16[64,896]{1,0:T(8,128)(2,1)S(1)}, bf16[64,896]{1,0:T(8,128)(2,1)S(1)}, u32[]{:S(2)}, u32[]{:S(2)}) %collective-permute-start.4) | collective-permute-done | bytes 114720 | tf_op jit(solution)/shard_map/ppermute | solution.py:308
  119.5 3.6 %all-to-all-start.1 = ((bf16[8,448,128]{2,1,0:T(8,128)(2,1)}), bf16[8,448,128]{2,1,0:T(8,128)(2,1)S(1)}, u32[]{:S(2)}, u32[]{:S(2)}) async-start(bf16[8,448,128]{2,1,0:T(8,128)(2,1)} %bitcast.76), calls=%async_computation.1 | async-start | bytes 1835008 | tf_op jit(solution)/shard_map/all_to_all | solution.py:394
  123.9 23.3 %all-to-all-done.1 = bf16[8,448,128]{2,1,0:T(8,128)(2,1)S(1)} async-done(((bf16[8,448,128]{2,1,0:T(8,128)(2,1)}), bf16[8,448,128]{2,1,0:T(8,128)(2,1)S(1)}, u32[]{:S(2)}, u32[]{:S(2)}) %all-to-all-start.1) | async-done | bytes 917536 | tf_op jit(solution)/shard_map/all_to_all | solution.py:394
  149.5 8.2 %all-to-all-start.2 = ((bf16[16,24,448]{2,1,0:T(8,128)(2,1)}), bf16[16,24,448]{2,1,0:T(8,128)(2,1)S(1)}, u32[]{:S(2)}, u32[]{:S(2)}) async-start(bf16[16,24,448]{2,1,0:T(8,128)(2,1)} %bitcast.18), calls=%async_computation.2 | async-start | bytes 786432 | tf_op jit(solution)/shard_map/all_to_all | solution.py:410
  157.8 3.6 %collective-permute-start.9 = (bf16[128,896]{1,0:T(8,128)(2,1)}, bf16[128,896]{1,0:T(8,128)(2,1)S(1)}, u32[]{:S(2)}, u32[]{:S(2)}) collective-permute-start(bf16[128,896]{1,0:T(8,128)(2,1)} %get-tuple-element.54), channel_id=1, source_target_pairs={{0,12},{2,14},{4,0},{6,2},{8,4},{10,6},{12,8},{14,10},{1,13},{3,15... | collective-permute-start | bytes 688136 | tf_op jit(solution)/shard_map/ppermute | solution.py:308
  161.3 5.3 %all-to-all-done.2 = bf16[16,24,448]{2,1,0:T(8,128)(2,1)S(1)} async-done(((bf16[16,24,448]{2,1,0:T(8,128)(2,1)}), bf16[16,24,448]{2,1,0:T(8,128)(2,1)S(1)}, u32[]{:S(2)}, u32[]{:S(2)}) %all-to-all-start.2) | async-done | bytes 344096 | tf_op jit(solution)/shard_map/all_to_all | solution.py:410
  170.3 46.4 %all-gather.9.cloned.1.call-done = bf16[1536,1792]{1,0:T(8,128)(2,1)} async-done(((bf16[96,1792]{1,0:T(8,128)(2,1)}), bf16[1536,1792]{1,0:T(8,128)(2,1)}) %all-gather.9.cloned.1.call-update) | async-done | bytes 5505040 | tf_op jit(solution)/shard_map/all_gather | solution.py:415
  216.6 6.1 %shard_map.141.refs_0_ = bf16[384,128]{1,0:T(8,128)(2,1)} custom-call(bf16[4,4,96,1792]{3,2,1,0:T(8,128)(2,1)} %bitcast.73, f32[4,1,1792]{2,1,0:T(1,128)} %reshape.97.gain_ref, bf16[4,4,448,128]{3,2,1,0:T(8,128)(2,1)} %bitcast.79, bf16[4,4,448,128]{3,2,1,0:T(8,128)(2,1)} %bitcast.80), custom_call_target="tpu_custom_call" | custom-call | flops 1409286144 | bytes 9175040 | tf_op jit(solution)/shard_map/pallas_call | solution.py:182
  242.6 4.7 %shard_map.142 = (f32[384,448]{1,0:T(8,128)}, bf16[384,448]{1,0:T(8,128)(2,1)}) custom-call(s32[1]{0:T(128)} %bitcast.core_ref, bf16[384,128]{1,0:T(8,128)(2,1)} %shard_map.141.refs_0_, bf16[384,128]{1,0:T(8,128)(2,1)} %copy-done.12, bf16[384,128]{1,0:T(8,128)(2,1)} %copy-done.14, bf16[384,128]{1,0:T(8,128)(2,1)} %copy-done.9, ...), custom_call_target="tpu_custom_call" | custom-call | flops 704643072 | bytes 5242880 | tf_op jit(solution)/shard_map/pallas_call | solution.py:245
  247.3 4.6 %collective-permute-start.19 = (bf16[384,448]{1,0:T(8,128)(2,1)}, bf16[384,448]{1,0:T(8,128)(2,1)S(1)}, u32[]{:S(2)}, u32[]{:S(2)}) collective-permute-start(bf16[384,448]{1,0:T(8,128)(2,1)} %get-tuple-element.68), channel_id=1, source_target_pairs={{0,1},{1,0},{2,3},{3,2},{4,5},{5,4},{6,7},{7,6},{8,9},{9,8},{10,11... | collective-permute-start | bytes 1032200 | tf_op jit(solution)/shard_map/ppermute | solution.py:305
  255.4 6.5 %all-to-all-start.3 = ((bf16[16,24,448]{2,1,0:T(8,128)(2,1)}), bf16[16,24,448]{2,1,0:T(8,128)(2,1)S(1)}, u32[]{:S(2)}, u32[]{:S(2)}) async-start(bf16[16,24,448]{2,1,0:T(8,128)(2,1)} %bitcast.29), calls=%async_computation.3 | async-start | bytes 786432 | tf_op jit(solution)/shard_map/all_to_all | solution.py:439
  262.1 9.1 %all-to-all-done.3 = bf16[16,24,448]{2,1,0:T(8,128)(2,1)S(1)} async-done(((bf16[16,24,448]{2,1,0:T(8,128)(2,1)}), bf16[16,24,448]{2,1,0:T(8,128)(2,1)S(1)}, u32[]{:S(2)}, u32[]{:S(2)}) %all-to-all-start.3) | async-done | bytes 344096 | tf_op jit(solution)/shard_map/all_to_all | solution.py:439
  271.6 15.3 %all_to_all.25 = bf16[16,8,448]{2,1,0:T(8,128)(2,1)S(1)} all-to-all(bf16[16,8,448]{2,1,0:T(8,128)(2,1)S(1)} %bitcast.86), channel_id=1, replica_groups=mesh['dx'=4,'dy'=4,'ep'=8,'tp'=2] {'ep','tp'}, dimensions={0} | all-to-all | bytes 229376 | tf_op jit(solution)/shard_map/all_to_all | solution.py:448
  (136 shorter events, 53.9 us)
Async XLA Ops:
  6.5 75.9 %all-gather.7.cloned.1.call-start = ((), (), s32[]{:S(2)}) async-start(), calls=%async_computation.5 | async-start | bytes 2293760 | tf_op jit(solution)/shard_map/all_gather | solution.py:326
  9.4 32.6 %all-to-all-start = ((bf16[16,2,16,576]{3,2,1,0:T(8,128)(2,1)}), bf16[16,2,16,576]{3,2,1,0:T(8,128)(2,1)S(1)}, u32[]{:S(2)}, u32[]{:S(2)}) async-start(bf16[16,2,16,576]{3,2,1,0:T(8,128)(2,1)} %broadcast_in_dim.12), calls=%async_computation | async-start | bytes 1310720 | tf_op jit(solution)/shard_map/all_to_all | solution.py:315
  22.4 19.6 %collective-permute-start = (bf16[128,896]{1,0:T(8,128)(2,1)}, bf16[128,896]{1,0:T(8,128)(2,1)S(1)}, u32[]{:S(2)}, u32[]{:S(2)}) collective-permute-start(bf16[128,896]{1,0:T(8,128)(2,1)} %get-tuple-element.39), channel_id=1, source_target_pairs={{0,6},{2,8},{4,10},{6,12},{8,14},{10,0},{12,2},{14,4},{1,7},{3,9},... | collective-permute-start | bytes 688136 | tf_op jit(solution)/shard_map/ppermute | solution.py:308
  26.8 15.2 %collective-permute-start.1 = (bf16[128,896]{1,0:T(8,128)(2,1)}, bf16[128,896]{1,0:T(8,128)(2,1)S(1)}, u32[]{:S(2)}, u32[]{:S(2)}) collective-permute-start(bf16[128,896]{1,0:T(8,128)(2,1)} %get-tuple-element.40), channel_id=1, source_target_pairs={{0,10},{2,12},{4,14},{6,0},{8,2},{10,4},{12,6},{14,8},{1,11},{3,13... | collective-permute-start | bytes 688136 | tf_op jit(solution)/shard_map/ppermute | solution.py:308
  85.7 15.5 %collective-permute-start.2 = (bf16[4,2,448,128]{3,2,1,0:T(8,128)(2,1)}, bf16[4,2,448,128]{3,2,1,0:T(8,128)(2,1)S(1)}, u32[]{:S(2)}, u32[]{:S(2)}) collective-permute-start(bf16[4,2,448,128]{3,2,1,0:T(8,128)(2,1)} %shard_map.139), channel_id=1, source_target_pairs={{0,1},{1,0},{2,3},{3,2},{4,5},{5,4},{6,7},{7,6},{8,9},{9,8},{10,11... | collective-permute-start | bytes 2752520 | tf_op jit(solution)/shard_map/ppermute | solution.py:305
  90.2 15.4 %collective-permute-start.7 = (bf16[464,128]{1,0:T(8,128)(2,1)S(1)}, bf16[464,128]{1,0:T(8,128)(2,1)S(1)}, u32[]{:S(2)}, u32[]{:S(2)}) collective-permute-start(bf16[464,128]{1,0:T(8,128)(2,1)S(1)} %maximum_maximum_fusion), channel_id=1, source_target_pairs={{0,0},{1,1},{2,2},{3,3},{4,64},{5,65},{6,66},{7,67},{8,128},{9,129... | collective-permute-start | bytes 356360 | tf_op jit(solution)/shard_map/ppermute | solution.py:338
  90.9 28.6 %collective-permute-start.5 = (bf16[128,896]{1,0:T(8,128)(2,1)}, bf16[128,896]{1,0:T(8,128)(2,1)S(1)}, u32[]{:S(2)}, u32[]{:S(2)}) collective-permute-start(bf16[128,896]{1,0:T(8,128)(2,1)} %get-tuple-element.46), channel_id=1, source_target_pairs={{0,2},{2,4},{4,6},{6,8},{8,10},{10,12},{12,14},{14,0},{1,3},{3,5},... | collective-permute-start | bytes 688136 | tf_op jit(solution)/shard_map/ppermute | solution.py:308
  91.0 28.5 %collective-permute-start.6 = (bf16[128,896]{1,0:T(8,128)(2,1)}, bf16[128,896]{1,0:T(8,128)(2,1)S(1)}, u32[]{:S(2)}, u32[]{:S(2)}) collective-permute-start(bf16[128,896]{1,0:T(8,128)(2,1)} %get-tuple-element.47), channel_id=1, source_target_pairs={{0,14},{2,0},{4,2},{6,4},{8,6},{10,8},{12,10},{14,12},{1,15},{3,1}... | collective-permute-start | bytes 688136 | tf_op jit(solution)/shard_map/ppermute | solution.py:308
  96.4 15.5 %collective-permute-start.3 = (bf16[64,896]{1,0:T(8,128)(2,1)S(1)}, bf16[64,896]{1,0:T(8,128)(2,1)S(1)}, u32[]{:S(2)}, u32[]{:S(2)}) collective-permute-start(bf16[64,896]{1,0:T(8,128)(2,1)S(1)} %get-tuple-element.74), channel_id=1, source_target_pairs={{0,8},{2,10},{4,12},{6,14},{8,0},{10,2},{12,4},{14,6},{1,9},{3,11}... | collective-permute-start | bytes 344072 | tf_op jit(solution)/shard_map/ppermute | solution.py:308
  101.3 15.3 %collective-permute-start.4 = (bf16[64,896]{1,0:T(8,128)(2,1)S(1)}, bf16[64,896]{1,0:T(8,128)(2,1)S(1)}, u32[]{:S(2)}, u32[]{:S(2)}) collective-permute-start(bf16[64,896]{1,0:T(8,128)(2,1)S(1)} %get-tuple-element.73), channel_id=1, source_target_pairs={{0,8},{2,10},{4,12},{6,14},{8,0},{10,2},{12,4},{14,6},{1,9},{3,11}... | collective-permute-start | bytes 344072 | tf_op jit(solution)/shard_map/ppermute | solution.py:308
  119.5 27.7 %all-to-all-start.1 = ((bf16[8,448,128]{2,1,0:T(8,128)(2,1)}), bf16[8,448,128]{2,1,0:T(8,128)(2,1)S(1)}, u32[]{:S(2)}, u32[]{:S(2)}) async-start(bf16[8,448,128]{2,1,0:T(8,128)(2,1)} %bitcast.76), calls=%async_computation.1 | async-start | bytes 1835008 | tf_op jit(solution)/shard_map/all_to_all | solution.py:394
  149.5 17.2 %all-to-all-start.2 = ((bf16[16,24,448]{2,1,0:T(8,128)(2,1)}), bf16[16,24,448]{2,1,0:T(8,128)(2,1)S(1)}, u32[]{:S(2)}, u32[]{:S(2)}) async-start(bf16[16,24,448]{2,1,0:T(8,128)(2,1)} %bitcast.18), calls=%async_computation.2 | async-start | bytes 786432 | tf_op jit(solution)/shard_map/all_to_all | solution.py:410
  157.6 59.0 %all-gather.9.cloned.1.call-start = ((), (), s32[]{:S(2)}) async-start(), calls=%async_computation.6 | async-start | bytes 5849088 | tf_op jit(solution)/shard_map/all_gather | solution.py:415
  157.7 10.4 %collective-permute-start.8 = (bf16[128,896]{1,0:T(8,128)(2,1)}, bf16[128,896]{1,0:T(8,128)(2,1)S(1)}, u32[]{:S(2)}, u32[]{:S(2)}) collective-permute-start(bf16[128,896]{1,0:T(8,128)(2,1)} %get-tuple-element.53), channel_id=1, source_target_pairs={{0,4},{2,6},{4,8},{6,10},{8,12},{10,14},{12,0},{14,2},{1,5},{3,7},... | collective-permute-start | bytes 688136 | tf_op jit(solution)/shard_map/ppermute | solution.py:308
  157.8 11.0 %collective-permute-start.9 = (bf16[128,896]{1,0:T(8,128)(2,1)}, bf16[128,896]{1,0:T(8,128)(2,1)S(1)}, u32[]{:S(2)}, u32[]{:S(2)}) collective-permute-start(bf16[128,896]{1,0:T(8,128)(2,1)} %get-tuple-element.54), channel_id=1, source_target_pairs={{0,12},{2,14},{4,0},{6,2},{8,4},{10,6},{12,8},{14,10},{1,13},{3,15... | collective-permute-start | bytes 688136 | tf_op jit(solution)/shard_map/ppermute | solution.py:308
  222.7 5.6 %collective-permute-start.11 = (bf16[384,128]{1,0:T(8,128)(2,1)}, bf16[384,128]{1,0:T(8,128)(2,1)S(1)}, u32[]{:S(2)}, u32[]{:S(2)}) collective-permute-start(bf16[384,128]{1,0:T(8,128)(2,1)} %shard_map.141.refs_0_), channel_id=1, source_target_pairs={{0,2},{2,4},{4,6},{6,8},{8,10},{10,12},{12,14},{14,0},{1,3},{3,5},... | collective-permute-start | bytes 294920 | tf_op jit(solution)/shard_map/ppermute | solution.py:308
  223.8 4.6 %collective-permute-start.15 = (bf16[384,128]{1,0:T(8,128)(2,1)}, bf16[384,128]{1,0:T(8,128)(2,1)S(1)}, u32[]{:S(2)}, u32[]{:S(2)}) collective-permute-start(bf16[384,128]{1,0:T(8,128)(2,1)} %shard_map.141.refs_0_), channel_id=1, source_target_pairs={{0,14},{2,0},{4,2},{6,4},{8,6},{10,8},{12,10},{14,12},{1,15},{3,1}... | collective-permute-start | bytes 294920 | tf_op jit(solution)/shard_map/ppermute | solution.py:308
  228.4 4.7 %collective-permute-start.12 = (bf16[384,128]{1,0:T(8,128)(2,1)S(1)}, bf16[384,128]{1,0:T(8,128)(2,1)S(1)}, u32[]{:S(2)}, u32[]{:S(2)}) collective-permute-start(bf16[384,128]{1,0:T(8,128)(2,1)S(1)} %collective-permute-done.11.refs_1_), channel_id=1, source_target_pairs={{0,2},{2,4},{4,6},{6,8},{8,10},{10,12},{12,14},{14,0},{1,3},{3,5},... | collective-permute-start | bytes 294920 | tf_op jit(solution)/shard_map/ppermute | solution.py:308
  228.4 4.7 %collective-permute-start.16 = (bf16[384,128]{1,0:T(8,128)(2,1)S(1)}, bf16[384,128]{1,0:T(8,128)(2,1)S(1)}, u32[]{:S(2)}, u32[]{:S(2)}) collective-permute-start(bf16[384,128]{1,0:T(8,128)(2,1)S(1)} %collective-permute-done.15.refs_7_), channel_id=1, source_target_pairs={{0,14},{2,0},{4,2},{6,4},{8,6},{10,8},{12,10},{14,12},{1,15},{3,1}... | collective-permute-start | bytes 294920 | tf_op jit(solution)/shard_map/ppermute | solution.py:308
  233.1 4.7 %collective-permute-start.13 = (bf16[384,128]{1,0:T(8,128)(2,1)S(1)}, bf16[384,128]{1,0:T(8,128)(2,1)S(1)}, u32[]{:S(2)}, u32[]{:S(2)}) collective-permute-start(bf16[384,128]{1,0:T(8,128)(2,1)S(1)} %collective-permute-done.12.refs_2_), channel_id=1, source_target_pairs={{0,2},{2,4},{4,6},{6,8},{8,10},{10,12},{12,14},{14,0},{1,3},{3,5},... | collective-permute-start | bytes 294920 | tf_op jit(solution)/shard_map/ppermute | solution.py:308
  233.1 4.7 %collective-permute-start.17 = (bf16[384,128]{1,0:T(8,128)(2,1)S(1)}, bf16[384,128]{1,0:T(8,128)(2,1)S(1)}, u32[]{:S(2)}, u32[]{:S(2)}) collective-permute-start(bf16[384,128]{1,0:T(8,128)(2,1)S(1)} %collective-permute-done.16.refs_6_), channel_id=1, source_target_pairs={{0,14},{2,0},{4,2},{6,4},{8,6},{10,8},{12,10},{14,12},{1,15},{3,1}... | collective-permute-start | bytes 294920 | tf_op jit(solution)/shard_map/ppermute | solution.py:308
  237.7 4.2 %collective-permute-start.14 = (bf16[192,128]{1,0:T(8,128)(2,1)S(1)}, bf16[192,128]{1,0:T(8,128)(2,1)S(1)}, u32[]{:S(2)}, u32[]{:S(2)}) collective-permute-start(bf16[192,128]{1,0:T(8,128)(2,1)S(1)} %slice.57), channel_id=1, source_target_pairs={{0,2},{2,4},{4,6},{6,8},{8,10},{10,12},{12,14},{14,0},{1,3},{3,5},... | collective-permute-start | bytes 147464 | tf_op jit(solution)/shard_map/ppermute | solution.py:308
  247.3 6.1 %collective-permute-start.19 = (bf16[384,448]{1,0:T(8,128)(2,1)}, bf16[384,448]{1,0:T(8,128)(2,1)S(1)}, u32[]{:S(2)}, u32[]{:S(2)}) collective-permute-start(bf16[384,448]{1,0:T(8,128)(2,1)} %get-tuple-element.68), channel_id=1, source_target_pairs={{0,1},{1,0},{2,3},{3,2},{4,5},{5,4},{6,7},{7,6},{8,9},{9,8},{10,11... | collective-permute-start | bytes 1032200 | tf_op jit(solution)/shard_map/ppermute | solution.py:305
  255.4 15.8 %all-to-all-start.3 = ((bf16[16,24,448]{2,1,0:T(8,128)(2,1)}), bf16[16,24,448]{2,1,0:T(8,128)(2,1)S(1)}, u32[]{:S(2)}, u32[]{:S(2)}) async-start(bf16[16,24,448]{2,1,0:T(8,128)(2,1)} %bitcast.29), calls=%async_computation.3 | async-start | bytes 786432 | tf_op jit(solution)/shard_map/all_to_all | solution.py:439
  (25 other events, 527.9 us)
Sparse Core Ops, SparseCore 0:
  9.2 35.8 all-gather.6
  168.9 47.7 all-gather.8

commit v5 on v4

v5 whole, which is shorter than its diff:
```python
import functools

import jax
import jax.numpy as jnp
from jax import lax
from jax.experimental import pallas as pl
from jax.experimental.pallas import tpu as pltpu
from jax.sharding import PartitionSpec as P

score_scale = 192.0 ** (-0.5)
norm_eps = 1e-06
DP = ("dp",)
MEM = ("ep", "tp")
bf16 = jnp.bfloat16
f32 = jnp.float32
VMEM_LIMIT = 56 << 20
NN = (((1,), (0,)), ((), ()))
NT = (((1,), (1,)), ((), ()))


def params():
    return pltpu.CompilerParams(vmem_limit_bytes=VMEM_LIMIT)


def cost(flops, nbytes):
    return pl.CostEstimate(flops=flops, bytes_accessed=nbytes, transcendentals=0)


def attend_one(rows, length, prefix, prefix_dims, span, uv_ref, latent, store):
    total, span_rows = rows.shape[0], span.shape[0]
    keys_first = prefix_dims is NT
    cached = prefix[:, :latent] if keys_first else prefix[:latent]
    first = lax.dot_general(rows, prefix, prefix_dims, preferred_element_type=f32) * score_scale
    second = lax.dot_general(rows, span, NT, preferred_element_type=f32) * score_scale
    key = lax.broadcasted_iota(jnp.int32, first.shape, 1)
    first = jnp.where(key < length, first, -jnp.inf)
    token = lax.rem(lax.broadcasted_iota(jnp.int32, second.shape, 0), span_rows)
    late = lax.broadcasted_iota(jnp.int32, second.shape, 1)
    second = jnp.where(late <= token, second, -jnp.inf)
    highest = jnp.maximum(
        jnp.max(first, axis=1, keepdims=True), jnp.max(second, axis=1, keepdims=True)
    )
    first = jnp.exp(first - highest)
    second = jnp.exp(second - highest)
    norm = jnp.sum(first, axis=1, keepdims=True) + jnp.sum(second, axis=1, keepdims=True)
    first = (first / norm).astype(bf16)
    second = (second / norm).astype(bf16)
    out = lax.dot_general(first, cached, NN if keys_first else NT, preferred_element_type=f32)
    out += jnp.dot(second, span[:, :latent], preferred_element_type=f32)
    out = out.astype(bf16)
    for h in range(total // span_rows):
        part = jnp.dot(
            out[h * span_rows : (h + 1) * span_rows], uv_ref[h], preferred_element_type=f32
        )
        store(h, part.astype(bf16))


def own_kernel(rank_ref, lengths_ref, destination_ref, query_ref, prefix_ref, span_ref, uv_ref, out_ref, rows_ref):
    heads, latent, value = uv_ref.shape
    span_rows = span_ref.shape[1]
    here = prefix_ref.shape[0]
    turned = [query_ref[h].T for h in range(heads)]
    for j in range(here + rows_ref.shape[0]):
        at = slice(j * span_rows, (j + 1) * span_rows)
        rows = jnp.concatenate([turned[h][at] for h in range(heads)], axis=0)
        if j >= here:
            rows_ref[j - here] = rows
            continue

        def store(h, part):
            out_ref[at, h * value : (h + 1) * value] = part

        length = lengths_ref[rank_ref[0] * (here + rows_ref.shape[0]) + j]
        attend_one(rows, length, prefix_ref[j], NN, span_ref[j], uv_ref, latent, store)


def moved_kernel(rank_ref, lengths_ref, destination_ref, rows_ref, prefix_ref, span_ref, uv_ref, out_ref):
    heads, latent, value = uv_ref.shape
    here, _, width = rows_ref.shape
    span_rows = span_ref.shape[1]
    for j in range(here):
        at = slice(j * span_rows, (j + 1) * span_rows)

        def store(h, part):
            out_ref[at, h * value : (h + 1) * value] = part

        ranks = destination_ref.shape[1]
        requests = lengths_ref.shape[0] // ranks
        source = jnp.int32(0)
        for s in range(ranks):
            source = jnp.where(destination_ref[j, s] == rank_ref[0], jnp.int32(s), source)
        length = lengths_ref[source * requests + requests - here + j]
        prefix = prefix_ref[:, j].reshape(-1, width)
        attend_one(rows_ref[j], length, prefix, NT, span_ref[j], uv_ref, latent, store)


def attend_call(kernel, operands, specs, shapes):
    flops = 2 * 2 * 128 * (288 * (576 + 512) + 512 * 128)
    outs = [jax.ShapeDtypeStruct(shape, bf16) for shape in shapes]
    return pl.pallas_call(
        kernel,
        out_shape=outs,
        in_specs=[pl.BlockSpec(memory_space=pltpu.SMEM)] * 3 + specs,
        out_specs=[whole(shape) for shape in shapes],
        grid=(1,),
        compiler_params=params(),
        cost_estimate=cost(flops, 2 << 20),
    )(*operands)


def whole(shape, block=0):
    return pl.BlockSpec(tuple(shape), lambda i: (block,) + (0,) * (len(shape) - 1))


def share_kernel(values_ref, *refs):
    weight_refs, out_ref = refs[:-1], refs[-1]
    half = weight_refs[0].shape[1]
    each = out_ref.shape[1] // half
    for n, weight_ref in enumerate(weight_refs):
        product = lax.dot_general(
            weight_ref[0], values_ref[...], NT, preferred_element_type=f32
        ).astype(bf16)
        out_ref[n // each, (n % each) * half : (n % each + 1) * half] = product


def project(values, weights, layers):
    rows, depth = values.shape
    blocks, half, _ = weights.shape
    each = blocks // layers
    flight = 4
    weight_specs = [
        pl.BlockSpec((1, half, depth), lambda i, n=n: (flight * i + n, 0, 0)) for n in range(flight)
    ]
    return pl.pallas_call(
        share_kernel,
        out_shape=jax.ShapeDtypeStruct((layers, each * half, rows), bf16),
        grid=(blocks // flight,),
        in_specs=[pl.BlockSpec((rows, depth), lambda i: (0, 0))] + weight_specs,
        out_specs=pl.BlockSpec((flight // each, each * half, rows), lambda i: (i, 0, 0)),
        compiler_params=params(),
        cost_estimate=cost(
            2 * rows * depth * blocks * half,
            2 * (rows * depth + blocks * half * depth + blocks * half * rows),
        ),
    )(values, *([weights] * flight))


def hidden_kernel(width, core_ref, *refs):
    rows_refs, (gate_ref, up_ref, kept_ref, sent_ref, total, squares) = refs[:-6], refs[-6:]
    step = pl.program_id(0)
    weight = jnp.concatenate([gate_ref[...], up_ref[...]], axis=0)
    depth = rows_refs[0].shape[0]
    product, square = 0.0, 0.0
    for n, rows_ref in enumerate(rows_refs):
        block = rows_ref[...]
        piece = weight[:, n * depth : (n + 1) * depth]
        product += jnp.dot(piece, block, preferred_element_type=f32)
        widened = block.astype(f32)
        square += jnp.sum(widened * widened, axis=0, keepdims=True)

    @pl.when(step == 0)
    def _():
        total[...] = product
        squares[...] = square

    @pl.when(step > 0)
    def _():
        total[...] += product
        squares[...] += square

    @pl.when(step == pl.num_programs(0) - 1)
    def _():
        factor = lax.rsqrt(squares[...] / width + norm_eps)
        half, ff = kept_ref.shape
        gate = total[:ff] * factor
        up = total[ff:] * factor
        hidden = (gate / (1.0 + jnp.exp(-gate)) * up).T
        first = core_ref[0] == 0
        kept_ref[...] = jnp.where(first, hidden[:half], hidden[half:]).astype(bf16)
        sent_ref[...] = jnp.where(first, hidden[half:], hidden[:half]).astype(bf16)


def hidden_of(core, rows_in, weight_in):
    width, slots = rows_in.shape
    ff = weight_in.shape[0] // 2
    steps, flight = 4, 2
    depth = width // steps // flight
    rows_specs = [
        pl.BlockSpec((depth, slots), lambda i, n=n: (flight * i + n, 0)) for n in range(flight)
    ]
    return pl.pallas_call(
        functools.partial(hidden_kernel, float(width)),
        out_shape=[jax.ShapeDtypeStruct((slots // 2, ff), bf16)] * 2,
        grid=(steps,),
        in_specs=[
            pl.BlockSpec(memory_space=pltpu.SMEM),
            *rows_specs,
            pl.BlockSpec((ff, width // steps), lambda i: (0, i)),
            pl.BlockSpec((ff, width // steps), lambda i: (1, i)),
        ],
        out_specs=[pl.BlockSpec((slots // 2, ff), lambda i: (0, 0))] * 2,
        scratch_shapes=[pltpu.VMEM((2 * ff, slots), f32), pltpu.VMEM((1, slots), f32)],
        compiler_params=params(),
        cost_estimate=cost(4 * width * slots * ff, 2 * width * (slots + 2 * ff)),
    )(core, *([rows_in] * flight), weight_in, weight_in)


def dispatch_kernel(capacity, top_k, shares_ref, packed_ref, mixed_ref, out_ref):
    col = mixed_ref.shape[0]
    total = packed_ref[:col].astype(f32)
    total += jnp.sum(shares_ref[...].astype(f32), axis=0)
    mixed = total.astype(bf16)
    mixed_ref[...] = mixed
    notes = packed_ref[col:].astype(f32)
    slot = lax.broadcasted_iota(jnp.int32, (out_ref.shape[0], mixed.shape[1]), 0)
    hit = None
    for k in range(top_k):
        named = notes[k : k + 1] * capacity + notes[top_k + k : top_k + k + 1]
        same = slot == named.astype(jnp.int32)
        hit = same if hit is None else hit | same
    placer = jnp.where(hit, 1.0, 0.0).astype(bf16)
    out_ref[...] = lax.dot_general(placer, mixed, NT, preferred_element_type=f32).astype(bf16)


def dispatch(shares, packed, capacity, top_k, slots):
    col, rows = shares.shape[1:]
    return pl.pallas_call(
        functools.partial(dispatch_kernel, capacity, top_k),
        out_shape=[
            jax.ShapeDtypeStruct((col, rows), bf16),
            jax.ShapeDtypeStruct((slots, col), bf16),
        ],
        grid=(1,),
        in_specs=[whole(shares.shape), whole(packed.shape)],
        out_specs=[whole((col, rows)), whole((slots, col))],
        compiler_params=params(),
        cost_estimate=cost(2 * slots * col * rows, 2 * (9 * col * rows + slots * col)),
    )(shares, packed)


def slices_kernel(layer_ref, in_ref, *refs):
    count = len(refs) - 3
    outs, (held, in_sems, out_sems) = refs[:count], refs[count:]
    width = outs[0].shape[1]
    loads, stores = [], []
    for hops, out_ref in enumerate(outs):
        at = pl.multiple_of(lax.rem(layer_ref[0] + hops, count) * width, 128)
        loads.append(
            pltpu.make_async_copy(in_ref.at[:, pl.ds(at, width)], held.at[hops], in_sems.at[hops])
        )
        stores.append(pltpu.make_async_copy(held.at[hops], out_ref, out_sems.at[hops]))
    for load in loads:
        load.start()
    for load, store in zip(loads, stores):
        load.wait()
        store.start()
    for store in stores:
        store.wait()


def slices_of(layer, array, count):
    rows, columns = array.shape
    width = columns // count
    return pl.pallas_call(
        slices_kernel,
        out_shape=[jax.ShapeDtypeStruct((rows, width), array.dtype)] * count,
        in_specs=[
            pl.BlockSpec(memory_space=pltpu.SMEM),
            pl.BlockSpec(memory_space=pl.ANY),
        ],
        out_specs=[pl.BlockSpec(memory_space=pl.ANY)] * count,
        scratch_shapes=[
            pltpu.VMEM((count, rows, width), array.dtype),
            pltpu.SemaphoreType.DMA((count,)),
            pltpu.SemaphoreType.DMA((count,)),
        ],
        compiler_params=params(),
        cost_estimate=cost(0, 4 * rows * columns),
    )(layer, array)


def down_kernel(hidden_ref, *refs):
    weight_refs, (out_ref, total) = refs[:-2], refs[-2:]
    step = pl.program_id(0)
    weight = jnp.concatenate([ref[0, 0] for ref in weight_refs], axis=0)
    product = jnp.dot(hidden_ref[...], weight, preferred_element_type=f32)

    @pl.when(step == 0)
    def _():
        total[...] = product

    @pl.when(step > 0)
    def _():
        total[...] += product

    @pl.when(step == pl.num_programs(0) - 1)
    def _():
        out_ref[...] = total[...].astype(bf16)


def down_project(hidden, weights):
    rows = hidden.shape[0]
    hops, _, ff, cols = weights.shape
    steps = 4
    each = hops // steps
    return pl.pallas_call(
        down_kernel,
        out_shape=jax.ShapeDtypeStruct((rows, cols), bf16),
        grid=(steps,),
        in_specs=[
            pl.BlockSpec((rows, each * 2 * ff), lambda i: (0, i)),
            *[
                pl.BlockSpec((1, 1, ff, cols), lambda i, n=n: (each * i + n // 2, n % 2, 0, 0))
                for n in range(2 * each)
            ],
        ],
        out_specs=pl.BlockSpec((rows, cols), lambda i: (0, 0)),
        scratch_shapes=[pltpu.VMEM((rows, cols), f32)],
        compiler_params=params(),
        cost_estimate=cost(2 * rows * cols * hidden.shape[1], 5 << 20),
    )(hidden, *([weights] * (2 * each)))


def combine_kernel(group, core_ref, combiner_ref, rows_ref, mixed_ref, kept_ref, sent_ref):
    total = jnp.dot(combiner_ref[...], rows_ref[...], preferred_element_type=f32)
    first = core_ref[0] == 0
    half = mixed_ref.shape[0] // 2
    pieces = []
    for j in range(2):
        piece = mixed_ref[j * half : (j + 1) * half].astype(f32)
        nothing = jnp.zeros_like(piece)
        pieces += [jnp.where(first, piece, nothing), jnp.where(first, nothing, piece)]
    total += jnp.concatenate(pieces, axis=0).T
    total = total.reshape(-1, 2, group, total.shape[1])
    low, high = total[:, 0].reshape(kept_ref.shape), total[:, 1].reshape(kept_ref.shape)
    kept_ref[...] = jnp.where(first, low, high)
    sent_ref[...] = jnp.where(first, high, low).astype(bf16)


def combine(core, combiner, rows, mixed, group):
    shape = (combiner.shape[0] // 2, rows.shape[1])
    return pl.pallas_call(
        functools.partial(combine_kernel, group),
        out_shape=[jax.ShapeDtypeStruct(shape, f32), jax.ShapeDtypeStruct(shape, bf16)],
        grid=(1,),
        in_specs=[pl.BlockSpec(memory_space=pltpu.SMEM)]
        + [whole(o.shape) for o in (combiner, rows, mixed)],
        out_specs=[whole(shape)] * 2,
        compiler_params=params(),
        cost_estimate=cost(4 * shape[0] * shape[1] * rows.shape[0], 1 << 20),
    )(core, combiner, rows, mixed)


def places_of(route_rows, experts):
    flat_routes = route_rows.reshape(-1)
    hits = (flat_routes[:, None] == jnp.arange(experts, dtype=jnp.int32)[None, :]).astype(jnp.int32)
    earlier = jnp.cumsum(hits, axis=0) - hits
    return jnp.sum(earlier * hits, axis=1).reshape(route_rows.shape)


def per_device(
    queries,
    cache,
    span_latent,
    prefix_len,
    destination,
    uv_weight,
    out_weight,
    residual,
    norm_gain,
    routes,
    route_weight,
    gate_weight,
    up_weight,
    down_weight,
):
    requests, prefix_rows, cached_width = cache.shape
    tok_rows = queries.shape[0]
    model_width = residual.shape[1]
    top_k = routes.shape[1]
    ff = gate_weight.shape[2]
    nz = lax.axis_size("ep")
    rank_count = lax.axis_size(DP)
    members = lax.axis_size(MEM)
    my_rank = lax.axis_index(DP)
    member = lax.axis_index(MEM)
    layer = lax.axis_index("ep")
    core = lax.axis_index("tp")
    core_at = jnp.reshape(core, (1,))
    col = model_width // members
    capacity = max(2, 3 * tok_rows * top_k // (2 * rank_count))

    def other_core(array):
        return lax.ppermute(array, "tp", [(0, 1), (1, 0)])

    def along(array, hops):
        return lax.ppermute(array, "ep", [(z, (z + hops) % nz) for z in range(nz)])

    ranks = jnp.arange(rank_count, dtype=jnp.int32)
    source_first = jnp.sum(ranks * (destination[0] == my_rank).astype(jnp.int32))
    source_second = jnp.sum(ranks * (destination[1] == my_rank).astype(jnp.int32))
    part = prefix_rows // members
    moving = lax.dynamic_slice_in_dim(cache[requests - 2 :], member * part, part, 1)
    arrived = lax.all_to_all(
        jnp.broadcast_to(moving[None], (rank_count,) + moving.shape), DP, 0, 0, tiled=True
    )
    turned_out = out_weight.T.reshape(2, col // 2, -1)
    out_mine = lax.dynamic_index_in_dim(turned_out, core, 0, keepdims=False)
    out_other = other_core(lax.dynamic_index_in_dim(turned_out, 1 - core, 0, keepdims=False))
    out_cols = lax.all_gather(jnp.concatenate([out_mine, out_other], axis=1), DP, axis=0)
    slices = slices_of(jnp.reshape(layer, (1,)), down_weight[0], nz)
    middle = nz // 2
    half_ff = ff // 2

    down = {0: slices[0], 1: along(slices[1], 1), nz - 1: along(slices[nz - 1], -1)}
    arrived, down = lax.optimization_barrier((arrived, down))
    chosen = jnp.stack(
        [
            lax.dynamic_index_in_dim(arrived[:, 0], source_first, 0, keepdims=False),
            lax.dynamic_index_in_dim(arrived[:, 1], source_second, 0, keepdims=False),
        ]
    )
    moved = lax.all_gather(chosen, MEM, axis=0)

    window, held = lax.optimization_barrier(
        ((slices[3], slices[nz - 3], slices[middle]), (cache, routes, norm_gain, moved))
    )
    cache, routes, norm_gain, moved = held
    window = (
        along(window[0], 3),
        along(window[1], -3),
        along(window[2][:half_ff], middle),
        along(window[2][half_ff:], -middle),
    )

    heads, latent = queries.shape[1], uv_weight.shape[1]
    value = uv_weight.shape[2]
    here = requests - 2
    span_rows = span_latent.shape[1]
    values_shape = (2 * span_rows, heads * value)
    turned = (queries.transpose(1, 2, 0), cache.transpose(0, 2, 1))
    spans = (2, span_rows, cached_width)
    scalars = (jnp.reshape(my_rank, (1,)).astype(jnp.int32), prefix_len, destination)
    values_own, query_rows = attend_call(
        own_kernel,
        (*scalars, *turned, span_latent, uv_weight),
        [
            whole(turned[0].shape),
            whole((here, cached_width, prefix_rows)),
            whole(spans),
            whole(uv_weight.shape),
        ],
        [values_shape, (2, heads * span_rows, cached_width)],
    )

    (values_moved,) = attend_call(
        moved_kernel,
        (*scalars, query_rows, moved, span_latent, uv_weight),
        [whole(query_rows.shape), whole(moved.shape), whole(spans, 1), whole(uv_weight.shape)],
        [values_shape],
    )
    values = jnp.concatenate([values_own, values_moved], axis=0)

    places = places_of(routes, rank_count)
    residual_t = lax.dynamic_slice_in_dim(residual, layer * 2 * col, 2 * col, 1).T
    residual_t = residual_t.reshape(2, 2, col // 2, tok_rows)
    residual_t = lax.dynamic_index_in_dim(residual_t, core, 1, keepdims=False)
    packed = jnp.concatenate(
        [
            residual_t.reshape(col, tok_rows),
            routes.T.astype(bf16),
            places.T.astype(bf16),
            jnp.zeros((16 - 2 * top_k, tok_rows), bf16),
        ],
        axis=0,
    )
    halves = jnp.arange(capacity // 2, dtype=jnp.int32) + core * (capacity // 2)
    slot_index = jnp.arange(rank_count, dtype=jnp.int32)[:, None] * capacity + halves[None, :]
    slots = (routes * capacity + places).T
    matches = slots[:, :, None] == slot_index.reshape(-1)[None, None, :]
    combiner = jnp.sum(
        jnp.where(matches, route_weight.T[:, :, None], jnp.zeros((), route_weight.dtype)), axis=0
    )
    gain = norm_gain.astype(f32)[:, None]
    weight_in = jnp.concatenate([gate_weight[0], up_weight[0]], axis=1)
    weight_in = (weight_in.astype(f32) * gain).astype(bf16)
    weight_in = weight_in.reshape(nz, 2, 2, col // 2, 2 * ff).transpose(0, 2, 1, 3, 4)
    weight_in = weight_in.reshape(model_width, 2 * ff).T

    values = jnp.concatenate([values, other_core(values)], axis=1)
    out_cols, window, packed, combiner, weight_in = lax.optimization_barrier(
        (out_cols, window, packed, combiner, weight_in)
    )
    down[3], down[nz - 3] = window[:2]
    down[middle] = jnp.concatenate(window[2:], axis=0)
    shares = project(values, out_cols, nz)
    shares = lax.all_to_all(shares, "ep", 0, 0, tiled=True)
    shares, down = lax.optimization_barrier((shares, down))

    window, _ = lax.optimization_barrier(((slices[2], slices[nz - 2]), shares))
    window = (along(window[0], 2), along(window[1], -2))
    mixed, outgoing = dispatch(shares, packed, capacity, top_k, rank_count * capacity)
    outgoing = outgoing.reshape(rank_count, capacity, col)
    received = lax.all_to_all(outgoing, DP, 0, 0, tiled=True)
    received, window = lax.optimization_barrier((received, window))
    down[2], down[nz - 2] = window
    received = received.reshape(rank_count, 2, capacity // 2, col).transpose(3, 1, 0, 2)
    received = received.reshape(col, rank_count * capacity)
    down, _ = lax.optimization_barrier((down, received))
    down_mine = jnp.stack([down[h] for h in range(nz)])
    down_all = jnp.stack([down_mine, other_core(down_mine)], axis=1)
    rows_in = lax.all_gather(received, MEM, axis=0)
    rows_in, down_all = lax.optimization_barrier((rows_in, down_all))
    hidden, sent = hidden_of(core_at, rows_in.reshape(model_width, -1), weight_in)

    hidden = jnp.concatenate([hidden, other_core(sent)], axis=1)
    half = hidden.shape[0] // 2
    blocks = {0: hidden}
    up_way, down_way = hidden, hidden
    for hops in range(1, middle):
        up_way, down_way = along(up_way, 1), along(down_way, -1)
        blocks[hops], blocks[nz - hops] = up_way, down_way
    blocks[middle] = jnp.concatenate([along(up_way[:half], 1), along(down_way[half:], -1)], axis=0)
    hidden_all = jnp.concatenate([blocks[h] for h in range(nz)], axis=1)
    expert_out = down_project(hidden_all, down_all)
    expert_out = expert_out.reshape(rank_count, capacity // 2, 2 * col)

    returned = lax.all_to_all(expert_out, DP, 0, 0, tiled=True)
    returned = returned.reshape(rank_count * capacity // 2, 2 * col)
    group = tok_rows // members
    kept, sent = combine(core_at, combiner, returned, mixed, group)
    total = (kept + other_core(sent).astype(f32)).astype(bf16)
    total = lax.all_to_all(total.reshape(nz, group, 2 * col), "ep", 0, 0, tiled=True)
    return total.transpose(1, 0, 2).reshape(group, model_width)


def solution(mesh):
    in_specs = (
        P(DP, MEM, None),
        P(DP, None, None),
        P(DP, None, None),
        P(),
        P(),
        P(MEM, None, None),
        P(MEM, DP),
        P(DP, None),
        P(),
        P(DP, None),
        P(DP, None),
        P(DP, None, MEM),
        P(DP, None, MEM),
        P(DP, MEM, None),
    )
    out_specs = P(DP + MEM, None)
    return jax.shard_map(
        per_device, mesh=mesh, in_specs=in_specs, out_specs=out_specs, check_vma=False
    )
```

time: 296 us -> 276 us (0.932)
  waiting for transfers between devices: 108 us -> 90.8 us
  blocking collectives: 51.1 us -> 36.4 us
  local copies, waits for them, and re-layouts: 9.07 us -> 23.7 us
    all_gather x1 -> x0, blocking collectives: 11.5 us -> none  [per_device(): values_x = lax.all_gather(values, 'dx', axis=0)]
    all_gather x1, waiting for transfers between devices: 46.4 us -> 36.8 us  [per_device(): rows_in = lax.all_gather(received, MEM, axis=0)]
    unnamed x46 -> x61, local copies, waits for them, and re-layouts: 0.63 us -> 6.28 us
    reshape x6 -> x3, local copies, waits for them, and re-layouts: 3.04 us -> 8.55 us  [the longest x1 5.92 us: per_device(): weight_in = weight_in.reshape(model_width, 2 * ff).T]
    all_to_all x1, waiting for transfers between devices: 5.34 us -> 0.01 us  [per_device(): received = lax.all_to_all(outgoing, DP, 0, 0, tiled=True)]
    ppermute x16, waiting for transfers between devices: 22.1 us -> 16.9 us  [along(): return lax.ppermute(array, 'ep', [(z, (z + hops) % nz) for z in range(nz)])]
    ppermute x2 -> x5, starting transfers between devices: 7.27 us -> 11.9 us  [other_core(): return lax.ppermute(array, 'tp', [(0, 1), (1, 0)])]
    ppermute x2 -> x5, waiting for transfers between devices: 1.56 us -> 6.07 us  [other_core(): return lax.ppermute(array, 'tp', [(0, 1), (1, 0)])]
  transfers between devices with their start and end apart: 26 -> 27, of which waited for: 13 -> 14; matrix products, arithmetic and copies ran while one was open for 4% -> 9% of each run, Pallas kernels for 6% -> 4%
where the time goes in v5:
time: 276 us; the launch traced here: 275 us
  waiting for transfers between devices  90.8 us (33%)
  starting transfers between devices  64.8 us (23%)
  blocking collectives  36.4 us (13%)
  Pallas kernels  31.7 us (11%)
  local copies, waits for them, and re-layouts  23.7 us (9%)
  between operations  17.7 us (6%)
  other arithmetic  10.2 us (4%)
    all_gather x1, waiting for transfers between devices, per_device(): rows_in = lax.all_gather(received, MEM, axis=0)  36.8 us
    ppermute x16, starting transfers between devices, along(): return lax.ppermute(array, 'ep', [(z, (z + hops) % nz) for z in range(nz)])  30.1 us
    all_gather x1, blocking collectives, per_device(): moved = lax.all_gather(chosen, MEM, axis=0)  24.5 us
    all_to_all x1, waiting for transfers between devices, per_device(): shares = lax.all_to_all(shares, 'ep', 0, 0, tiled=True)  23.2 us
    ppermute x16, waiting for transfers between devices, along(): return lax.ppermute(array, 'ep', [(z, (z + hops) % nz) for z in range(nz)])  16.9 us
    all_to_all x1, blocking collectives, per_device(): lax.all_to_all(total.reshape(nz, group, 2 * col), 'ep', 0, 0, tiled=True)  11.9 us
    ppermute x5, starting transfers between devices, other_core(): return lax.ppermute(array, 'tp', [(0, 1), (1, 0)])  11.9 us
    all_to_all x1, waiting for transfers between devices, per_device(): returned = lax.all_to_all(expert_out, DP, 0, 0, tiled=True)  7.86 us
  transfers between devices with their start and end apart: 27, of which 14 were waited for; matrix products, arithmetic and copies ran while one was open for 9% of the time, Pallas kernels for 4%

profile of v5, /device:TPU:1, one launch (start us, length us, event | category | flops | bytes accessed | tf_op | source)
XLA Modules:
  0.0 275.3 jit_solution(14281878029059397066)
XLA Ops:
  7.8 3.3 %collective-permute-start = (bf16[224,512]{1,0:T(8,128)(2,1)S(1)}, bf16[224,512]{1,0:T(8,128)(2,1)S(1)}, u32[]{:S(2)}, u32[]{:S(2)}) collective-permute-start(bf16[224,512]{1,0:T(8,128)(2,1)S(1)} %get-tuple-element.124), channel_id=1, source_target_pairs={{0,1},{1,0},{2,3},{3,2},{4,5},{5,4},{6,7},{7,6},{8,9},{9,8},{10,11... | collective-permute-start | bytes 688136 | tf_op jit(solution)/shard_map/ppermute | solution.py:394
  14.4 5.0 %all-to-all-start = ((bf16[16,2,16,576]{3,2,1,0:T(8,128)(2,1)}), bf16[16,2,16,576]{3,2,1,0:T(8,128)(2,1)S(1)}, u32[]{:S(2)}, u32[]{:S(2)}) async-start(bf16[16,2,16,576]{3,2,1,0:T(8,128)(2,1)} %broadcast_in_dim.12), calls=%async_computation | async-start | bytes 1310720 | tf_op jit(solution)/shard_map/all_to_all | solution.py:404
  23.7 4.0 %collective-permute-start.2 = (bf16[128,896]{1,0:T(8,128)(2,1)}, bf16[128,896]{1,0:T(8,128)(2,1)S(1)}, u32[]{:S(2)}, u32[]{:S(2)}) collective-permute-start(bf16[128,896]{1,0:T(8,128)(2,1)} %get-tuple-element.67), channel_id=1, source_target_pairs={{0,14},{2,0},{4,2},{6,4},{8,6},{10,8},{12,10},{14,12},{1,15},{3,1}... | collective-permute-start | bytes 688136 | tf_op jit(solution)/shard_map/ppermute | solution.py:397
  33.5 24.5 %all-gather.1 = bf16[32,16,576]{2,1,0:T(8,128)(2,1)} all-gather(bf16[2,16,576]{2,1,0:T(8,128)(2,1)S(1)} %pad_maximum_fusion.5), channel_id=3, replica_groups=mesh['dp'=16,'ep'=8,'tp'=2] {'ep','tp'}, dimensions={0}, use_global_device_ids=true | all-gather | bytes 626688 | tf_op jit(solution)/shard_map/all_gather | solution.py:423
  61.3 4.4 %collective-permute-start.6 = (bf16[64,896]{1,0:T(8,128)(2,1)}, bf16[64,896]{1,0:T(8,128)(2,1)S(1)}, u32[]{:S(2)}, u32[]{:S(2)}) collective-permute-start(bf16[64,896]{1,0:T(8,128)(2,1)} %get-tuple-element.125), channel_id=1, source_target_pairs={{0,8},{2,10},{4,12},{6,14},{8,0},{10,2},{12,4},{14,6},{1,9},{3,11}... | collective-permute-start | bytes 344072 | tf_op jit(solution)/shard_map/ppermute | solution.py:397
  65.7 4.5 %collective-permute-start.4 = (bf16[128,896]{1,0:T(8,128)(2,1)}, bf16[128,896]{1,0:T(8,128)(2,1)S(1)}, u32[]{:S(2)}, u32[]{:S(2)}) collective-permute-start(bf16[128,896]{1,0:T(8,128)(2,1)} %get-tuple-element.70), channel_id=1, source_target_pairs={{0,10},{2,12},{4,14},{6,0},{8,2},{10,4},{12,6},{14,8},{1,11},{3,13... | collective-permute-start | bytes 688136 | tf_op jit(solution)/shard_map/ppermute | solution.py:397
  70.2 3.9 %shard_map.137 = (bf16[64,512]{1,0:T(8,128)(2,1)}, bf16[2,128,576]{2,1,0:T(8,128)(2,1)}) custom-call(s32[1]{0:T(128)} %bitcast.27.rank_ref, s32[64]{0:T(128)} %lengths_ref.3, s32[2,16]{1,0:T(2,128)} %destination_ref.3, bf16[4,576,128]{2,1,0:T(8,128)(2,1)} %bitcast.112, bf16[4,576,256]{2,1,0:T(8,128)(2,1)} %bitcast.104, bf16[4,32,576]{2,1,0:T(8,128)(2,1)} %span_ref.3, ...), custom_call_target="tpu_custom_call" | custom-call | flops 193986560 | bytes 2097152 | tf_op jit(solution)/shard_map/pallas_call | solution.py:100
  74.1 3.6 %shard_map.138 = bf16[64,512]{1,0:T(8,128)(2,1)} custom-call(s32[1]{0:T(128)} %bitcast.27.rank_ref, s32[64]{0:T(128)} %lengths_ref.3, s32[2,16]{1,0:T(2,128)} %destination_ref.3, bf16[2,128,576]{2,1,0:T(8,128)(2,1)} %get-tuple-element.77.rows_ref, bf16[16,2,16,576]{3,2,1,0:T(8,128)(2,1)} %bitcast.105, bf16[4,32,576]{2,1,0:T(8,128)(2,1)} %span_ref.3, ...), custom_call_target="tpu_custom_call" | custom-call | flops 193986560 | bytes 2097152 | tf_op jit(solution)/shard_map/pallas_call | solution.py:100
  84.1 5.9 %copy.90 = bf16[7168,256]{0,1:T(8,128)(2,1)} copy(bf16[7168,256]{1,0:T(8,128)(2,1)} %bitcast.103) | data formatting | bytes 7340032 | tf_op jit(solution)/shard_map/reshape | solution.py:488
  91.0 6.2 %shard_map.139 = bf16[8,448,128]{2,1,0:T(8,128)(2,1)} custom-call(bf16[128,1024]{1,0:T(8,128)(2,1)} %pad_maximum_fusion.2.values_ref, bf16[16,224,1024]{2,1,0:T(8,128)(2,1)} %bitcast.95, bf16[16,224,1024]{2,1,0:T(8,128)(2,1)} %bitcast.96, bf16[16,224,1024]{2,1,0:T(8,128)(2,1)} %bitcast.97, bf16[16,224,1024]{2,1,0:T(8,128)(2,1)} %bitcast.98), custom_call_target="tpu_custom_call" | custom-call | flops 939524096 | bytes 8519680 | tf_op jit(solution)/shard_map/pallas_call | solution.py:134
  97.2 3.6 %all-to-all-start.1 = ((bf16[8,448,128]{2,1,0:T(8,128)(2,1)}), bf16[8,448,128]{2,1,0:T(8,128)(2,1)S(1)}, u32[]{:S(2)}, u32[]{:S(2)}) async-start(bf16[8,448,128]{2,1,0:T(8,128)(2,1)} %shard_map.139), calls=%async_computation.1 | async-start | bytes 1835008 | tf_op jit(solution)/shard_map/all_to_all | solution.py:497
  101.7 23.2 %all-to-all-done.1.shares_ref = bf16[8,448,128]{2,1,0:T(8,128)(2,1)S(1)} async-done(((bf16[8,448,128]{2,1,0:T(8,128)(2,1)}), bf16[8,448,128]{2,1,0:T(8,128)(2,1)S(1)}, u32[]{:S(2)}, u32[]{:S(2)}) %all-to-all-start.1) | async-done | bytes 917536 | tf_op jit(solution)/shard_map/all_to_all | solution.py:497
  128.1 7.5 %all-to-all-start.2 = ((bf16[16,24,448]{2,1,0:T(8,128)(2,1)}), bf16[16,24,448]{2,1,0:T(8,128)(2,1)S(1)}, u32[]{:S(2)}, u32[]{:S(2)}) async-start(bf16[16,24,448]{2,1,0:T(8,128)(2,1)} %bitcast.117), calls=%async_computation.2 | async-start | bytes 786432 | tf_op jit(solution)/shard_map/all_to_all | solution.py:504
  136.0 3.6 %collective-permute-start.9 = (bf16[128,896]{1,0:T(8,128)(2,1)}, bf16[128,896]{1,0:T(8,128)(2,1)S(1)}, u32[]{:S(2)}, u32[]{:S(2)}) collective-permute-start(bf16[128,896]{1,0:T(8,128)(2,1)} %get-tuple-element.93), channel_id=1, source_target_pairs={{0,12},{2,14},{4,0},{6,2},{8,4},{10,6},{12,8},{14,10},{1,13},{3,15... | collective-permute-start | bytes 688136 | tf_op jit(solution)/shard_map/ppermute | solution.py:397
  139.6 7.7 %collective-permute-done.8 = bf16[128,896]{1,0:T(8,128)(2,1)S(1)} collective-permute-done((bf16[128,896]{1,0:T(8,128)(2,1)}, bf16[128,896]{1,0:T(8,128)(2,1)S(1)}, u32[]{:S(2)}, u32[]{:S(2)}) %collective-permute-start.8) | collective-permute-done | bytes 229408 | tf_op jit(solution)/shard_map/ppermute | solution.py:397
  153.1 3.4 %collective-permute-done.10 = bf16[8,128,896]{2,1,0:T(8,128)(2,1)S(1)} collective-permute-done((bf16[8,128,896]{2,1,0:T(8,128)(2,1)S(1)}, bf16[8,128,896]{2,1,0:T(8,128)(2,1)S(1)}, u32[]{:S(2)}, u32[]{:S(2)}) %collective-permute-start.10) | collective-permute-done | bytes 1835040 | tf_op jit(solution)/shard_map/ppermute | solution.py:394
  158.7 36.8 %all-gather.5.cloned.1.call-done = bf16[16,448,384]{2,1,0:T(8,128)(2,1)} async-done(((bf16[1,448,384]{2,1,0:T(8,128)(2,1)}), bf16[16,448,384]{2,1,0:T(8,128)(2,1)}) %all-gather.5.cloned.1.call-update) | async-done | bytes 5505040 | tf_op jit(solution)/shard_map/all_gather | solution.py:512
  195.5 6.3 %shard_map.141 = (bf16[192,128]{1,0:T(8,128)(2,1)}, bf16[192,128]{1,0:T(8,128)(2,1)}) custom-call(s32[1]{0:T(128)} %bitcast.core_ref, bf16[7168,384]{1,0:T(8,128)(2,1)} %bitcast.101, bf16[7168,384]{1,0:T(8,128)(2,1)} %bitcast.102, bf16[256,7168]{1,0:T(8,128)(2,1)} %bitcast.99, bf16[256,7168]{1,0:T(8,128)(2,1)} %bitcast.100), custom_call_target="tpu_custom_call" | custom-call | flops 1409286144 | bytes 9175040 | tf_op jit(solution)/shard_map/pallas_call | solution.py:191
  218.1 2.7 collective-permute-start.19
  223.2 4.8 %shard_map.142 = bf16[192,896]{1,0:T(8,128)(2,1)} custom-call(bf16[192,2048]{1,0:T(8,128)(2,1)} %copy-done.4, bf16[8,2,128,896]{3,2,1,0:T(8,128)(2,1)} %pad_maximum_fusion.refs_0_.refs_1_.refs_2_.refs_3_, bf16[8,2,128,896]{3,2,1,0:T(8,128)(2,1)} %pad_maximum_fusion.refs_0_.refs_1_.refs_2_.refs_3_, ...), custom_call_target="tpu_custom_call" | custom-call | flops 704643072 | bytes 5242880 | tf_op jit(solution)/shard_map/pallas_call | solution.py:306
  229.9 6.5 %all-to-all-start.3 = ((bf16[16,12,896]{2,1,0:T(8,128)(2,1)}), bf16[16,12,896]{2,1,0:T(8,128)(2,1)S(1)}, u32[]{:S(2)}, u32[]{:S(2)}) async-start(bf16[16,12,896]{2,1,0:T(8,128)(2,1)} %reshape.120), calls=%async_computation.3 | async-start | bytes 917504 | tf_op jit(solution)/shard_map/all_to_all | solution.py:528
  237.2 7.9 %all-to-all-done.3 = bf16[16,12,896]{2,1,0:T(8,128)(2,1)S(1)} async-done(((bf16[16,12,896]{2,1,0:T(8,128)(2,1)}), bf16[16,12,896]{2,1,0:T(8,128)(2,1)S(1)}, u32[]{:S(2)}, u32[]{:S(2)}) %all-to-all-start.3) | async-done | bytes 344096 | tf_op jit(solution)/shard_map/all_to_all | solution.py:528
  247.8 6.0 %collective-permute-start.20 = (bf16[64,896]{1,0:T(8,128)(2,1)}, bf16[64,896]{1,0:T(8,128)(2,1)S(1)}, u32[]{:S(2)}, u32[]{:S(2)}) collective-permute-start(bf16[64,896]{1,0:T(8,128)(2,1)} %get-tuple-element.118), channel_id=1, source_target_pairs={{0,1},{1,0},{2,3},{3,2},{4,5},{5,4},{6,7},{7,6},{8,9},{9,8},{10,11... | collective-permute-start | bytes 344072 | tf_op jit(solution)/shard_map/ppermute | solution.py:394
  255.9 11.9 %all_to_all.25 = bf16[8,8,896]{2,1,0:T(8,128)(2,1)S(1)} all-to-all(bf16[8,8,896]{2,1,0:T(8,128)(2,1)S(1)} %fusion.1), channel_id=1, replica_groups=mesh['dp'=16,'ep'=8,'tp'=2] {'ep'}, dimensions={0} | all-to-all | bytes 229376 | tf_op jit(solution)/shard_map/all_to_all | solution.py:533
  (159 shorter events, 60.4 us)
Async XLA Ops:
  6.5 84.5 %all-gather.7.cloned.1.call-start = ((), (), s32[]{:S(2)}) async-start(), calls=%async_computation.6 | async-start | bytes 7798784 | tf_op jit(solution)/shard_map/all_gather | solution.py:410
  7.8 4.4 %collective-permute-start = (bf16[224,512]{1,0:T(8,128)(2,1)S(1)}, bf16[224,512]{1,0:T(8,128)(2,1)S(1)}, u32[]{:S(2)}, u32[]{:S(2)}) collective-permute-start(bf16[224,512]{1,0:T(8,128)(2,1)S(1)} %get-tuple-element.124), channel_id=1, source_target_pairs={{0,1},{1,0},{2,3},{3,2},{4,5},{5,4},{6,7},{7,6},{8,9},{9,8},{10,11... | collective-permute-start | bytes 688136 | tf_op jit(solution)/shard_map/ppermute | solution.py:394
  14.4 19.0 %all-to-all-start = ((bf16[16,2,16,576]{3,2,1,0:T(8,128)(2,1)}), bf16[16,2,16,576]{3,2,1,0:T(8,128)(2,1)S(1)}, u32[]{:S(2)}, u32[]{:S(2)}) async-start(bf16[16,2,16,576]{3,2,1,0:T(8,128)(2,1)} %broadcast_in_dim.12), calls=%async_computation | async-start | bytes 1310720 | tf_op jit(solution)/shard_map/all_to_all | solution.py:404
  22.0 11.3 %collective-permute-start.1 = (bf16[128,896]{1,0:T(8,128)(2,1)}, bf16[128,896]{1,0:T(8,128)(2,1)S(1)}, u32[]{:S(2)}, u32[]{:S(2)}) collective-permute-start(bf16[128,896]{1,0:T(8,128)(2,1)} %get-tuple-element.66), channel_id=1, source_target_pairs={{0,2},{2,4},{4,6},{6,8},{8,10},{10,12},{12,14},{14,0},{1,3},{3,5},... | collective-permute-start | bytes 688136 | tf_op jit(solution)/shard_map/ppermute | solution.py:397
  23.7 9.6 %collective-permute-start.2 = (bf16[128,896]{1,0:T(8,128)(2,1)}, bf16[128,896]{1,0:T(8,128)(2,1)S(1)}, u32[]{:S(2)}, u32[]{:S(2)}) collective-permute-start(bf16[128,896]{1,0:T(8,128)(2,1)} %get-tuple-element.67), channel_id=1, source_target_pairs={{0,14},{2,0},{4,2},{6,4},{8,6},{10,8},{12,10},{14,12},{1,15},{3,1}... | collective-permute-start | bytes 688136 | tf_op jit(solution)/shard_map/ppermute | solution.py:397
  60.3 30.6 %collective-permute-start.5 = (bf16[64,896]{1,0:T(8,128)(2,1)}, bf16[64,896]{1,0:T(8,128)(2,1)S(1)}, u32[]{:S(2)}, u32[]{:S(2)}) collective-permute-start(bf16[64,896]{1,0:T(8,128)(2,1)} %get-tuple-element.126), channel_id=1, source_target_pairs={{0,8},{2,10},{4,12},{6,14},{8,0},{10,2},{12,4},{14,6},{1,9},{3,11}... | collective-permute-start | bytes 344072 | tf_op jit(solution)/shard_map/ppermute | solution.py:397
  61.3 29.6 %collective-permute-start.6 = (bf16[64,896]{1,0:T(8,128)(2,1)}, bf16[64,896]{1,0:T(8,128)(2,1)S(1)}, u32[]{:S(2)}, u32[]{:S(2)}) collective-permute-start(bf16[64,896]{1,0:T(8,128)(2,1)} %get-tuple-element.125), channel_id=1, source_target_pairs={{0,8},{2,10},{4,12},{6,14},{8,0},{10,2},{12,4},{14,6},{1,9},{3,11}... | collective-permute-start | bytes 344072 | tf_op jit(solution)/shard_map/ppermute | solution.py:397
  65.7 25.2 %collective-permute-start.3 = (bf16[128,896]{1,0:T(8,128)(2,1)}, bf16[128,896]{1,0:T(8,128)(2,1)S(1)}, u32[]{:S(2)}, u32[]{:S(2)}) collective-permute-start(bf16[128,896]{1,0:T(8,128)(2,1)} %get-tuple-element.69), channel_id=1, source_target_pairs={{0,6},{2,8},{4,10},{6,12},{8,14},{10,0},{12,2},{14,4},{1,7},{3,9},... | collective-permute-start | bytes 688136 | tf_op jit(solution)/shard_map/ppermute | solution.py:397
  65.7 25.2 %collective-permute-start.4 = (bf16[128,896]{1,0:T(8,128)(2,1)}, bf16[128,896]{1,0:T(8,128)(2,1)S(1)}, u32[]{:S(2)}, u32[]{:S(2)}) collective-permute-start(bf16[128,896]{1,0:T(8,128)(2,1)} %get-tuple-element.70), channel_id=1, source_target_pairs={{0,10},{2,12},{4,14},{6,0},{8,2},{10,4},{12,6},{14,8},{1,11},{3,13... | collective-permute-start | bytes 688136 | tf_op jit(solution)/shard_map/ppermute | solution.py:397
  78.6 11.5 %collective-permute-start.7 = (bf16[128,512]{1,0:T(8,128)(2,1)S(1)}, bf16[128,512]{1,0:T(8,128)(2,1)S(1)}, u32[]{:S(2)}, u32[]{:S(2)}) collective-permute-start(bf16[128,512]{1,0:T(8,128)(2,1)S(1)} %pad_maximum_fusion.4), channel_id=1, source_target_pairs={{0,1},{1,0},{2,3},{3,2},{4,5},{5,4},{6,7},{7,6},{8,9},{9,8},{10,11... | collective-permute-start | bytes 393224 | tf_op jit(solution)/shard_map/ppermute | solution.py:394
  97.2 27.7 %all-to-all-start.1 = ((bf16[8,448,128]{2,1,0:T(8,128)(2,1)}), bf16[8,448,128]{2,1,0:T(8,128)(2,1)S(1)}, u32[]{:S(2)}, u32[]{:S(2)}) async-start(bf16[8,448,128]{2,1,0:T(8,128)(2,1)} %shard_map.139), calls=%async_computation.1 | async-start | bytes 1835008 | tf_op jit(solution)/shard_map/all_to_all | solution.py:497
  128.1 19.6 %all-to-all-start.2 = ((bf16[16,24,448]{2,1,0:T(8,128)(2,1)}), bf16[16,24,448]{2,1,0:T(8,128)(2,1)S(1)}, u32[]{:S(2)}, u32[]{:S(2)}) async-start(bf16[16,24,448]{2,1,0:T(8,128)(2,1)} %bitcast.117), calls=%async_computation.2 | async-start | bytes 786432 | tf_op jit(solution)/shard_map/all_to_all | solution.py:504
  135.7 59.8 %all-gather.5.cloned.1.call-start = ((), (), s32[]{:S(2)}) async-start(), calls=%async_computation.5 | async-start | bytes 5849088 | tf_op jit(solution)/shard_map/all_gather | solution.py:512
  135.9 11.4 %collective-permute-start.8 = (bf16[128,896]{1,0:T(8,128)(2,1)}, bf16[128,896]{1,0:T(8,128)(2,1)S(1)}, u32[]{:S(2)}, u32[]{:S(2)}) collective-permute-start(bf16[128,896]{1,0:T(8,128)(2,1)} %get-tuple-element.92), channel_id=1, source_target_pairs={{0,4},{2,6},{4,8},{6,10},{8,12},{10,14},{12,0},{14,2},{1,5},{3,7},... | collective-permute-start | bytes 688136 | tf_op jit(solution)/shard_map/ppermute | solution.py:397
  136.0 11.8 %collective-permute-start.9 = (bf16[128,896]{1,0:T(8,128)(2,1)}, bf16[128,896]{1,0:T(8,128)(2,1)S(1)}, u32[]{:S(2)}, u32[]{:S(2)}) collective-permute-start(bf16[128,896]{1,0:T(8,128)(2,1)} %get-tuple-element.93), channel_id=1, source_target_pairs={{0,12},{2,14},{4,0},{6,2},{8,4},{10,6},{12,8},{14,10},{1,13},{3,15... | collective-permute-start | bytes 688136 | tf_op jit(solution)/shard_map/ppermute | solution.py:397
  152.1 4.4 %collective-permute-start.10 = (bf16[8,128,896]{2,1,0:T(8,128)(2,1)S(1)}, bf16[8,128,896]{2,1,0:T(8,128)(2,1)S(1)}, u32[]{:S(2)}, u32[]{:S(2)}) collective-permute-start(bf16[8,128,896]{2,1,0:T(8,128)(2,1)S(1)} %bitcast_dynamic-update-slice_fusion), channel_id=1, source_target_pairs={{0,1},{1,0},{2,3},{3,2},{4,5},{5,4},{6,7},{7,6},{8,9},{9,8},{10,11... | collective-permute-start | bytes 5505032 | tf_op jit(solution)/shard_map/ppermute | solution.py:394
  203.3 5.4 %collective-permute-start.12 = (bf16[192,256]{1,0:T(8,128)(2,1)S(1)}, bf16[192,256]{1,0:T(8,128)(2,1)S(1)}, u32[]{:S(2)}, u32[]{:S(2)}) collective-permute-start(bf16[192,256]{1,0:T(8,128)(2,1)S(1)} %get-tuple-element.127), channel_id=1, source_target_pairs={{0,2},{2,4},{4,6},{6,8},{8,10},{10,12},{12,14},{14,0},{1,3},{3,5},... | collective-permute-start | bytes 294920 | tf_op jit(solution)/shard_map/ppermute | solution.py:397
  204.4 4.3 %collective-permute-start.16 = (bf16[192,256]{1,0:T(8,128)(2,1)S(1)}, bf16[192,256]{1,0:T(8,128)(2,1)S(1)}, u32[]{:S(2)}, u32[]{:S(2)}) collective-permute-start(bf16[192,256]{1,0:T(8,128)(2,1)S(1)} %get-tuple-element.127), channel_id=1, source_target_pairs={{0,14},{2,0},{4,2},{6,4},{8,6},{10,8},{12,10},{14,12},{1,15},{3,1}... | collective-permute-start | bytes 294920 | tf_op jit(solution)/shard_map/ppermute | solution.py:397
  208.7 4.7 %collective-permute-start.13 = (bf16[192,256]{1,0:T(8,128)(2,1)S(1)}, bf16[192,256]{1,0:T(8,128)(2,1)S(1)}, u32[]{:S(2)}, u32[]{:S(2)}) collective-permute-start(bf16[192,256]{1,0:T(8,128)(2,1)S(1)} %collective-permute-done.12), channel_id=1, source_target_pairs={{0,2},{2,4},{4,6},{6,8},{8,10},{10,12},{12,14},{14,0},{1,3},{3,5},... | collective-permute-start | bytes 294920 | tf_op jit(solution)/shard_map/ppermute | solution.py:397
  208.8 4.7 %collective-permute-start.17 = (bf16[192,256]{1,0:T(8,128)(2,1)S(1)}, bf16[192,256]{1,0:T(8,128)(2,1)S(1)}, u32[]{:S(2)}, u32[]{:S(2)}) collective-permute-start(bf16[192,256]{1,0:T(8,128)(2,1)S(1)} %collective-permute-done.16), channel_id=1, source_target_pairs={{0,14},{2,0},{4,2},{6,4},{8,6},{10,8},{12,10},{14,12},{1,15},{3,1}... | collective-permute-start | bytes 294920 | tf_op jit(solution)/shard_map/ppermute | solution.py:397
  213.4 4.7 %collective-permute-start.14 = (bf16[192,256]{1,0:T(8,128)(2,1)S(1)}, bf16[192,256]{1,0:T(8,128)(2,1)S(1)}, u32[]{:S(2)}, u32[]{:S(2)}) collective-permute-start(bf16[192,256]{1,0:T(8,128)(2,1)S(1)} %collective-permute-done.13), channel_id=1, source_target_pairs={{0,2},{2,4},{4,6},{6,8},{8,10},{10,12},{12,14},{14,0},{1,3},{3,5},... | collective-permute-start | bytes 294920 | tf_op jit(solution)/shard_map/ppermute | solution.py:397
  213.4 4.7 %collective-permute-start.18 = (bf16[192,256]{1,0:T(8,128)(2,1)S(1)}, bf16[192,256]{1,0:T(8,128)(2,1)S(1)}, u32[]{:S(2)}, u32[]{:S(2)}) collective-permute-start(bf16[192,256]{1,0:T(8,128)(2,1)S(1)} %collective-permute-done.17), channel_id=1, source_target_pairs={{0,14},{2,0},{4,2},{6,4},{8,6},{10,8},{12,10},{14,12},{1,15},{3,1}... | collective-permute-start | bytes 294920 | tf_op jit(solution)/shard_map/ppermute | solution.py:397
  229.9 15.1 %all-to-all-start.3 = ((bf16[16,12,896]{2,1,0:T(8,128)(2,1)}), bf16[16,12,896]{2,1,0:T(8,128)(2,1)S(1)}, u32[]{:S(2)}, u32[]{:S(2)}) async-start(bf16[16,12,896]{2,1,0:T(8,128)(2,1)} %reshape.120), calls=%async_computation.3 | async-start | bytes 917504 | tf_op jit(solution)/shard_map/all_to_all | solution.py:528
  247.8 7.1 %collective-permute-start.20 = (bf16[64,896]{1,0:T(8,128)(2,1)}, bf16[64,896]{1,0:T(8,128)(2,1)S(1)}, u32[]{:S(2)}, u32[]{:S(2)}) collective-permute-start(bf16[64,896]{1,0:T(8,128)(2,1)} %get-tuple-element.118), channel_id=1, source_target_pairs={{0,1},{1,0},{2,3},{3,2},{4,5},{5,4},{6,7},{7,6},{8,9},{9,8},{10,11... | collective-permute-start | bytes 344072 | tf_op jit(solution)/shard_map/ppermute | solution.py:394
  (27 other events, 283.5 us)
Sparse Core Ops, SparseCore 0:
  13.2 72.6 all-gather.6
  150.0 45.4 all-gather.4

commit v6 on v5

v6 whole, which is shorter than its diff:
```python
import functools

import jax
import jax.numpy as jnp
from jax import lax
from jax.experimental import pallas as pl
from jax.experimental.pallas import tpu as pltpu
from jax.sharding import PartitionSpec as P

score_scale = 192.0 ** (-0.5)
norm_eps = 1e-06
DP = ("dp",)
MEM = ("ep", "tp")
bf16 = jnp.bfloat16
f32 = jnp.float32
VMEM_LIMIT = 56 << 20
NN = (((1,), (0,)), ((), ()))
NT = (((1,), (1,)), ((), ()))


def params():
    return pltpu.CompilerParams(vmem_limit_bytes=VMEM_LIMIT)


def cost(flops, nbytes):
    return pl.CostEstimate(flops=flops, bytes_accessed=nbytes, transcendentals=0)


def attend_one(rows, length, prefix, prefix_dims, span, uv_ref, latent, store, place=None):
    total, span_rows = rows.shape[0], span.shape[0]
    keys_first = prefix_dims is NT
    cached = prefix[:, :latent] if keys_first else prefix[:latent]
    first = lax.dot_general(rows, prefix, prefix_dims, preferred_element_type=f32) * score_scale
    second = lax.dot_general(rows, span, NT, preferred_element_type=f32) * score_scale
    key = lax.broadcasted_iota(jnp.int32, first.shape, 1)
    if place is not None:
        key = place(key)
    first = jnp.where(key < length, first, -jnp.inf)
    token = lax.rem(lax.broadcasted_iota(jnp.int32, second.shape, 0), span_rows)
    late = lax.broadcasted_iota(jnp.int32, second.shape, 1)
    second = jnp.where(late <= token, second, -jnp.inf)
    highest = jnp.maximum(
        jnp.max(first, axis=1, keepdims=True), jnp.max(second, axis=1, keepdims=True)
    )
    first = jnp.exp(first - highest)
    second = jnp.exp(second - highest)
    norm = jnp.sum(first, axis=1, keepdims=True) + jnp.sum(second, axis=1, keepdims=True)
    first = (first / norm).astype(bf16)
    second = (second / norm).astype(bf16)
    out = lax.dot_general(first, cached, NN if keys_first else NT, preferred_element_type=f32)
    out += jnp.dot(second, span[:, :latent], preferred_element_type=f32)
    out = out.astype(bf16)
    for h in range(total // span_rows):
        part = jnp.dot(
            out[h * span_rows : (h + 1) * span_rows], uv_ref[h], preferred_element_type=f32
        )
        store(h, part.astype(bf16))


def own_kernel(rank_ref, lengths_ref, destination_ref, query_ref, prefix_ref, span_ref, uv_ref, out_ref, rows_ref):
    heads, latent, value = uv_ref.shape
    span_rows = span_ref.shape[1]
    here = prefix_ref.shape[0]
    turned = [query_ref[h].T for h in range(heads)]
    for j in range(here + rows_ref.shape[0]):
        at = slice(j * span_rows, (j + 1) * span_rows)
        rows = jnp.concatenate([turned[h][at] for h in range(heads)], axis=0)
        if j >= here:
            rows_ref[j - here] = rows
            continue

        def store(h, part):
            out_ref[at, h * value : (h + 1) * value] = part

        length = lengths_ref[rank_ref[0] * (here + rows_ref.shape[0]) + j]
        attend_one(rows, length, prefix_ref[j], NN, span_ref[j], uv_ref, latent, store)


def moved_kernel(
    rank_ref,
    lengths_ref,
    destination_ref,
    member_ref,
    rows_ref,
    mine_ref,
    other_ref,
    span_ref,
    uv_ref,
    out_ref,
):
    heads, latent, value = uv_ref.shape
    here, _, width = rows_ref.shape
    span_rows = span_ref.shape[1]
    hops, _, part, _ = mine_ref.shape

    def place(key):
        side = lax.div(key, hops * part)
        hop = lax.rem(lax.div(key, part), hops)
        layer = lax.rem(member_ref[0] - hop + hops, hops)
        core = jnp.where(side == 0, member_ref[1], 1 - member_ref[1])
        return (layer * 2 + core) * part + lax.rem(key, part)

    for j in range(here):
        at = slice(j * span_rows, (j + 1) * span_rows)

        def store(h, part):
            out_ref[at, h * value : (h + 1) * value] = part

        ranks = destination_ref.shape[1]
        requests = lengths_ref.shape[0] // ranks
        source = jnp.int32(0)
        for s in range(ranks):
            source = jnp.where(destination_ref[j, s] == rank_ref[0], jnp.int32(s), source)
        length = lengths_ref[source * requests + requests - here + j]
        prefix = jnp.concatenate(
            [mine_ref[:, j].reshape(-1, width), other_ref[:, j].reshape(-1, width)], axis=0
        )
        attend_one(
            rows_ref[j], length, prefix, NT, span_ref[j], uv_ref, latent, store, place
        )


def attend_call(kernel, operands, specs, shapes):
    flops = 2 * 2 * 128 * (288 * (576 + 512) + 512 * 128)
    outs = [jax.ShapeDtypeStruct(shape, bf16) for shape in shapes]
    return pl.pallas_call(
        kernel,
        out_shape=outs,
        in_specs=[pl.BlockSpec(memory_space=pltpu.SMEM)] * (len(operands) - len(specs)) + specs,
        out_specs=[whole(shape) for shape in shapes],
        grid=(1,),
        compiler_params=params(),
        cost_estimate=cost(flops, 2 << 20),
    )(*operands)


def whole(shape, block=0):
    return pl.BlockSpec(tuple(shape), lambda i: (block,) + (0,) * (len(shape) - 1))


def share_kernel(values_ref, weight_ref, out_ref, turned):
    @pl.when(pl.program_id(0) == 0)
    def _():
        turned[...] = values_ref[...].T

    blocks, half, depth = weight_ref.shape
    weight = weight_ref[...].reshape(blocks * half, depth)
    product = jnp.dot(weight, turned[...], preferred_element_type=f32).astype(bf16)
    out_ref[...] = product.reshape(out_ref.shape)


def project(values, weights, layers):
    rows, depth = values.shape
    blocks, half, _ = weights.shape
    each = blocks // layers
    steps = 2
    return pl.pallas_call(
        share_kernel,
        out_shape=jax.ShapeDtypeStruct((layers, each * half, rows), bf16),
        grid=(steps,),
        in_specs=[
            pl.BlockSpec((rows, depth), lambda i: (0, 0)),
            pl.BlockSpec((blocks // steps, half, depth), lambda i: (i, 0, 0)),
        ],
        out_specs=pl.BlockSpec((layers // steps, each * half, rows), lambda i: (i, 0, 0)),
        scratch_shapes=[pltpu.VMEM((depth, rows), bf16)],
        compiler_params=params(),
        cost_estimate=cost(
            2 * rows * depth * blocks * half,
            2 * (rows * depth + blocks * half * depth + blocks * half * rows),
        ),
    )(values, weights)


def hidden_kernel(width, rows_ref, weight_ref, out_ref, total, squares):
    step = pl.program_id(0)
    block = rows_ref[...]
    product = jnp.dot(weight_ref[...], block, preferred_element_type=f32)
    widened = block.astype(f32)
    square = jnp.sum(widened * widened, axis=0, keepdims=True)

    @pl.when(step == 0)
    def _():
        total[...] = product
        squares[...] = square

    @pl.when(step > 0)
    def _():
        total[...] += product
        squares[...] += square

    @pl.when(step == pl.num_programs(0) - 1)
    def _():
        factor = lax.rsqrt(squares[...] / width + norm_eps)
        ff = out_ref.shape[1]
        gate = total[:ff] * factor
        up = total[ff:] * factor
        out_ref[...] = (gate / (1.0 + jnp.exp(-gate)) * up).T.astype(bf16)


def hidden_of(rows_in, weight_in):
    width, slots = rows_in.shape
    ff = weight_in.shape[0] // 2
    steps = 2
    return pl.pallas_call(
        functools.partial(hidden_kernel, float(width)),
        out_shape=jax.ShapeDtypeStruct((slots, ff), bf16),
        grid=(steps,),
        in_specs=[
            pl.BlockSpec((width // steps, slots), lambda i: (i, 0)),
            pl.BlockSpec((2 * ff, width // steps), lambda i: (0, i)),
        ],
        out_specs=pl.BlockSpec((slots, ff), lambda i: (0, 0)),
        scratch_shapes=[pltpu.VMEM((2 * ff, slots), f32), pltpu.VMEM((1, slots), f32)],
        compiler_params=params(),
        cost_estimate=cost(4 * width * slots * ff, 2 * width * (slots + 2 * ff)),
    )(rows_in, weight_in)


def dispatch_kernel(capacity, top_k, shares_ref, packed_ref, mixed_ref, out_ref):
    col = mixed_ref.shape[0]
    total = packed_ref[:col].astype(f32)
    total += jnp.sum(shares_ref[...].astype(f32), axis=0)
    mixed = total.astype(bf16)
    mixed_ref[...] = mixed
    notes = packed_ref[col:].astype(f32)
    slot = lax.broadcasted_iota(jnp.int32, (out_ref.shape[0], mixed.shape[1]), 0)
    hit = None
    for k in range(top_k):
        named = notes[k : k + 1] * capacity + notes[top_k + k : top_k + k + 1]
        same = slot == named.astype(jnp.int32)
        hit = same if hit is None else hit | same
    placer = jnp.where(hit, 1.0, 0.0).astype(bf16)
    out_ref[...] = lax.dot_general(placer, mixed, NT, preferred_element_type=f32).astype(bf16)


def dispatch(shares, packed, capacity, top_k, slots):
    col, rows = shares.shape[1:]
    return pl.pallas_call(
        functools.partial(dispatch_kernel, capacity, top_k),
        out_shape=[
            jax.ShapeDtypeStruct((col, rows), bf16),
            jax.ShapeDtypeStruct((slots, col), bf16),
        ],
        grid=(1,),
        in_specs=[whole(shares.shape), whole(packed.shape)],
        out_specs=[whole((col, rows)), whole((slots, col))],
        compiler_params=params(),
        cost_estimate=cost(2 * slots * col * rows, 2 * (9 * col * rows + slots * col)),
    )(shares, packed)


def slices_kernel(layer_ref, in_ref, *refs):
    outs, (held, in_sems, out_sems) = refs[:-3], refs[-3:]
    count, rows, width = held.shape
    loads, stores = [], []
    for hops in range(count):
        at = pl.multiple_of(lax.rem(layer_ref[0] + hops, count) * width, 128)
        loads.append(
            pltpu.make_async_copy(in_ref.at[:, pl.ds(at, width)], held.at[hops], in_sems.at[hops])
        )
        stores.append(pltpu.make_async_copy(held.at[hops], outs[hops], out_sems.at[hops]))
    half = rows // 2
    stores[count // 2] = pltpu.make_async_copy(
        held.at[count // 2, pl.ds(0, half)], outs[count // 2], out_sems.at[count // 2]
    )
    stores.append(
        pltpu.make_async_copy(
            held.at[count // 2, pl.ds(half, half)], outs[count], out_sems.at[count]
        )
    )
    for load in loads:
        load.start()
    for hops, load in enumerate(loads):
        load.wait()
        stores[hops].start()
        if hops == count // 2:
            stores[count].start()
    for store in stores:
        store.wait()


def slices_of(layer, array, count):
    rows, columns = array.shape
    width = columns // count
    shapes = [(rows, width)] * (count + 1)
    shapes[count // 2] = shapes[count] = (rows // 2, width)
    return pl.pallas_call(
        slices_kernel,
        out_shape=[jax.ShapeDtypeStruct(shape, array.dtype) for shape in shapes],
        in_specs=[
            pl.BlockSpec(memory_space=pltpu.SMEM),
            pl.BlockSpec(memory_space=pl.ANY),
        ],
        out_specs=[pl.BlockSpec(memory_space=pl.ANY)] * (count + 1),
        scratch_shapes=[
            pltpu.VMEM((count, rows, width), array.dtype),
            pltpu.SemaphoreType.DMA((count,)),
            pltpu.SemaphoreType.DMA((count + 1,)),
        ],
        compiler_params=params(),
        cost_estimate=cost(0, 4 * rows * columns),
    )(layer, array)


def down_kernel(mine_ref, other_ref, mine_weight_ref, other_weight_ref, out_ref):
    depth = mine_ref.shape[1]
    total = jnp.dot(
        mine_ref[...], mine_weight_ref[...].reshape(depth, -1), preferred_element_type=f32
    )
    total += jnp.dot(
        other_ref[...], other_weight_ref[...].reshape(depth, -1), preferred_element_type=f32
    )
    out_ref[...] = total.astype(bf16)


def down_project(*operands):
    shape = (operands[0].shape[0], operands[2].shape[2])
    return pl.pallas_call(
        down_kernel,
        out_shape=jax.ShapeDtypeStruct(shape, bf16),
        grid=(1,),
        in_specs=[whole(o.shape) for o in operands],
        out_specs=whole(shape),
        compiler_params=params(),
        cost_estimate=cost(4 * shape[0] * shape[1] * operands[0].shape[1], 5 << 20),
    )(*operands)


def combine_kernel(combiner_ref, rows_ref, mixed_ref, out_ref):
    total = jnp.dot(combiner_ref[...], rows_ref[...], preferred_element_type=f32)
    out_ref[...] = (total + mixed_ref[...].astype(f32).T).astype(bf16)


def combine(combiner, rows, mixed):
    shape = (combiner.shape[0], rows.shape[1])
    return pl.pallas_call(
        combine_kernel,
        out_shape=jax.ShapeDtypeStruct(shape, bf16),
        grid=(1,),
        in_specs=[whole(o.shape) for o in (combiner, rows, mixed)],
        out_specs=whole(shape),
        compiler_params=params(),
        cost_estimate=cost(2 * shape[0] * shape[1] * rows.shape[0], 1 << 20),
    )(combiner, rows, mixed)


def places_of(route_rows, experts):
    flat_routes = route_rows.reshape(-1)
    hits = (flat_routes[:, None] == jnp.arange(experts, dtype=jnp.int32)[None, :]).astype(jnp.int32)
    earlier = jnp.cumsum(hits, axis=0) - hits
    return jnp.sum(earlier * hits, axis=1).reshape(route_rows.shape)


def per_device(
    queries,
    cache,
    span_latent,
    prefix_len,
    destination,
    uv_weight,
    out_weight,
    residual,
    norm_gain,
    routes,
    route_weight,
    gate_weight,
    up_weight,
    down_weight,
):
    requests, prefix_rows, cached_width = cache.shape
    tok_rows = queries.shape[0]
    model_width = residual.shape[1]
    top_k = routes.shape[1]
    ff = gate_weight.shape[2]
    nz = lax.axis_size("ep")
    rank_count = lax.axis_size(DP)
    members = lax.axis_size(MEM)
    my_rank = lax.axis_index(DP)
    member = lax.axis_index(MEM)
    layer = lax.axis_index("ep")
    core = lax.axis_index("tp")
    col = model_width // members
    capacity = max(2, 3 * tok_rows * top_k // (2 * rank_count))

    def other_core(array):
        return lax.ppermute(array, "tp", [(0, 1), (1, 0)])

    def along(array, hops):
        return lax.ppermute(array, "ep", [(z, (z + hops) % nz) for z in range(nz)])

    ranks = jnp.arange(rank_count, dtype=jnp.int32)
    source_first = jnp.sum(ranks * (destination[0] == my_rank).astype(jnp.int32))
    source_second = jnp.sum(ranks * (destination[1] == my_rank).astype(jnp.int32))
    part = prefix_rows // members
    moving = lax.dynamic_slice_in_dim(cache[requests - 2 :], member * part, part, 1)
    arrived = lax.all_to_all(
        jnp.broadcast_to(moving[None], (rank_count,) + moving.shape), DP, 0, 0, tiled=True
    )
    turned_out = out_weight.T.reshape(2, col // 2, -1)
    out_mine = lax.dynamic_index_in_dim(turned_out, core, 0, keepdims=False)
    out_other = other_core(lax.dynamic_index_in_dim(turned_out, 1 - core, 0, keepdims=False))
    out_cols = lax.all_gather(jnp.concatenate([out_mine, out_other], axis=1), DP, axis=0)
    slices = slices_of(jnp.reshape(layer, (1,)), down_weight[0], nz)
    middle = nz // 2

    down = {0: slices[0], 1: along(slices[1], 1), nz - 1: along(slices[nz - 1], -1)}
    arrived, down = lax.optimization_barrier((arrived, down))
    chosen = jnp.stack(
        [
            lax.dynamic_index_in_dim(arrived[:, 0], source_first, 0, keepdims=False),
            lax.dynamic_index_in_dim(arrived[:, 1], source_second, 0, keepdims=False),
        ]
    )
    moved = [chosen] + [along(chosen, hops) for hops in range(1, nz)]
    first_piece = moved[1]
    moved = jnp.stack(moved)

    window, cache, routes, _ = lax.optimization_barrier((slices[2:], cache, routes, first_piece))
    window = {hops: piece for hops, piece in enumerate(window, 2)}
    window = [
        along(window[middle], middle),
        along(window[nz], -middle),
        along(window[3], 3),
        along(window[nz - 3], -3),
        along(window[2], 2),
        along(window[nz - 2], -2),
    ]

    heads, latent = queries.shape[1], uv_weight.shape[1]
    value = uv_weight.shape[2]
    here = requests - 2
    span_rows = span_latent.shape[1]
    values_shape = (2 * span_rows, heads * value)
    turned = (queries.transpose(1, 2, 0), cache.transpose(0, 2, 1))
    spans = (2, span_rows, cached_width)
    scalars = (jnp.reshape(my_rank, (1,)).astype(jnp.int32), prefix_len, destination)
    values_own, query_rows = attend_call(
        own_kernel,
        (*scalars, *turned, span_latent, uv_weight),
        [
            whole(turned[0].shape),
            whole((here, cached_width, prefix_rows)),
            whole(spans),
            whole(uv_weight.shape),
        ],
        [values_shape, (2, heads * span_rows, cached_width)],
    )

    member_at = jnp.stack([layer, core]).astype(jnp.int32)
    moved_other = other_core(moved)
    (values_moved,) = attend_call(
        moved_kernel,
        (*scalars, member_at, query_rows, moved, moved_other, span_latent, uv_weight),
        [
            whole(query_rows.shape),
            whole(moved.shape),
            whole(moved.shape),
            whole(spans, 1),
            whole(uv_weight.shape),
        ],
        [values_shape],
    )
    values = jnp.concatenate([values_own, values_moved], axis=0)

    places = places_of(routes, rank_count)
    residual_t = lax.dynamic_slice_in_dim(residual, layer * 2 * col, 2 * col, 1).T
    residual_t = residual_t.reshape(2, 2, col // 2, tok_rows)
    residual_t = lax.dynamic_index_in_dim(residual_t, core, 1, keepdims=False)
    packed = jnp.concatenate(
        [
            residual_t.reshape(col, tok_rows),
            routes.T.astype(bf16),
            places.T.astype(bf16),
            jnp.zeros((16 - 2 * top_k, tok_rows), bf16),
        ],
        axis=0,
    )
    values = jnp.concatenate([values, other_core(values)], axis=1)
    out_cols, window, packed = lax.optimization_barrier((out_cols, window, packed))
    down[middle] = jnp.concatenate(window[:2], axis=0)
    down[3], down[nz - 3] = window[2:4]
    down[2], down[nz - 2] = window[4:]
    shares = project(values, out_cols, nz)

    norm_gain, route_weight, shares = lax.optimization_barrier((norm_gain, route_weight, shares))
    slot_index = jnp.arange(rank_count * capacity, dtype=jnp.int32)
    slots = (routes * capacity + places).T
    matches = slots[:, :, None] == slot_index[None, None, :]
    combiner = jnp.sum(
        jnp.where(matches, route_weight.T[:, :, None], jnp.zeros((), route_weight.dtype)), axis=0
    )
    gain = norm_gain.astype(f32)[:, None]
    weight_in = jnp.concatenate([gate_weight[0], up_weight[0]], axis=1)
    weight_in = (weight_in.astype(f32) * gain).astype(bf16)
    weight_in = weight_in.reshape(nz, 2, 2, col // 2, 2 * ff).transpose(0, 2, 1, 3, 4)
    weight_in = weight_in.reshape(model_width, 2 * ff).T
    shares = lax.all_to_all(shares, "ep", 0, 0, tiled=True)
    shares, down, combiner, weight_in = lax.optimization_barrier(
        (shares, down, combiner, weight_in)
    )

    mixed, outgoing = dispatch(shares, packed, capacity, top_k, rank_count * capacity)
    outgoing = outgoing.reshape(rank_count, capacity, col)
    received = lax.all_to_all(outgoing, DP, 0, 0, tiled=True)
    received = received.reshape(rank_count * capacity, col).T
    down, _ = lax.optimization_barrier((down, received))
    down_all = jnp.stack([down[h] for h in range(nz)])
    half = col // 2
    even = jnp.concatenate([down_all[..., :half], down_all[..., col : col + half]], axis=2)
    odd = jnp.concatenate([down_all[..., half:col], down_all[..., col + half :]], axis=2)
    down_mine = jnp.where(core == 0, even, odd)
    down_other = other_core(jnp.where(core == 0, odd, even))
    rows_in = lax.all_gather(received, MEM, axis=0)
    rows_in, down_mine, down_other = lax.optimization_barrier((rows_in, down_mine, down_other))
    hidden = hidden_of(rows_in.reshape(model_width, -1), weight_in)

    half = hidden.shape[0] // 2
    blocks = {0: hidden}
    up_way, down_way = hidden, hidden
    for hops in range(1, middle):
        up_way, down_way = along(up_way, 1), along(down_way, -1)
        blocks[hops], blocks[nz - hops] = up_way, down_way
    blocks[middle] = jnp.concatenate([along(up_way[:half], 1), along(down_way[half:], -1)], axis=0)
    hidden_all = jnp.concatenate([blocks[h] for h in range(nz)], axis=1)
    expert_out = down_project(hidden_all, other_core(hidden_all), down_mine, down_other)
    expert_out = expert_out.reshape(rank_count, capacity, col)

    returned = lax.all_to_all(expert_out, DP, 0, 0, tiled=True)
    total = combine(combiner, returned.reshape(rank_count * capacity, col), mixed)
    group = tok_rows // members
    total = lax.all_to_all(total.reshape(members, group, col), MEM, 0, 0, tiled=True)
    total = total.reshape(nz, 2, group, 2, col // 2).transpose(2, 0, 3, 1, 4)
    return total.reshape(group, model_width)


def solution(mesh):
    in_specs = (
        P(DP, MEM, None),
        P(DP, None, None),
        P(DP, None, None),
        P(),
        P(),
        P(MEM, None, None),
        P(MEM, DP),
        P(DP, None),
        P(),
        P(DP, None),
        P(DP, None),
        P(DP, None, MEM),
        P(DP, None, MEM),
        P(DP, MEM, None),
    )
    out_specs = P(DP + MEM, None)
    return jax.shard_map(
        per_device, mesh=mesh, in_specs=in_specs, out_specs=out_specs, check_vma=False
    )
```

time: 276 us -> 275 us (level)
  waiting for transfers between devices: 90.8 us -> 73 us
  blocking collectives: 36.4 us -> 47 us
  starting transfers between devices: 64.8 us -> 70.9 us
  other arithmetic: 10.2 us -> 13.5 us
  Pallas kernels: 31.7 us -> 28.8 us
    all_to_all x1 -> x3, blocking collectives: 11.9 us -> 47 us  [the longest x1 15.9 us: per_device(): returned = lax.all_to_all(expert_out, DP, 0, 0, tiled=True)]
    all_gather x1 -> x0, blocking collectives: 24.5 us -> none  [per_device(): moved = lax.all_gather(chosen, MEM, axis=0)]
    all_to_all x2 -> x0, starting transfers between devices: 14.1 us -> none  [the longest x1 7.53 us: per_device(): received = lax.all_to_all(outgoing, DP, 0, 0, tiled=True)]
    ppermute x16 -> x23, waiting for transfers between devices: 16.9 us -> 28.5 us  [along(): return lax.ppermute(array, 'ep', [(z, (z + hops) % nz) for z in range(nz)])]
    all_to_all x1, waiting for transfers between devices: 23.2 us -> 13.2 us  [per_device(): shares = lax.all_to_all(shares, 'ep', 0, 0, tiled=True)]
    all_gather x1, waiting for transfers between devices: 36.8 us -> 26.9 us  [per_device(): rows_in = lax.all_gather(received, MEM, axis=0)]
    ppermute x16 -> x23, starting transfers between devices: 30.1 us -> 39.8 us  [along(): return lax.ppermute(array, 'ep', [(z, (z + hops) % nz) for z in range(nz)])]
    all_to_all x2 -> x0, waiting for transfers between devices: 7.86 us -> none  [the longest x1 7.86 us: per_device(): returned = lax.all_to_all(expert_out, DP, 0, 0, tiled=True)]
  transfers between devices with their start and end apart: 27 -> 32, of which waited for: 14 -> 14; matrix products, arithmetic and copies ran while one was open for 9% -> 12% of each run, Pallas kernels for 4% -> 4%
where the time goes in v6:
time: 275 us; the launch traced here: 274 us
  waiting for transfers between devices  73 us (27%)
  starting transfers between devices  70.9 us (26%)
  blocking collectives  47 us (17%)
  Pallas kernels  28.8 us (10%)
  local copies, waits for them, and re-layouts  23.2 us (8%)
  between operations  17.6 us (6%)
  other arithmetic  13.5 us (5%)
    ppermute x23, starting transfers between devices, along(): return lax.ppermute(array, 'ep', [(z, (z + hops) % nz) for z in range(nz)])  39.8 us
    ppermute x23, waiting for transfers between devices, along(): return lax.ppermute(array, 'ep', [(z, (z + hops) % nz) for z in range(nz)])  28.5 us
    all_gather x1, waiting for transfers between devices, per_device(): rows_in = lax.all_gather(received, MEM, axis=0)  26.9 us
    ppermute x5, starting transfers between devices, other_core(): return lax.ppermute(array, 'tp', [(0, 1), (1, 0)])  17.7 us
    all_to_all x1, blocking collectives, per_device(): returned = lax.all_to_all(expert_out, DP, 0, 0, tiled=True)  15.9 us
    all_to_all x1, blocking collectives, per_device(): received = lax.all_to_all(outgoing, DP, 0, 0, tiled=True)  15.6 us
    all_to_all x1, blocking collectives, per_device(): lax.all_to_all(total.reshape(members, group, col), MEM, 0, 0, tiled=True)  15.5 us
    all_to_all x1, waiting for transfers between devices, per_device(): shares = lax.all_to_all(shares, 'ep', 0, 0, tiled=True)  13.2 us
  transfers between devices with their start and end apart: 32, of which 14 were waited for; matrix products, arithmetic and copies ran while one was open for 12% of the time, Pallas kernels for 4%

profile of v6, /device:TPU:1, one launch (start us, length us, event | category | flops | bytes accessed | tf_op | source)
XLA Modules:
  0.0 274.0 jit_solution(2326203922246172130)
XLA Ops:
  7.8 3.3 %collective-permute-start.11 = (bf16[224,512]{1,0:T(8,128)(2,1)S(1)}, bf16[224,512]{1,0:T(8,128)(2,1)S(1)}, u32[]{:S(2)}, u32[]{:S(2)}) collective-permute-start(bf16[224,512]{1,0:T(8,128)(2,1)S(1)} %get-tuple-element.132), channel_id=1, source_target_pairs={{0,1},{1,0},{2,3},{3,2},{4,5},{5,4},{6,7},{7,6},{8,9},{9,8},{10,11... | collective-permute-start | bytes 688136 | tf_op jit(solution)/shard_map/ppermute | solution.py:387
  14.4 5.2 %all-to-all-start = ((bf16[16,2,16,576]{3,2,1,0:T(8,128)(2,1)}), bf16[16,2,16,576]{3,2,1,0:T(8,128)(2,1)S(1)}, u32[]{:S(2)}, u32[]{:S(2)}) async-start(bf16[16,2,16,576]{3,2,1,0:T(8,128)(2,1)} %broadcast_in_dim.12), calls=%async_computation | async-start | bytes 1310720 | tf_op jit(solution)/shard_map/all_to_all | solution.py:397
  22.0 5.7 %collective-permute-start.1 = (bf16[128,896]{1,0:T(8,128)(2,1)}, bf16[128,896]{1,0:T(8,128)(2,1)S(1)}, u32[]{:S(2)}, u32[]{:S(2)}) collective-permute-start(bf16[128,896]{1,0:T(8,128)(2,1)} %get-tuple-element.68), channel_id=1, source_target_pairs={{0,14},{2,0},{4,2},{6,4},{8,6},{10,8},{12,10},{14,12},{1,15},{3,1}... | collective-permute-start | bytes 688136 | tf_op jit(solution)/shard_map/ppermute | solution.py:390
  35.9 3.8 %collective-permute-start.4 = (bf16[2,16,576]{2,1,0:T(8,128)(2,1)S(1)}, bf16[2,16,576]{2,1,0:T(8,128)(2,1)S(1)}, u32[]{:S(2)}, u32[]{:S(2)}) collective-permute-start(bf16[2,16,576]{2,1,0:T(8,128)(2,1)S(1)} %pad_maximum_fusion.6), channel_id=1, source_target_pairs={{0,6},{2,8},{4,10},{6,12},{8,14},{10,0},{12,2},{14,4},{1,7},{3,9},... | collective-permute-start | bytes 110600 | tf_op jit(solution)/shard_map/ppermute | solution.py:390
  41.2 3.4 %collective-permute-start.6 = (bf16[2,16,576]{2,1,0:T(8,128)(2,1)S(1)}, bf16[2,16,576]{2,1,0:T(8,128)(2,1)S(1)}, u32[]{:S(2)}, u32[]{:S(2)}) collective-permute-start(bf16[2,16,576]{2,1,0:T(8,128)(2,1)S(1)} %pad_maximum_fusion.6), channel_id=1, source_target_pairs={{0,10},{2,12},{4,14},{6,0},{8,2},{10,4},{12,6},{14,8},{1,11},{3,13... | collective-permute-start | bytes 110600 | tf_op jit(solution)/shard_map/ppermute | solution.py:390
  50.2 5.8 %collective-permute-start.9 = (bf16[8,2,16,576]{3,2,1,0:T(8,128)(2,1)S(1)}, bf16[8,2,16,576]{3,2,1,0:T(8,128)(2,1)S(1)}, u32[]{:S(2)}, u32[]{:S(2)}) collective-permute-start(bf16[8,2,16,576]{3,2,1,0:T(8,128)(2,1)S(1)} %constant_dynamic-update-slice_fusion.mine_ref), channel_id=1, source_target_pairs={{0,1},{1,0},{2,3},{3,2},{4,5},{5,4},{6,7},{7,6},{8,9},{9,8},{10,11... | collective-permute-start | bytes 884744 | tf_op jit(solution)/shard_map/ppermute | solution.py:387
  57.9 2.9 %collective-permute-start.15 = (bf16[128,896]{1,0:T(8,128)(2,1)}, bf16[128,896]{1,0:T(8,128)(2,1)}, u32[]{:S(2)}, u32[]{:S(2)}) collective-permute-start(bf16[128,896]{1,0:T(8,128)(2,1)} %get-tuple-element.79), channel_id=1, source_target_pairs={{0,10},{2,12},{4,14},{6,0},{8,2},{10,4},{12,6},{14,8},{1,11},{3,13... | collective-permute-start | bytes 688136 | tf_op jit(solution)/shard_map/ppermute | solution.py:390
  61.6 2.7 collective-permute-start.17
  64.3 3.9 %shard_map.137 = (bf16[64,512]{1,0:T(8,128)(2,1)}, bf16[2,128,576]{2,1,0:T(8,128)(2,1)}) custom-call(s32[1]{0:T(128)} %bitcast.rank_ref, s32[64]{0:T(128)} %lengths_ref.3, s32[2,16]{1,0:T(2,128)} %destination_ref.3, bf16[4,576,128]{2,1,0:T(8,128)(2,1)} %bitcast.116, bf16[4,576,256]{2,1,0:T(8,128)(2,1)} %bitcast.108, bf16[4,32,576]{2,1,0:T(8,128)(2,1)} %span_ref.3, ...), custom_call_target="tpu_custom_call" | custom-call | flops 193986560 | bytes 2097152 | tf_op jit(solution)/shard_map/pallas_call | solution.py:126
  70.3 3.6 %shard_map.138 = bf16[64,512]{1,0:T(8,128)(2,1)} custom-call(s32[1]{0:T(128)} %bitcast.rank_ref, s32[64]{0:T(128)} %lengths_ref.3, s32[2,16]{1,0:T(2,128)} %destination_ref.3, s32[2]{0:T(128)} %pad_add_fusion.member_ref, bf16[2,128,576]{2,1,0:T(8,128)(2,1)} %get-tuple-element.75.rows_ref, bf16[8,2,16,576]{3,2,1,0:T(8,128)(2,1)} %copy-done.3, ...), custom_call_target="tpu_custom_call" | custom-call | flops 193986560 | bytes 2097152 | tf_op jit(solution)/shard_map/pallas_call | solution.py:126
  74.7 12.7 %collective-permute-done.12 = bf16[64,896]{1,0:T(8,128)(2,1)S(1)} collective-permute-done((bf16[64,896]{1,0:T(8,128)(2,1)}, bf16[64,896]{1,0:T(8,128)(2,1)S(1)}, u32[]{:S(2)}, u32[]{:S(2)}) %collective-permute-start.12) | collective-permute-done | bytes 114720 | tf_op jit(solution)/shard_map/ppermute | solution.py:390
  93.8 5.2 %collective-permute-done.13 = bf16[64,896]{1,0:T(8,128)(2,1)S(1)} collective-permute-done((bf16[64,896]{1,0:T(8,128)(2,1)S(1)}, bf16[64,896]{1,0:T(8,128)(2,1)S(1)}, u32[]{:S(2)}, u32[]{:S(2)}) %collective-permute-start.13) | collective-permute-done | bytes 114720 | tf_op jit(solution)/shard_map/ppermute | solution.py:390
  99.1 5.2 %shard_map.139 = bf16[8,448,128]{2,1,0:T(8,128)(2,1)} custom-call(bf16[128,1024]{1,0:T(8,128)(2,1)} %pad_maximum_fusion.3.values_ref, bf16[16,224,1024]{2,1,0:T(8,128)(2,1)} %bitcast.107), custom_call_target="tpu_custom_call" | custom-call | flops 939524096 | bytes 8519680 | tf_op jit(solution)/shard_map/pallas_call | solution.py:157
  104.3 8.2 %all-to-all-start.1 = ((bf16[8,448,128]{2,1,0:T(8,128)(2,1)}), bf16[8,448,128]{2,1,0:T(8,128)(2,1)S(1)}, u32[]{:S(2)}, u32[]{:S(2)}) async-start(bf16[8,448,128]{2,1,0:T(8,128)(2,1)} %shard_map.139), calls=%async_computation.1 | async-start | bytes 1835008 | tf_op jit(solution)/shard_map/all_to_all | solution.py:498
  117.4 5.9 %copy.85 = bf16[7168,256]{0,1:T(8,128)(2,1)} copy(bf16[7168,256]{1,0:T(8,128)(2,1)} %bitcast.106) | data formatting | bytes 7340032 | tf_op jit(solution)/shard_map/reshape | solution.py:497
  125.7 13.2 %all-to-all-done.1.shares_ref = bf16[8,448,128]{2,1,0:T(8,128)(2,1)S(1)} async-done(((bf16[8,448,128]{2,1,0:T(8,128)(2,1)}), bf16[8,448,128]{2,1,0:T(8,128)(2,1)S(1)}, u32[]{:S(2)}, u32[]{:S(2)}) %all-to-all-start.1) | async-done | bytes 917536 | tf_op jit(solution)/shard_map/all_to_all | solution.py:498
  142.1 15.6 %all_to_all.25 = bf16[16,24,448]{2,1,0:T(8,128)(2,1)S(1)} all-to-all(bf16[16,24,448]{2,1,0:T(8,128)(2,1)} %bitcast.122), channel_id=1, replica_groups=mesh['dp'=16,'ep'=8,'tp'=2] {'dp'}, dimensions={0} | all-to-all | bytes 688128 | tf_op jit(solution)/shard_map/all_to_all | solution.py:505
  170.7 26.9 %all-gather.7.cloned.1.call-done = bf16[7168,384]{1,0:T(8,128)(2,1)} async-done(((bf16[448,384]{1,0:T(8,128)(2,1)}), bf16[7168,384]{1,0:T(8,128)(2,1)}) %all-gather.7.cloned.1.call-update) | async-done | bytes 5505040 | tf_op jit(solution)/shard_map/all_gather | solution.py:514
  197.6 5.6 %shard_map.141 = bf16[384,128]{1,0:T(8,128)(2,1)} custom-call(bf16[7168,384]{1,0:T(8,128)(2,1)} %all-gather.7.cloned.1.call-done, bf16[256,7168]{1,0:T(8,128)(2,1)} %bitcast.105), custom_call_target="tpu_custom_call" | custom-call | flops 1409286144 | bytes 9175040 | tf_op jit(solution)/shard_map/pallas_call | solution.py:205
  218.2 2.7 collective-permute-start.26
  222.4 4.6 %collective-permute-start.27 = (bf16[384,1024]{1,0:T(8,128)(2,1)S(1)}, bf16[384,1024]{1,0:T(8,128)(2,1)}, u32[]{:S(2)}, u32[]{:S(2)}) collective-permute-start(bf16[384,1024]{1,0:T(8,128)(2,1)S(1)} %constant_dynamic-update-slice_fusion.8.mine_ref), channel_id=1, source_target_pairs={{0,1},{1,0},{2,3},{3,2},{4,5},{5,4},{6,7},{7,6},{8,9},{9,8},{10,11... | collective-permute-start | bytes 2359304 | tf_op jit(solution)/shard_map/ppermute | solution.py:387
  229.1 3.7 %shard_map.142 = bf16[384,448]{1,0:T(8,128)(2,1)} custom-call(bf16[384,1024]{1,0:T(8,128)(2,1)} %copy-done.2, bf16[384,1024]{1,0:T(8,128)(2,1)} %collective-permute-done.27.other_ref, bf16[8,128,448]{2,1,0:T(8,128)(2,1)} %get-tuple-element.118.mine_weight_ref, bf16[8,128,448]{2,1,0:T(8,128)(2,1)} %copy.88.other_weight_ref), custom_call_target="tpu_custom_call" | custom-call | flops 704643072 | bytes 5242880 | tf_op jit(solution)/shard_map/pallas_call | solution.py:319
  232.8 15.9 %all_to_all.26 = bf16[16,24,448]{2,1,0:T(8,128)(2,1)} all-to-all(bf16[16,24,448]{2,1,0:T(8,128)(2,1)} %bitcast.114), channel_id=1, replica_groups=mesh['dp'=16,'ep'=8,'tp'=2] {'dp'}, dimensions={0} | all-to-all | bytes 688128 | tf_op jit(solution)/shard_map/all_to_all | solution.py:529
  250.6 15.5 %all_to_all.27 = bf16[16,8,448]{2,1,0:T(8,128)(2,1)S(1)} all-to-all(bf16[16,8,448]{2,1,0:T(8,128)(2,1)} %bitcast.118), channel_id=1, replica_groups=mesh['dp'=16,'ep'=8,'tp'=2] {'ep','tp'}, dimensions={0} | all-to-all | bytes 229376 | tf_op jit(solution)/shard_map/all_to_all | solution.py:532
  (153 shorter events, 75.3 us)
Async XLA Ops:
  6.5 92.5 %all-gather.5.cloned.1.call-start = ((), (), s32[]{:S(2)}) async-start(), calls=%async_computation.5 | async-start | bytes 7798784 | tf_op jit(solution)/shard_map/all_gather | solution.py:403
  14.4 20.9 %all-to-all-start = ((bf16[16,2,16,576]{3,2,1,0:T(8,128)(2,1)}), bf16[16,2,16,576]{3,2,1,0:T(8,128)(2,1)S(1)}, u32[]{:S(2)}, u32[]{:S(2)}) async-start(bf16[16,2,16,576]{3,2,1,0:T(8,128)(2,1)} %broadcast_in_dim.12), calls=%async_computation | async-start | bytes 1310720 | tf_op jit(solution)/shard_map/all_to_all | solution.py:397
  22.0 11.0 %collective-permute-start.1 = (bf16[128,896]{1,0:T(8,128)(2,1)}, bf16[128,896]{1,0:T(8,128)(2,1)S(1)}, u32[]{:S(2)}, u32[]{:S(2)}) collective-permute-start(bf16[128,896]{1,0:T(8,128)(2,1)} %get-tuple-element.68), channel_id=1, source_target_pairs={{0,14},{2,0},{4,2},{6,4},{8,6},{10,8},{12,10},{14,12},{1,15},{3,1}... | collective-permute-start | bytes 688136 | tf_op jit(solution)/shard_map/ppermute | solution.py:390
  27.7 7.6 %collective-permute-start = (bf16[128,896]{1,0:T(8,128)(2,1)}, bf16[128,896]{1,0:T(8,128)(2,1)S(1)}, u32[]{:S(2)}, u32[]{:S(2)}) collective-permute-start(bf16[128,896]{1,0:T(8,128)(2,1)} %get-tuple-element.71), channel_id=1, source_target_pairs={{0,2},{2,4},{4,6},{6,8},{8,10},{10,12},{12,14},{14,0},{1,3},{3,5},... | collective-permute-start | bytes 688136 | tf_op jit(solution)/shard_map/ppermute | solution.py:390
  35.4 9.2 %collective-permute-start.2 = (bf16[2,16,576]{2,1,0:T(8,128)(2,1)S(1)}, bf16[2,16,576]{2,1,0:T(8,128)(2,1)S(1)}, u32[]{:S(2)}, u32[]{:S(2)}) collective-permute-start(bf16[2,16,576]{2,1,0:T(8,128)(2,1)S(1)} %pad_maximum_fusion.6), channel_id=1, source_target_pairs={{0,2},{2,4},{4,6},{6,8},{8,10},{10,12},{12,14},{14,0},{1,3},{3,5},... | collective-permute-start | bytes 110600 | tf_op jit(solution)/shard_map/ppermute | solution.py:390
  35.5 11.4 %collective-permute-start.3 = (bf16[2,16,576]{2,1,0:T(8,128)(2,1)S(1)}, bf16[2,16,576]{2,1,0:T(8,128)(2,1)S(1)}, u32[]{:S(2)}, u32[]{:S(2)}) collective-permute-start(bf16[2,16,576]{2,1,0:T(8,128)(2,1)S(1)} %pad_maximum_fusion.6), channel_id=1, source_target_pairs={{0,4},{2,6},{4,8},{6,10},{8,12},{10,14},{12,0},{14,2},{1,5},{3,7},... | collective-permute-start | bytes 110600 | tf_op jit(solution)/shard_map/ppermute | solution.py:390
  35.9 11.9 %collective-permute-start.4 = (bf16[2,16,576]{2,1,0:T(8,128)(2,1)S(1)}, bf16[2,16,576]{2,1,0:T(8,128)(2,1)S(1)}, u32[]{:S(2)}, u32[]{:S(2)}) collective-permute-start(bf16[2,16,576]{2,1,0:T(8,128)(2,1)S(1)} %pad_maximum_fusion.6), channel_id=1, source_target_pairs={{0,6},{2,8},{4,10},{6,12},{8,14},{10,0},{12,2},{14,4},{1,7},{3,9},... | collective-permute-start | bytes 110600 | tf_op jit(solution)/shard_map/ppermute | solution.py:390
  39.6 8.1 %collective-permute-start.5 = (bf16[2,16,576]{2,1,0:T(8,128)(2,1)S(1)}, bf16[2,16,576]{2,1,0:T(8,128)(2,1)S(1)}, u32[]{:S(2)}, u32[]{:S(2)}) collective-permute-start(bf16[2,16,576]{2,1,0:T(8,128)(2,1)S(1)} %pad_maximum_fusion.6), channel_id=1, source_target_pairs={{0,8},{2,10},{4,12},{6,14},{8,0},{10,2},{12,4},{14,6},{1,9},{3,11}... | collective-permute-start | bytes 110600 | tf_op jit(solution)/shard_map/ppermute | solution.py:390
  41.2 6.8 %collective-permute-start.6 = (bf16[2,16,576]{2,1,0:T(8,128)(2,1)S(1)}, bf16[2,16,576]{2,1,0:T(8,128)(2,1)S(1)}, u32[]{:S(2)}, u32[]{:S(2)}) collective-permute-start(bf16[2,16,576]{2,1,0:T(8,128)(2,1)S(1)} %pad_maximum_fusion.6), channel_id=1, source_target_pairs={{0,10},{2,12},{4,14},{6,0},{8,2},{10,4},{12,6},{14,8},{1,11},{3,13... | collective-permute-start | bytes 110600 | tf_op jit(solution)/shard_map/ppermute | solution.py:390
  50.2 18.6 %collective-permute-start.9 = (bf16[8,2,16,576]{3,2,1,0:T(8,128)(2,1)S(1)}, bf16[8,2,16,576]{3,2,1,0:T(8,128)(2,1)S(1)}, u32[]{:S(2)}, u32[]{:S(2)}) collective-permute-start(bf16[8,2,16,576]{3,2,1,0:T(8,128)(2,1)S(1)} %constant_dynamic-update-slice_fusion.mine_ref), channel_id=1, source_target_pairs={{0,1},{1,0},{2,3},{3,2},{4,5},{5,4},{6,7},{7,6},{8,9},{9,8},{10,11... | collective-permute-start | bytes 884744 | tf_op jit(solution)/shard_map/ppermute | solution.py:387
  56.3 42.8 %collective-permute-start.14 = (bf16[128,896]{1,0:T(8,128)(2,1)}, bf16[128,896]{1,0:T(8,128)(2,1)}, u32[]{:S(2)}, u32[]{:S(2)}) collective-permute-start(bf16[128,896]{1,0:T(8,128)(2,1)} %get-tuple-element.78), channel_id=1, source_target_pairs={{0,6},{2,8},{4,10},{6,12},{8,14},{10,0},{12,2},{14,4},{1,7},{3,9},... | collective-permute-start | bytes 688136 | tf_op jit(solution)/shard_map/ppermute | solution.py:390
  57.9 41.2 %collective-permute-start.15 = (bf16[128,896]{1,0:T(8,128)(2,1)}, bf16[128,896]{1,0:T(8,128)(2,1)}, u32[]{:S(2)}, u32[]{:S(2)}) collective-permute-start(bf16[128,896]{1,0:T(8,128)(2,1)} %get-tuple-element.79), channel_id=1, source_target_pairs={{0,10},{2,12},{4,14},{6,0},{8,2},{10,4},{12,6},{14,8},{1,11},{3,13... | collective-permute-start | bytes 688136 | tf_op jit(solution)/shard_map/ppermute | solution.py:390
  60.8 38.3 %collective-permute-start.16 = (bf16[128,896]{1,0:T(8,128)(2,1)}, bf16[128,896]{1,0:T(8,128)(2,1)}, u32[]{:S(2)}, u32[]{:S(2)}) collective-permute-start(bf16[128,896]{1,0:T(8,128)(2,1)} %get-tuple-element.80), channel_id=1, source_target_pairs={{0,4},{2,6},{4,8},{6,10},{8,12},{10,14},{12,0},{14,2},{1,5},{3,7},... | collective-permute-start | bytes 688136 | tf_op jit(solution)/shard_map/ppermute | solution.py:390
  61.6 37.4 %collective-permute-start.17 = (bf16[128,896]{1,0:T(8,128)(2,1)}, bf16[128,896]{1,0:T(8,128)(2,1)}, u32[]{:S(2)}, u32[]{:S(2)}) collective-permute-start(bf16[128,896]{1,0:T(8,128)(2,1)} %get-tuple-element.81), channel_id=1, source_target_pairs={{0,12},{2,14},{4,0},{6,2},{8,4},{10,6},{12,8},{14,10},{1,13},{3,15... | collective-permute-start | bytes 688136 | tf_op jit(solution)/shard_map/ppermute | solution.py:390
  68.8 18.7 %collective-permute-start.12 = (bf16[64,896]{1,0:T(8,128)(2,1)}, bf16[64,896]{1,0:T(8,128)(2,1)S(1)}, u32[]{:S(2)}, u32[]{:S(2)}) collective-permute-start(bf16[64,896]{1,0:T(8,128)(2,1)} %get-tuple-element.76), channel_id=1, source_target_pairs={{0,8},{2,10},{4,12},{6,14},{8,0},{10,2},{12,4},{14,6},{1,9},{3,11}... | collective-permute-start | bytes 344072 | tf_op jit(solution)/shard_map/ppermute | solution.py:390
  90.8 8.3 %collective-permute-start.13 = (bf16[64,896]{1,0:T(8,128)(2,1)S(1)}, bf16[64,896]{1,0:T(8,128)(2,1)S(1)}, u32[]{:S(2)}, u32[]{:S(2)}) collective-permute-start(bf16[64,896]{1,0:T(8,128)(2,1)S(1)} %copy-done.13), channel_id=1, source_target_pairs={{0,8},{2,10},{4,12},{6,14},{8,0},{10,2},{12,4},{14,6},{1,9},{3,11}... | collective-permute-start | bytes 344072 | tf_op jit(solution)/shard_map/ppermute | solution.py:390
  104.3 34.6 %all-to-all-start.1 = ((bf16[8,448,128]{2,1,0:T(8,128)(2,1)}), bf16[8,448,128]{2,1,0:T(8,128)(2,1)S(1)}, u32[]{:S(2)}, u32[]{:S(2)}) async-start(bf16[8,448,128]{2,1,0:T(8,128)(2,1)} %shard_map.139), calls=%async_computation.1 | async-start | bytes 1835008 | tf_op jit(solution)/shard_map/all_to_all | solution.py:498
  112.5 85.0 %all-gather.7.cloned.1.call-start = ((), (), s32[]{:S(2)}) async-start(), calls=%async_computation.6 | async-start | bytes 5849088 | tf_op jit(solution)/shard_map/all_gather | solution.py:514
  203.2 5.6 %collective-permute-start.19 = (bf16[384,128]{1,0:T(8,128)(2,1)}, bf16[384,128]{1,0:T(8,128)(2,1)S(1)}, u32[]{:S(2)}, u32[]{:S(2)}) collective-permute-start(bf16[384,128]{1,0:T(8,128)(2,1)} %shard_map.141), channel_id=1, source_target_pairs={{0,2},{2,4},{4,6},{6,8},{8,10},{10,12},{12,14},{14,0},{1,3},{3,5},... | collective-permute-start | bytes 294920 | tf_op jit(solution)/shard_map/ppermute | solution.py:390
  208.8 4.7 %collective-permute-start.20 = (bf16[384,128]{1,0:T(8,128)(2,1)S(1)}, bf16[384,128]{1,0:T(8,128)(2,1)S(1)}, u32[]{:S(2)}, u32[]{:S(2)}) collective-permute-start(bf16[384,128]{1,0:T(8,128)(2,1)S(1)} %collective-permute-done.19), channel_id=1, source_target_pairs={{0,2},{2,4},{4,6},{6,8},{8,10},{10,12},{12,14},{14,0},{1,3},{3,5},... | collective-permute-start | bytes 294920 | tf_op jit(solution)/shard_map/ppermute | solution.py:390
  208.8 4.7 %collective-permute-start.24 = (bf16[384,128]{1,0:T(8,128)(2,1)S(1)}, bf16[384,128]{1,0:T(8,128)(2,1)S(1)}, u32[]{:S(2)}, u32[]{:S(2)}) collective-permute-start(bf16[384,128]{1,0:T(8,128)(2,1)S(1)} %collective-permute-done.23), channel_id=1, source_target_pairs={{0,14},{2,0},{4,2},{6,4},{8,6},{10,8},{12,10},{14,12},{1,15},{3,1}... | collective-permute-start | bytes 294920 | tf_op jit(solution)/shard_map/ppermute | solution.py:390
  213.4 4.7 %collective-permute-start.21 = (bf16[384,128]{1,0:T(8,128)(2,1)S(1)}, bf16[384,128]{1,0:T(8,128)(2,1)S(1)}, u32[]{:S(2)}, u32[]{:S(2)}) collective-permute-start(bf16[384,128]{1,0:T(8,128)(2,1)S(1)} %collective-permute-done.20), channel_id=1, source_target_pairs={{0,2},{2,4},{4,6},{6,8},{8,10},{10,12},{12,14},{14,0},{1,3},{3,5},... | collective-permute-start | bytes 294920 | tf_op jit(solution)/shard_map/ppermute | solution.py:390
  213.4 4.7 %collective-permute-start.25 = (bf16[384,128]{1,0:T(8,128)(2,1)S(1)}, bf16[384,128]{1,0:T(8,128)(2,1)S(1)}, u32[]{:S(2)}, u32[]{:S(2)}) collective-permute-start(bf16[384,128]{1,0:T(8,128)(2,1)S(1)} %collective-permute-done.24), channel_id=1, source_target_pairs={{0,14},{2,0},{4,2},{6,4},{8,6},{10,8},{12,10},{14,12},{1,15},{3,1}... | collective-permute-start | bytes 294920 | tf_op jit(solution)/shard_map/ppermute | solution.py:390
  222.4 6.6 %collective-permute-start.27 = (bf16[384,1024]{1,0:T(8,128)(2,1)S(1)}, bf16[384,1024]{1,0:T(8,128)(2,1)}, u32[]{:S(2)}, u32[]{:S(2)}) collective-permute-start(bf16[384,1024]{1,0:T(8,128)(2,1)S(1)} %constant_dynamic-update-slice_fusion.8.mine_ref), channel_id=1, source_target_pairs={{0,1},{1,0},{2,3},{3,2},{4,5},{5,4},{6,7},{7,6},{8,9},{9,8},{10,11... | collective-permute-start | bytes 2359304 | tf_op jit(solution)/shard_map/ppermute | solution.py:387
  (23 other events, 276.8 us)
Sparse Core Ops, SparseCore 0:
  13.2 72.8 all-gather.4
  158.8 38.6 all-gather.6

commit v7 on v6

--- a/solution.py
+++ b/solution.py
@@ -26,15 +26,13 @@
     return pl.CostEstimate(flops=flops, bytes_accessed=nbytes, transcendentals=0)
 
 
-def attend_one(rows, length, prefix, prefix_dims, span, uv_ref, latent, store, place=None):
+def attend_one(rows, length, prefix, prefix_dims, span, uv_ref, latent, store):
     total, span_rows = rows.shape[0], span.shape[0]
     keys_first = prefix_dims is NT
     cached = prefix[:, :latent] if keys_first else prefix[:latent]
     first = lax.dot_general(rows, prefix, prefix_dims, preferred_element_type=f32) * score_scale
     second = lax.dot_general(rows, span, NT, preferred_element_type=f32) * score_scale
     key = lax.broadcasted_iota(jnp.int32, first.shape, 1)
-    if place is not None:
-        key = place(key)
     first = jnp.where(key < length, first, -jnp.inf)
     token = lax.rem(lax.broadcasted_iota(jnp.int32, second.shape, 0), span_rows)
     late = lax.broadcasted_iota(jnp.int32, second.shape, 1)
@@ -76,30 +74,10 @@
         attend_one(rows, length, prefix_ref[j], NN, span_ref[j], uv_ref, latent, store)
 
 
-def moved_kernel(
-    rank_ref,
-    lengths_ref,
-    destination_ref,
-    member_ref,
-    rows_ref,
-    mine_ref,
-    other_ref,
-    span_ref,
-    uv_ref,
-    out_ref,
-):
+def moved_kernel(rank_ref, lengths_ref, destination_ref, rows_ref, prefix_ref, span_ref, uv_ref, out_ref):
     heads, latent, value = uv_ref.shape
     here, _, width = rows_ref.shape
     span_rows = span_ref.shape[1]
-    hops, _, part, _ = mine_ref.shape
-
-    def place(key):
-        side = lax.div(key, hops * part)
-        hop = lax.rem(lax.div(key, part), hops)
-        layer = lax.rem(member_ref[0] - hop + hops, hops)
-        core = jnp.where(side == 0, member_ref[1], 1 - member_ref[1])
-        return (layer * 2 + core) * part + lax.rem(key, part)
-
     for j in range(here):
         at = slice(j * span_rows, (j + 1) * span_rows)
 
@@ -112,12 +90,8 @@
         for s in range(ranks):
             source = jnp.where(destination_ref[j, s] == rank_ref[0], jnp.int32(s), source)
         length = lengths_ref[source * requests + requests - here + j]
-        prefix = jnp.concatenate(
-            [mine_ref[:, j].reshape(-1, width), other_ref[:, j].reshape(-1, width)], axis=0
-        )
-        attend_one(
-            rows_ref[j], length, prefix, NT, span_ref[j], uv_ref, latent, store, place
-        )
+        prefix = prefix_ref[:, j].reshape(-1, width)
+        attend_one(rows_ref[j], length, prefix, NT, span_ref[j], uv_ref, latent, store)
 
 
 def attend_call(kernel, operands, specs, shapes):
@@ -126,7 +100,7 @@
     return pl.pallas_call(
         kernel,
         out_shape=outs,
-        in_specs=[pl.BlockSpec(memory_space=pltpu.SMEM)] * (len(operands) - len(specs)) + specs,
+        in_specs=[pl.BlockSpec(memory_space=pltpu.SMEM)] * 3 + specs,
         out_specs=[whole(shape) for shape in shapes],
         grid=(1,),
         compiler_params=params(),
@@ -412,20 +386,18 @@
             lax.dynamic_index_in_dim(arrived[:, 1], source_second, 0, keepdims=False),
         ]
     )
-    moved = [chosen] + [along(chosen, hops) for hops in range(1, nz)]
-    first_piece = moved[1]
-    moved = jnp.stack(moved)
-
-    window, cache, routes, _ = lax.optimization_barrier((slices[2:], cache, routes, first_piece))
-    window = {hops: piece for hops, piece in enumerate(window, 2)}
-    window = [
-        along(window[middle], middle),
-        along(window[nz], -middle),
-        along(window[3], 3),
-        along(window[nz - 3], -3),
-        along(window[2], 2),
-        along(window[nz - 2], -2),
-    ]
+    moved = lax.all_gather(chosen, MEM, axis=0)
+
+    window, held = lax.optimization_barrier(
+        ((slices[3], slices[nz - 3], slices[middle], slices[nz]), (cache, routes, moved))
+    )
+    cache, routes, moved = held
+    window = (
+        along(window[0], 3),
+        along(window[1], -3),
+        along(window[2], middle),
+        along(window[3], -middle),
+    )
 
     heads, latent = queries.shape[1], uv_weight.shape[1]
     value = uv_weight.shape[2]
@@ -447,18 +419,10 @@
         [values_shape, (2, heads * span_rows, cached_width)],
     )
 
-    member_at = jnp.stack([layer, core]).astype(jnp.int32)
-    moved_other = other_core(moved)
     (values_moved,) = attend_call(
         moved_kernel,
-        (*scalars, member_at, query_rows, moved, moved_other, span_latent, uv_weight),
-        [
-            whole(query_rows.shape),
-            whole(moved.shape),
-            whole(moved.shape),
-            whole(spans, 1),
-            whole(uv_weight.shape),
-        ],
+        (*scalars, query_rows, moved, span_latent, uv_weight),
+        [whole(query_rows.shape), whole(moved.shape), whole(spans, 1), whole(uv_weight.shape)],
         [values_shape],
     )
     values = jnp.concatenate([values_own, values_moved], axis=0)
@@ -478,9 +442,8 @@
     )
     values = jnp.concatenate([values, other_core(values)], axis=1)
     out_cols, window, packed = lax.optimization_barrier((out_cols, window, packed))
-    down[middle] = jnp.concatenate(window[:2], axis=0)
-    down[3], down[nz - 3] = window[2:4]
-    down[2], down[nz - 2] = window[4:]
+    down[3], down[nz - 3] = window[:2]
+    down[middle] = jnp.concatenate(window[2:], axis=0)
     shares = project(values, out_cols, nz)
 
     norm_gain, route_weight, shares = lax.optimization_barrier((norm_gain, route_weight, shares))
@@ -500,9 +463,13 @@
         (shares, down, combiner, weight_in)
     )
 
+    window, _ = lax.optimization_barrier(((slices[2], slices[nz - 2]), shares))
+    window = (along(window[0], 2), along(window[1], -2))
     mixed, outgoing = dispatch(shares, packed, capacity, top_k, rank_count * capacity)
     outgoing = outgoing.reshape(rank_count, capacity, col)
     received = lax.all_to_all(outgoing, DP, 0, 0, tiled=True)
+    received, window = lax.optimization_barrier((received, window))
+    down[2], down[nz - 2] = window
     received = received.reshape(rank_count * capacity, col).T
     down, _ = lax.optimization_barrier((down, received))
     down_all = jnp.stack([down[h] for h in range(nz)])

time: 275 us -> 271 us (0.985)
  starting transfers between devices: 70.9 us -> 60.9 us
  blocking collectives: 47 us -> 55.9 us
  waiting for transfers between devices: 73 us -> 70 us
    all_gather x0 -> x1, blocking collectives: none -> 24.6 us  [per_device(): moved = lax.all_gather(chosen, MEM, axis=0)]
    all_to_all x1 -> x0, blocking collectives: 15.6 us -> none  [per_device(): received = lax.all_to_all(outgoing, DP, 0, 0, tiled=True)]
    ppermute x23 -> x16, waiting for transfers between devices: 28.5 us -> 15.5 us  [along(): return lax.ppermute(array, 'ep', [(z, (z + hops) % nz) for z in range(nz)])]
    ppermute x23 -> x16, starting transfers between devices: 39.8 us -> 30 us  [along(): return lax.ppermute(array, 'ep', [(z, (z + hops) % nz) for z in range(nz)])]
    all_gather x1, waiting for transfers between devices: 26.9 us -> 35 us  [per_device(): rows_in = lax.all_gather(received, MEM, axis=0)]
    ppermute x5 -> x4, starting transfers between devices: 17.7 us -> 11.9 us  [other_core(): return lax.ppermute(array, 'tp', [(0, 1), (1, 0)])]
    all_to_all x0 -> x1, starting transfers between devices: none -> 4.57 us  [per_device(): received = lax.all_to_all(outgoing, DP, 0, 0, tiled=True)]
    unnamed x48 -> x42, local copies, waits for them, and re-layouts: 6.24 us -> 6.56 us
  transfers between devices with their start and end apart: 32 -> 25, of which waited for: 14 -> 13; matrix products, arithmetic and copies ran while one was open for 12% -> 11% of each run, Pallas kernels for 4% -> 4%
where the time goes in v7:
time: 271 us; the launch traced here: 269 us
  waiting for transfers between devices  70 us (26%)
  starting transfers between devices  60.9 us (22%)
  blocking collectives  55.9 us (21%)
  Pallas kernels  28.7 us (11%)
  local copies, waits for them, and re-layouts  23.5 us (9%)
  between operations  17.4 us (6%)
  other arithmetic  13 us (5%)
    all_gather x1, waiting for transfers between devices, per_device(): rows_in = lax.all_gather(received, MEM, axis=0)  35 us
    ppermute x16, starting transfers between devices, along(): return lax.ppermute(array, 'ep', [(z, (z + hops) % nz) for z in range(nz)])  30 us
    all_gather x1, blocking collectives, per_device(): moved = lax.all_gather(chosen, MEM, axis=0)  24.6 us
    all_to_all x1, blocking collectives, per_device(): returned = lax.all_to_all(expert_out, DP, 0, 0, tiled=True)  15.9 us
    ppermute x16, waiting for transfers between devices, along(): return lax.ppermute(array, 'ep', [(z, (z + hops) % nz) for z in range(nz)])  15.5 us
    all_to_all x1, blocking collectives, per_device(): lax.all_to_all(total.reshape(members, group, col), MEM, 0, 0, tiled=True)  15.5 us
    all_to_all x1, waiting for transfers between devices, per_device(): shares = lax.all_to_all(shares, 'ep', 0, 0, tiled=True)  13.2 us
    ppermute x4, starting transfers between devices, other_core(): return lax.ppermute(array, 'tp', [(0, 1), (1, 0)])  11.9 us
  transfers between devices with their start and end apart: 25, of which 13 were waited for; matrix products, arithmetic and copies ran while one was open for 11% of the time, Pallas kernels for 4%

profile of v7, /device:TPU:1, one launch (start us, length us, event | category | flops | bytes accessed | tf_op | source)
XLA Modules:
  0.0 269.5 jit_solution(6411313755372901928)
XLA Ops:
  7.8 3.3 %collective-permute-start.3 = (bf16[224,512]{1,0:T(8,128)(2,1)S(1)}, bf16[224,512]{1,0:T(8,128)(2,1)S(1)}, u32[]{:S(2)}, u32[]{:S(2)}) collective-permute-start(bf16[224,512]{1,0:T(8,128)(2,1)S(1)} %get-tuple-element.132), channel_id=1, source_target_pairs={{0,1},{1,0},{2,3},{3,2},{4,5},{5,4},{6,7},{7,6},{8,9},{9,8},{10,11... | collective-permute-start | bytes 688136 | tf_op jit(solution)/shard_map/ppermute | solution.py:361
  14.4 5.0 %all-to-all-start = ((bf16[16,2,16,576]{3,2,1,0:T(8,128)(2,1)}), bf16[16,2,16,576]{3,2,1,0:T(8,128)(2,1)S(1)}, u32[]{:S(2)}, u32[]{:S(2)}) async-start(bf16[16,2,16,576]{3,2,1,0:T(8,128)(2,1)} %broadcast_in_dim.12), calls=%async_computation | async-start | bytes 1310720 | tf_op jit(solution)/shard_map/all_to_all | solution.py:371
  23.6 4.0 %collective-permute-start.1 = (bf16[128,896]{1,0:T(8,128)(2,1)}, bf16[128,896]{1,0:T(8,128)(2,1)S(1)}, u32[]{:S(2)}, u32[]{:S(2)}) collective-permute-start(bf16[128,896]{1,0:T(8,128)(2,1)} %get-tuple-element.69), channel_id=1, source_target_pairs={{0,14},{2,0},{4,2},{6,4},{8,6},{10,8},{12,10},{14,12},{1,15},{3,1}... | collective-permute-start | bytes 688136 | tf_op jit(solution)/shard_map/ppermute | solution.py:364
  33.3 24.6 %all-gather = bf16[32,16,576]{2,1,0:T(8,128)(2,1)} all-gather(bf16[2,16,576]{2,1,0:T(8,128)(2,1)S(1)} %pad_maximum_fusion.6), channel_id=2, replica_groups=mesh['dp'=16,'ep'=8,'tp'=2] {'ep','tp'}, dimensions={0}, use_global_device_ids=true | all-gather | bytes 626688 | tf_op jit(solution)/shard_map/all_gather | solution.py:389
  59.5 4.5 %collective-permute-start.5 = (bf16[128,896]{1,0:T(8,128)(2,1)}, bf16[128,896]{1,0:T(8,128)(2,1)S(1)}, u32[]{:S(2)}, u32[]{:S(2)}) collective-permute-start(bf16[128,896]{1,0:T(8,128)(2,1)} %get-tuple-element.76), channel_id=1, source_target_pairs={{0,10},{2,12},{4,14},{6,0},{8,2},{10,4},{12,6},{14,8},{1,11},{3,13... | collective-permute-start | bytes 688136 | tf_op jit(solution)/shard_map/ppermute | solution.py:364
  64.9 4.5 %collective-permute-start.7 = (bf16[64,896]{1,0:T(8,128)(2,1)}, bf16[64,896]{1,0:T(8,128)(2,1)S(1)}, u32[]{:S(2)}, u32[]{:S(2)}) collective-permute-start(bf16[64,896]{1,0:T(8,128)(2,1)} %get-tuple-element.78), channel_id=1, source_target_pairs={{0,8},{2,10},{4,12},{6,14},{8,0},{10,2},{12,4},{14,6},{1,9},{3,11}... | collective-permute-start | bytes 344072 | tf_op jit(solution)/shard_map/ppermute | solution.py:364
  69.3 3.8 %shard_map.137 = (bf16[64,512]{1,0:T(8,128)(2,1)}, bf16[2,128,576]{2,1,0:T(8,128)(2,1)}) custom-call(s32[1]{0:T(128)} %bitcast.rank_ref, s32[64]{0:T(128)} %lengths_ref.3, s32[2,16]{1,0:T(2,128)} %destination_ref.3, bf16[4,576,128]{2,1,0:T(8,128)(2,1)} %bitcast.101, bf16[4,576,256]{2,1,0:T(8,128)(2,1)} %bitcast.92, bf16[4,32,576]{2,1,0:T(8,128)(2,1)} %span_ref.3, ...), custom_call_target="tpu_custom_call" | custom-call | flops 193986560 | bytes 2097152 | tf_op jit(solution)/shard_map/pallas_call | solution.py:100
  73.2 3.6 %shard_map.138 = bf16[64,512]{1,0:T(8,128)(2,1)} custom-call(s32[1]{0:T(128)} %bitcast.rank_ref, s32[64]{0:T(128)} %lengths_ref.3, s32[2,16]{1,0:T(2,128)} %destination_ref.3, bf16[2,128,576]{2,1,0:T(8,128)(2,1)} %get-tuple-element.73.rows_ref, bf16[16,2,16,576]{3,2,1,0:T(8,128)(2,1)} %bitcast.93, bf16[4,32,576]{2,1,0:T(8,128)(2,1)} %span_ref.3, ...), custom_call_target="tpu_custom_call" | custom-call | flops 193986560 | bytes 2097152 | tf_op jit(solution)/shard_map/pallas_call | solution.py:100
  85.9 5.2 %shard_map.139 = bf16[8,448,128]{2,1,0:T(8,128)(2,1)} custom-call(bf16[128,1024]{1,0:T(8,128)(2,1)} %pad_maximum_fusion.3.values_ref, bf16[16,224,1024]{2,1,0:T(8,128)(2,1)} %bitcast.91), custom_call_target="tpu_custom_call" | custom-call | flops 939524096 | bytes 8519680 | tf_op jit(solution)/shard_map/pallas_call | solution.py:131
  91.1 9.3 %all-to-all-start.1 = ((bf16[8,448,128]{2,1,0:T(8,128)(2,1)}), bf16[8,448,128]{2,1,0:T(8,128)(2,1)S(1)}, u32[]{:S(2)}, u32[]{:S(2)}) async-start(bf16[8,448,128]{2,1,0:T(8,128)(2,1)} %shard_map.139), calls=%async_computation.1 | async-start | bytes 1835008 | tf_op jit(solution)/shard_map/all_to_all | solution.py:461
  105.3 5.9 %copy.85 = bf16[7168,256]{0,1:T(8,128)(2,1)} copy(bf16[7168,256]{1,0:T(8,128)(2,1)} %bitcast.90) | data formatting | bytes 7340032 | tf_op jit(solution)/shard_map/reshape | solution.py:460
  113.6 13.2 %all-to-all-done.1.shares_ref = bf16[8,448,128]{2,1,0:T(8,128)(2,1)S(1)} async-done(((bf16[8,448,128]{2,1,0:T(8,128)(2,1)}), bf16[8,448,128]{2,1,0:T(8,128)(2,1)S(1)}, u32[]{:S(2)}, u32[]{:S(2)}) %all-to-all-start.1) | async-done | bytes 917536 | tf_op jit(solution)/shard_map/all_to_all | solution.py:461
  130.1 4.6 %all-to-all-start.2 = ((bf16[16,24,448]{2,1,0:T(8,128)(2,1)}), bf16[16,24,448]{2,1,0:T(8,128)(2,1)S(1)}, u32[]{:S(2)}, u32[]{:S(2)}) async-start(bf16[16,24,448]{2,1,0:T(8,128)(2,1)} %bitcast.107), calls=%async_computation.2 | async-start | bytes 786432 | tf_op jit(solution)/shard_map/all_to_all | solution.py:470
  134.8 3.6 %collective-permute-start.9 = (bf16[128,896]{1,0:T(8,128)(2,1)}, bf16[128,896]{1,0:T(8,128)(2,1)}, u32[]{:S(2)}, u32[]{:S(2)}) collective-permute-start(bf16[128,896]{1,0:T(8,128)(2,1)} %get-tuple-element.98), channel_id=1, source_target_pairs={{0,12},{2,14},{4,0},{6,2},{8,4},{10,6},{12,8},{14,10},{1,13},{3,15... | collective-permute-start | bytes 688136 | tf_op jit(solution)/shard_map/ppermute | solution.py:364
  138.3 6.1 %collective-permute-done.8 = bf16[128,896]{1,0:T(8,128)(2,1)S(1)} collective-permute-done((bf16[128,896]{1,0:T(8,128)(2,1)}, bf16[128,896]{1,0:T(8,128)(2,1)S(1)}, u32[]{:S(2)}, u32[]{:S(2)}) %collective-permute-start.8) | collective-permute-done | bytes 229408 | tf_op jit(solution)/shard_map/ppermute | solution.py:364
  158.0 35.0 %all-gather.8.cloned.1.call-done = bf16[7168,384]{1,0:T(8,128)(2,1)} async-done(((bf16[448,384]{1,0:T(8,128)(2,1)}), bf16[7168,384]{1,0:T(8,128)(2,1)}) %all-gather.8.cloned.1.call-update) | async-done | bytes 5505040 | tf_op jit(solution)/shard_map/all_gather | solution.py:481
  193.0 5.6 %shard_map.141 = bf16[384,128]{1,0:T(8,128)(2,1)} custom-call(bf16[7168,384]{1,0:T(8,128)(2,1)} %all-gather.8.cloned.1.call-done, bf16[256,7168]{1,0:T(8,128)(2,1)} %bitcast.89), custom_call_target="tpu_custom_call" | custom-call | flops 1409286144 | bytes 9175040 | tf_op jit(solution)/shard_map/pallas_call | solution.py:179
  204.2 2.7 collective-permute-start.16
  208.9 2.7 collective-permute-start.17
  213.6 2.7 %collective-permute-start.18 = (bf16[192,128]{1,0:T(8,128)(2,1)S(1)}, bf16[192,128]{1,0:T(8,128)(2,1)S(1)}, u32[]{:S(2)}, u32[]{:S(2)}) collective-permute-start(bf16[192,128]{1,0:T(8,128)(2,1)S(1)} %slice.58), channel_id=1, source_target_pairs={{0,14},{2,0},{4,2},{6,4},{8,6},{10,8},{12,10},{14,12},{1,15},{3,1}... | collective-permute-start | bytes 147464 | tf_op jit(solution)/shard_map/ppermute | solution.py:364
  217.9 4.6 %collective-permute-start.19 = (bf16[384,1024]{1,0:T(8,128)(2,1)S(1)}, bf16[384,1024]{1,0:T(8,128)(2,1)}, u32[]{:S(2)}, u32[]{:S(2)}) collective-permute-start(bf16[384,1024]{1,0:T(8,128)(2,1)S(1)} %constant_dynamic-update-slice_fusion.mine_ref), channel_id=1, source_target_pairs={{0,1},{1,0},{2,3},{3,2},{4,5},{5,4},{6,7},{7,6},{8,9},{9,8},{10,11... | collective-permute-start | bytes 2359304 | tf_op jit(solution)/shard_map/ppermute | solution.py:361
  224.5 3.7 %shard_map.142 = bf16[384,448]{1,0:T(8,128)(2,1)} custom-call(bf16[384,1024]{1,0:T(8,128)(2,1)} %copy-done.2, bf16[384,1024]{1,0:T(8,128)(2,1)} %collective-permute-done.19.other_ref, bf16[8,128,448]{2,1,0:T(8,128)(2,1)} %get-tuple-element.118.mine_weight_ref, bf16[8,128,448]{2,1,0:T(8,128)(2,1)} %copy.88.other_weight_ref), custom_call_target="tpu_custom_call" | custom-call | flops 704643072 | bytes 5242880 | tf_op jit(solution)/shard_map/pallas_call | solution.py:293
  228.3 15.9 %all_to_all.25 = bf16[16,24,448]{2,1,0:T(8,128)(2,1)} all-to-all(bf16[16,24,448]{2,1,0:T(8,128)(2,1)} %bitcast.99), channel_id=1, replica_groups=mesh['dp'=16,'ep'=8,'tp'=2] {'dp'}, dimensions={0} | all-to-all | bytes 688128 | tf_op jit(solution)/shard_map/all_to_all | solution.py:496
  246.1 15.5 %all_to_all.26 = bf16[16,8,448]{2,1,0:T(8,128)(2,1)S(1)} all-to-all(bf16[16,8,448]{2,1,0:T(8,128)(2,1)} %bitcast.103), channel_id=1, replica_groups=mesh['dp'=16,'ep'=8,'tp'=2] {'ep','tp'}, dimensions={0} | all-to-all | bytes 229376 | tf_op jit(solution)/shard_map/all_to_all | solution.py:499
  (130 shorter events, 62.5 us)
Async XLA Ops:
  6.5 79.4 %all-gather.6.cloned.1.call-start = ((), (), s32[]{:S(2)}) async-start(), calls=%async_computation.5 | async-start | bytes 7798784 | tf_op jit(solution)/shard_map/all_gather | solution.py:377
  7.8 4.4 %collective-permute-start.3 = (bf16[224,512]{1,0:T(8,128)(2,1)S(1)}, bf16[224,512]{1,0:T(8,128)(2,1)S(1)}, u32[]{:S(2)}, u32[]{:S(2)}) collective-permute-start(bf16[224,512]{1,0:T(8,128)(2,1)S(1)} %get-tuple-element.132), channel_id=1, source_target_pairs={{0,1},{1,0},{2,3},{3,2},{4,5},{5,4},{6,7},{7,6},{8,9},{9,8},{10,11... | collective-permute-start | bytes 688136 | tf_op jit(solution)/shard_map/ppermute | solution.py:361
  14.4 18.8 %all-to-all-start = ((bf16[16,2,16,576]{3,2,1,0:T(8,128)(2,1)}), bf16[16,2,16,576]{3,2,1,0:T(8,128)(2,1)S(1)}, u32[]{:S(2)}, u32[]{:S(2)}) async-start(bf16[16,2,16,576]{3,2,1,0:T(8,128)(2,1)} %broadcast_in_dim.12), calls=%async_computation | async-start | bytes 1310720 | tf_op jit(solution)/shard_map/all_to_all | solution.py:371
  21.9 11.3 %collective-permute-start = (bf16[128,896]{1,0:T(8,128)(2,1)}, bf16[128,896]{1,0:T(8,128)(2,1)S(1)}, u32[]{:S(2)}, u32[]{:S(2)}) collective-permute-start(bf16[128,896]{1,0:T(8,128)(2,1)} %get-tuple-element.68), channel_id=1, source_target_pairs={{0,2},{2,4},{4,6},{6,8},{8,10},{10,12},{12,14},{14,0},{1,3},{3,5},... | collective-permute-start | bytes 688136 | tf_op jit(solution)/shard_map/ppermute | solution.py:364
  23.6 9.6 %collective-permute-start.1 = (bf16[128,896]{1,0:T(8,128)(2,1)}, bf16[128,896]{1,0:T(8,128)(2,1)S(1)}, u32[]{:S(2)}, u32[]{:S(2)}) collective-permute-start(bf16[128,896]{1,0:T(8,128)(2,1)} %get-tuple-element.69), channel_id=1, source_target_pairs={{0,14},{2,0},{4,2},{6,4},{8,6},{10,8},{12,10},{14,12},{1,15},{3,1}... | collective-permute-start | bytes 688136 | tf_op jit(solution)/shard_map/ppermute | solution.py:364
  59.4 24.4 %collective-permute-start.4 = (bf16[128,896]{1,0:T(8,128)(2,1)}, bf16[128,896]{1,0:T(8,128)(2,1)}, u32[]{:S(2)}, u32[]{:S(2)}) collective-permute-start(bf16[128,896]{1,0:T(8,128)(2,1)} %get-tuple-element.75), channel_id=1, source_target_pairs={{0,6},{2,8},{4,10},{6,12},{8,14},{10,0},{12,2},{14,4},{1,7},{3,9},... | collective-permute-start | bytes 688136 | tf_op jit(solution)/shard_map/ppermute | solution.py:364
  59.5 24.4 %collective-permute-start.5 = (bf16[128,896]{1,0:T(8,128)(2,1)}, bf16[128,896]{1,0:T(8,128)(2,1)S(1)}, u32[]{:S(2)}, u32[]{:S(2)}) collective-permute-start(bf16[128,896]{1,0:T(8,128)(2,1)} %get-tuple-element.76), channel_id=1, source_target_pairs={{0,10},{2,12},{4,14},{6,0},{8,2},{10,4},{12,6},{14,8},{1,11},{3,13... | collective-permute-start | bytes 688136 | tf_op jit(solution)/shard_map/ppermute | solution.py:364
  64.0 18.0 %collective-permute-start.6 = (bf16[64,896]{1,0:T(8,128)(2,1)}, bf16[64,896]{1,0:T(8,128)(2,1)S(1)}, u32[]{:S(2)}, u32[]{:S(2)}) collective-permute-start(bf16[64,896]{1,0:T(8,128)(2,1)} %get-tuple-element.77), channel_id=1, source_target_pairs={{0,8},{2,10},{4,12},{6,14},{8,0},{10,2},{12,4},{14,6},{1,9},{3,11}... | collective-permute-start | bytes 344072 | tf_op jit(solution)/shard_map/ppermute | solution.py:364
  64.9 18.3 %collective-permute-start.7 = (bf16[64,896]{1,0:T(8,128)(2,1)}, bf16[64,896]{1,0:T(8,128)(2,1)S(1)}, u32[]{:S(2)}, u32[]{:S(2)}) collective-permute-start(bf16[64,896]{1,0:T(8,128)(2,1)} %get-tuple-element.78), channel_id=1, source_target_pairs={{0,8},{2,10},{4,12},{6,14},{8,0},{10,2},{12,4},{14,6},{1,9},{3,11}... | collective-permute-start | bytes 344072 | tf_op jit(solution)/shard_map/ppermute | solution.py:364
  91.1 35.7 %all-to-all-start.1 = ((bf16[8,448,128]{2,1,0:T(8,128)(2,1)}), bf16[8,448,128]{2,1,0:T(8,128)(2,1)S(1)}, u32[]{:S(2)}, u32[]{:S(2)}) async-start(bf16[8,448,128]{2,1,0:T(8,128)(2,1)} %shard_map.139), calls=%async_computation.1 | async-start | bytes 1835008 | tf_op jit(solution)/shard_map/all_to_all | solution.py:461
  130.1 15.1 %all-to-all-start.2 = ((bf16[16,24,448]{2,1,0:T(8,128)(2,1)}), bf16[16,24,448]{2,1,0:T(8,128)(2,1)S(1)}, u32[]{:S(2)}, u32[]{:S(2)}) async-start(bf16[16,24,448]{2,1,0:T(8,128)(2,1)} %bitcast.107), calls=%async_computation.2 | async-start | bytes 786432 | tf_op jit(solution)/shard_map/all_to_all | solution.py:470
  134.6 58.4 %all-gather.8.cloned.1.call-start = ((), (), s32[]{:S(2)}) async-start(), calls=%async_computation.6 | async-start | bytes 5849088 | tf_op jit(solution)/shard_map/all_gather | solution.py:481
  134.7 9.7 %collective-permute-start.8 = (bf16[128,896]{1,0:T(8,128)(2,1)}, bf16[128,896]{1,0:T(8,128)(2,1)S(1)}, u32[]{:S(2)}, u32[]{:S(2)}) collective-permute-start(bf16[128,896]{1,0:T(8,128)(2,1)} %get-tuple-element.97), channel_id=1, source_target_pairs={{0,4},{2,6},{4,8},{6,10},{8,12},{10,14},{12,0},{14,2},{1,5},{3,7},... | collective-permute-start | bytes 688136 | tf_op jit(solution)/shard_map/ppermute | solution.py:364
  134.8 10.3 %collective-permute-start.9 = (bf16[128,896]{1,0:T(8,128)(2,1)}, bf16[128,896]{1,0:T(8,128)(2,1)}, u32[]{:S(2)}, u32[]{:S(2)}) collective-permute-start(bf16[128,896]{1,0:T(8,128)(2,1)} %get-tuple-element.98), channel_id=1, source_target_pairs={{0,12},{2,14},{4,0},{6,2},{8,4},{10,6},{12,8},{14,10},{1,13},{3,15... | collective-permute-start | bytes 688136 | tf_op jit(solution)/shard_map/ppermute | solution.py:364
  153.1 4.9 %collective-permute-start.10 = (bf16[8,128,448]{1,2,0:T(8,128)(2,1)}, bf16[8,128,448]{1,2,0:T(8,128)(2,1)S(1)}, u32[]{:S(2)}, u32[]{:S(2)}) collective-permute-start(bf16[8,128,448]{1,2,0:T(8,128)(2,1)} %copy.87), channel_id=1, source_target_pairs={{0,1},{1,0},{2,3},{3,2},{4,5},{5,4},{6,7},{7,6},{8,9},{9,8},{10,11... | collective-permute-start | bytes 2752520 | tf_op jit(solution)/shard_map/ppermute | solution.py:361
  198.7 5.6 %collective-permute-start.11 = (bf16[384,128]{1,0:T(8,128)(2,1)}, bf16[384,128]{1,0:T(8,128)(2,1)S(1)}, u32[]{:S(2)}, u32[]{:S(2)}) collective-permute-start(bf16[384,128]{1,0:T(8,128)(2,1)} %shard_map.141), channel_id=1, source_target_pairs={{0,2},{2,4},{4,6},{6,8},{8,10},{10,12},{12,14},{14,0},{1,3},{3,5},... | collective-permute-start | bytes 294920 | tf_op jit(solution)/shard_map/ppermute | solution.py:364
  199.7 4.6 %collective-permute-start.15 = (bf16[384,128]{1,0:T(8,128)(2,1)}, bf16[384,128]{1,0:T(8,128)(2,1)S(1)}, u32[]{:S(2)}, u32[]{:S(2)}) collective-permute-start(bf16[384,128]{1,0:T(8,128)(2,1)} %shard_map.141), channel_id=1, source_target_pairs={{0,14},{2,0},{4,2},{6,4},{8,6},{10,8},{12,10},{14,12},{1,15},{3,1}... | collective-permute-start | bytes 294920 | tf_op jit(solution)/shard_map/ppermute | solution.py:364
  204.2 4.7 %collective-permute-start.12 = (bf16[384,128]{1,0:T(8,128)(2,1)S(1)}, bf16[384,128]{1,0:T(8,128)(2,1)S(1)}, u32[]{:S(2)}, u32[]{:S(2)}) collective-permute-start(bf16[384,128]{1,0:T(8,128)(2,1)S(1)} %collective-permute-done.11), channel_id=1, source_target_pairs={{0,2},{2,4},{4,6},{6,8},{8,10},{10,12},{12,14},{14,0},{1,3},{3,5},... | collective-permute-start | bytes 294920 | tf_op jit(solution)/shard_map/ppermute | solution.py:364
  204.2 4.7 %collective-permute-start.16 = (bf16[384,128]{1,0:T(8,128)(2,1)S(1)}, bf16[384,128]{1,0:T(8,128)(2,1)S(1)}, u32[]{:S(2)}, u32[]{:S(2)}) collective-permute-start(bf16[384,128]{1,0:T(8,128)(2,1)S(1)} %collective-permute-done.15), channel_id=1, source_target_pairs={{0,14},{2,0},{4,2},{6,4},{8,6},{10,8},{12,10},{14,12},{1,15},{3,1}... | collective-permute-start | bytes 294920 | tf_op jit(solution)/shard_map/ppermute | solution.py:364
  208.9 4.7 %collective-permute-start.13 = (bf16[384,128]{1,0:T(8,128)(2,1)S(1)}, bf16[384,128]{1,0:T(8,128)(2,1)S(1)}, u32[]{:S(2)}, u32[]{:S(2)}) collective-permute-start(bf16[384,128]{1,0:T(8,128)(2,1)S(1)} %collective-permute-done.12), channel_id=1, source_target_pairs={{0,2},{2,4},{4,6},{6,8},{8,10},{10,12},{12,14},{14,0},{1,3},{3,5},... | collective-permute-start | bytes 294920 | tf_op jit(solution)/shard_map/ppermute | solution.py:364
  208.9 4.7 %collective-permute-start.17 = (bf16[384,128]{1,0:T(8,128)(2,1)S(1)}, bf16[384,128]{1,0:T(8,128)(2,1)S(1)}, u32[]{:S(2)}, u32[]{:S(2)}) collective-permute-start(bf16[384,128]{1,0:T(8,128)(2,1)S(1)} %collective-permute-done.16), channel_id=1, source_target_pairs={{0,14},{2,0},{4,2},{6,4},{8,6},{10,8},{12,10},{14,12},{1,15},{3,1}... | collective-permute-start | bytes 294920 | tf_op jit(solution)/shard_map/ppermute | solution.py:364
  213.6 4.2 %collective-permute-start.14 = (bf16[192,128]{1,0:T(8,128)(2,1)S(1)}, bf16[192,128]{1,0:T(8,128)(2,1)S(1)}, u32[]{:S(2)}, u32[]{:S(2)}) collective-permute-start(bf16[192,128]{1,0:T(8,128)(2,1)S(1)} %slice.57), channel_id=1, source_target_pairs={{0,2},{2,4},{4,6},{6,8},{8,10},{10,12},{12,14},{14,0},{1,3},{3,5},... | collective-permute-start | bytes 147464 | tf_op jit(solution)/shard_map/ppermute | solution.py:364
  213.6 4.1 %collective-permute-start.18 = (bf16[192,128]{1,0:T(8,128)(2,1)S(1)}, bf16[192,128]{1,0:T(8,128)(2,1)S(1)}, u32[]{:S(2)}, u32[]{:S(2)}) collective-permute-start(bf16[192,128]{1,0:T(8,128)(2,1)S(1)} %slice.58), channel_id=1, source_target_pairs={{0,14},{2,0},{4,2},{6,4},{8,6},{10,8},{12,10},{14,12},{1,15},{3,1}... | collective-permute-start | bytes 147464 | tf_op jit(solution)/shard_map/ppermute | solution.py:364
  217.9 6.6 %collective-permute-start.19 = (bf16[384,1024]{1,0:T(8,128)(2,1)S(1)}, bf16[384,1024]{1,0:T(8,128)(2,1)}, u32[]{:S(2)}, u32[]{:S(2)}) collective-permute-start(bf16[384,1024]{1,0:T(8,128)(2,1)S(1)} %constant_dynamic-update-slice_fusion.mine_ref), channel_id=1, source_target_pairs={{0,1},{1,0},{2,3},{3,2},{4,5},{5,4},{6,7},{7,6},{8,9},{9,8},{10,11... | collective-permute-start | bytes 2359304 | tf_op jit(solution)/shard_map/ppermute | solution.py:361
  (16 other events, 221.0 us)
Sparse Core Ops, SparseCore 0:
  13.2 72.6 all-gather.5
  146.2 46.7 all-gather.7

commit v8 on v7

--- a/solution.py
+++ b/solution.py
@@ -277,19 +277,27 @@
     )(layer, array)
 
 
-def down_kernel(mine_ref, other_ref, mine_weight_ref, other_weight_ref, out_ref):
-    depth = mine_ref.shape[1]
-    total = jnp.dot(
-        mine_ref[...], mine_weight_ref[...].reshape(depth, -1), preferred_element_type=f32
-    )
-    total += jnp.dot(
-        other_ref[...], other_weight_ref[...].reshape(depth, -1), preferred_element_type=f32
-    )
+def down_kernel(mine_weight_ref, other_weight_ref, *refs):
+    hidden_refs, out_ref = refs[:-1], refs[-1]
+    total = None
+    for weight_ref, refs_here in (
+        (mine_weight_ref, hidden_refs[:2]),
+        (other_weight_ref, hidden_refs[2:]),
+    ):
+        first = 0
+        for hidden_ref in refs_here:
+            depth = hidden_ref.shape[1]
+            hops = depth // weight_ref.shape[1]
+            weight = weight_ref[first : first + hops].reshape(depth, -1)
+            product = jnp.dot(hidden_ref[...], weight, preferred_element_type=f32)
+            total = product if total is None else total + product
+            first += hops
     out_ref[...] = total.astype(bf16)
 
 
 def down_project(*operands):
-    shape = (operands[0].shape[0], operands[2].shape[2])
+    shape = (operands[2].shape[0], operands[0].shape[2])
+    depth = operands[0].shape[0] * operands[0].shape[1]
     return pl.pallas_call(
         down_kernel,
         out_shape=jax.ShapeDtypeStruct(shape, bf16),
@@ -297,7 +305,7 @@
         in_specs=[whole(o.shape) for o in operands],
         out_specs=whole(shape),
         compiler_params=params(),
-        cost_estimate=cost(4 * shape[0] * shape[1] * operands[0].shape[1], 5 << 20),
+        cost_estimate=cost(4 * shape[0] * shape[1] * depth, 5 << 20),
     )(*operands)
 
 
@@ -472,7 +480,9 @@
     down[2], down[nz - 2] = window
     received = received.reshape(rank_count * capacity, col).T
     down, _ = lax.optimization_barrier((down, received))
-    down_all = jnp.stack([down[h] for h in range(nz)])
+    early = [0, 1, nz - 1, 2, nz - 2]
+    late = [h for h in range(nz) if h not in early]
+    down_all = jnp.stack([down[h] for h in early + late])
     half = col // 2
     even = jnp.concatenate([down_all[..., :half], down_all[..., col : col + half]], axis=2)
     odd = jnp.concatenate([down_all[..., half:col], down_all[..., col + half :]], axis=2)
@@ -489,8 +499,16 @@
         up_way, down_way = along(up_way, 1), along(down_way, -1)
         blocks[hops], blocks[nz - hops] = up_way, down_way
     blocks[middle] = jnp.concatenate([along(up_way[:half], 1), along(down_way[half:], -1)], axis=0)
-    hidden_all = jnp.concatenate([blocks[h] for h in range(nz)], axis=1)
-    expert_out = down_project(hidden_all, other_core(hidden_all), down_mine, down_other)
+    hidden_early = jnp.concatenate([blocks[h] for h in early], axis=1)
+    hidden_late = jnp.concatenate([blocks[h] for h in late], axis=1)
+    expert_out = down_project(
+        down_mine,
+        down_other,
+        hidden_early,
+        hidden_late,
+        other_core(hidden_early),
+        other_core(hidden_late),
+    )
     expert_out = expert_out.reshape(rank_count, capacity, col)
 
     returned = lax.all_to_all(expert_out, DP, 0, 0, tiled=True)

time: 271 us -> 270 us (level)
    ppermute x4 -> x5, starting transfers between devices: 11.9 us -> 13.8 us  [other_core(): return lax.ppermute(array, 'tp', [(0, 1), (1, 0)])]
    unnamed x42 -> x48, local copies, waits for them, and re-layouts: 6.56 us -> 5.78 us
  transfers between devices with their start and end apart: 25 -> 26, of which waited for: 13 -> 12; matrix products, arithmetic and copies ran while one was open for 11% -> 11% of each run, Pallas kernels for 4% -> 4%
where the time goes in v8:
time: 270 us; the launch traced here: 269 us
  waiting for transfers between devices  69.8 us (26%)
  starting transfers between devices  60.3 us (22%)
  blocking collectives  55.9 us (21%)
  Pallas kernels  29 us (11%)
  local copies, waits for them, and re-layouts  23.4 us (9%)
  between operations  17.4 us (6%)
  other arithmetic  13.1 us (5%)
    all_gather x1, waiting for transfers between devices, per_device(): rows_in = lax.all_gather(received, MEM, axis=0)  35.1 us
    ppermute x16, starting transfers between devices, along(): return lax.ppermute(array, 'ep', [(z, (z + hops) % nz) for z in range(nz)])  30.1 us
    all_gather x1, blocking collectives, per_device(): moved = lax.all_gather(chosen, MEM, axis=0)  24.6 us
    ppermute x16, waiting for transfers between devices, along(): return lax.ppermute(array, 'ep', [(z, (z + hops) % nz) for z in range(nz)])  18 us
    all_to_all x1, blocking collectives, per_device(): returned = lax.all_to_all(expert_out, DP, 0, 0, tiled=True)  15.9 us
    all_to_all x1, blocking collectives, per_device(): lax.all_to_all(total.reshape(members, group, col), MEM, 0, 0, tiled=True)  15.5 us
    ppermute x5, starting transfers between devices, other_core(): return lax.ppermute(array, 'tp', [(0, 1), (1, 0)])  13.8 us
    all_to_all x1, waiting for transfers between devices, per_device(): shares = lax.all_to_all(shares, 'ep', 0, 0, tiled=True)  13.2 us
  transfers between devices with their start and end apart: 26, of which 12 were waited for; matrix products, arithmetic and copies ran while one was open for 11% of the time, Pallas kernels for 4%

profile of v8, /device:TPU:1, one launch (start us, length us, event | category | flops | bytes accessed | tf_op | source)
XLA Modules:
  0.0 269.0 jit_solution(3586303933318941980)
XLA Ops:
  7.8 3.3 %collective-permute-start.3 = (bf16[224,512]{1,0:T(8,128)(2,1)S(1)}, bf16[224,512]{1,0:T(8,128)(2,1)S(1)}, u32[]{:S(2)}, u32[]{:S(2)}) collective-permute-start(bf16[224,512]{1,0:T(8,128)(2,1)S(1)} %get-tuple-element.132), channel_id=1, source_target_pairs={{0,1},{1,0},{2,3},{3,2},{4,5},{5,4},{6,7},{7,6},{8,9},{9,8},{10,11... | collective-permute-start | bytes 688136 | tf_op jit(solution)/shard_map/ppermute | solution.py:369
  14.4 5.0 %all-to-all-start = ((bf16[16,2,16,576]{3,2,1,0:T(8,128)(2,1)}), bf16[16,2,16,576]{3,2,1,0:T(8,128)(2,1)S(1)}, u32[]{:S(2)}, u32[]{:S(2)}) async-start(bf16[16,2,16,576]{3,2,1,0:T(8,128)(2,1)} %broadcast_in_dim.12), calls=%async_computation | async-start | bytes 1310720 | tf_op jit(solution)/shard_map/all_to_all | solution.py:379
  23.6 4.0 %collective-permute-start.1 = (bf16[128,896]{1,0:T(8,128)(2,1)}, bf16[128,896]{1,0:T(8,128)(2,1)S(1)}, u32[]{:S(2)}, u32[]{:S(2)}) collective-permute-start(bf16[128,896]{1,0:T(8,128)(2,1)} %get-tuple-element.69), channel_id=1, source_target_pairs={{0,14},{2,0},{4,2},{6,4},{8,6},{10,8},{12,10},{14,12},{1,15},{3,1}... | collective-permute-start | bytes 688136 | tf_op jit(solution)/shard_map/ppermute | solution.py:372
  33.3 24.6 %all-gather = bf16[32,16,576]{2,1,0:T(8,128)(2,1)} all-gather(bf16[2,16,576]{2,1,0:T(8,128)(2,1)S(1)} %pad_maximum_fusion.7), channel_id=2, replica_groups=mesh['dp'=16,'ep'=8,'tp'=2] {'ep','tp'}, dimensions={0}, use_global_device_ids=true | all-gather | bytes 626688 | tf_op jit(solution)/shard_map/all_gather | solution.py:397
  59.5 4.5 %collective-permute-start.5 = (bf16[128,896]{1,0:T(8,128)(2,1)}, bf16[128,896]{1,0:T(8,128)(2,1)S(1)}, u32[]{:S(2)}, u32[]{:S(2)}) collective-permute-start(bf16[128,896]{1,0:T(8,128)(2,1)} %get-tuple-element.76), channel_id=1, source_target_pairs={{0,10},{2,12},{4,14},{6,0},{8,2},{10,4},{12,6},{14,8},{1,11},{3,13... | collective-permute-start | bytes 688136 | tf_op jit(solution)/shard_map/ppermute | solution.py:372
  64.9 4.4 %collective-permute-start.7 = (bf16[64,896]{1,0:T(8,128)(2,1)}, bf16[64,896]{1,0:T(8,128)(2,1)S(1)}, u32[]{:S(2)}, u32[]{:S(2)}) collective-permute-start(bf16[64,896]{1,0:T(8,128)(2,1)} %get-tuple-element.78), channel_id=1, source_target_pairs={{0,8},{2,10},{4,12},{6,14},{8,0},{10,2},{12,4},{14,6},{1,9},{3,11}... | collective-permute-start | bytes 344072 | tf_op jit(solution)/shard_map/ppermute | solution.py:372
  69.4 3.8 %shard_map.137 = (bf16[64,512]{1,0:T(8,128)(2,1)}, bf16[2,128,576]{2,1,0:T(8,128)(2,1)}) custom-call(s32[1]{0:T(128)} %bitcast.rank_ref, s32[64]{0:T(128)} %lengths_ref.3, s32[2,16]{1,0:T(2,128)} %destination_ref.3, bf16[4,576,128]{2,1,0:T(8,128)(2,1)} %bitcast.101, bf16[4,576,256]{2,1,0:T(8,128)(2,1)} %bitcast.92, bf16[4,32,576]{2,1,0:T(8,128)(2,1)} %span_ref.3, ...), custom_call_target="tpu_custom_call" | custom-call | flops 193986560 | bytes 2097152 | tf_op jit(solution)/shard_map/pallas_call | solution.py:100
  73.2 3.6 %shard_map.138 = bf16[64,512]{1,0:T(8,128)(2,1)} custom-call(s32[1]{0:T(128)} %bitcast.rank_ref, s32[64]{0:T(128)} %lengths_ref.3, s32[2,16]{1,0:T(2,128)} %destination_ref.3, bf16[2,128,576]{2,1,0:T(8,128)(2,1)} %get-tuple-element.73.rows_ref, bf16[16,2,16,576]{3,2,1,0:T(8,128)(2,1)} %bitcast.93, bf16[4,32,576]{2,1,0:T(8,128)(2,1)} %span_ref.3, ...), custom_call_target="tpu_custom_call" | custom-call | flops 193986560 | bytes 2097152 | tf_op jit(solution)/shard_map/pallas_call | solution.py:100
  83.9 4.4 %collective-permute-done.5 = bf16[128,896]{1,0:T(8,128)(2,1)S(1)} collective-permute-done((bf16[128,896]{1,0:T(8,128)(2,1)}, bf16[128,896]{1,0:T(8,128)(2,1)S(1)}, u32[]{:S(2)}, u32[]{:S(2)}) %collective-permute-start.5) | collective-permute-done | bytes 229408 | tf_op jit(solution)/shard_map/ppermute | solution.py:372
  88.3 5.3 %shard_map.139 = bf16[8,448,128]{2,1,0:T(8,128)(2,1)} custom-call(bf16[128,1024]{1,0:T(8,128)(2,1)} %pad_maximum_fusion.4.values_ref, bf16[16,224,1024]{2,1,0:T(8,128)(2,1)} %bitcast.91), custom_call_target="tpu_custom_call" | custom-call | flops 939524096 | bytes 8519680 | tf_op jit(solution)/shard_map/pallas_call | solution.py:131
  93.6 6.8 %all-to-all-start.1 = ((bf16[8,448,128]{2,1,0:T(8,128)(2,1)}), bf16[8,448,128]{2,1,0:T(8,128)(2,1)S(1)}, u32[]{:S(2)}, u32[]{:S(2)}) async-start(bf16[8,448,128]{2,1,0:T(8,128)(2,1)} %shard_map.139), calls=%async_computation.1 | async-start | bytes 1835008 | tf_op jit(solution)/shard_map/all_to_all | solution.py:469
  105.3 5.9 %copy.85 = bf16[7168,256]{0,1:T(8,128)(2,1)} copy(bf16[7168,256]{1,0:T(8,128)(2,1)} %bitcast.90) | data formatting | bytes 7340032 | tf_op jit(solution)/shard_map/reshape | solution.py:468
  113.6 13.2 %all-to-all-done.1.shares_ref = bf16[8,448,128]{2,1,0:T(8,128)(2,1)S(1)} async-done(((bf16[8,448,128]{2,1,0:T(8,128)(2,1)}), bf16[8,448,128]{2,1,0:T(8,128)(2,1)S(1)}, u32[]{:S(2)}, u32[]{:S(2)}) %all-to-all-start.1) | async-done | bytes 917536 | tf_op jit(solution)/shard_map/all_to_all | solution.py:469
  130.1 4.6 %all-to-all-start.2 = ((bf16[16,24,448]{2,1,0:T(8,128)(2,1)}), bf16[16,24,448]{2,1,0:T(8,128)(2,1)S(1)}, u32[]{:S(2)}, u32[]{:S(2)}) async-start(bf16[16,24,448]{2,1,0:T(8,128)(2,1)} %bitcast.107), calls=%async_computation.2 | async-start | bytes 786432 | tf_op jit(solution)/shard_map/all_to_all | solution.py:478
  134.8 3.6 %collective-permute-start.9 = (bf16[128,896]{1,0:T(8,128)(2,1)}, bf16[128,896]{1,0:T(8,128)(2,1)}, u32[]{:S(2)}, u32[]{:S(2)}) collective-permute-start(bf16[128,896]{1,0:T(8,128)(2,1)} %get-tuple-element.98), channel_id=1, source_target_pairs={{0,12},{2,14},{4,0},{6,2},{8,4},{10,6},{12,8},{14,10},{1,13},{3,15... | collective-permute-start | bytes 688136 | tf_op jit(solution)/shard_map/ppermute | solution.py:372
  138.4 6.1 %collective-permute-done.8 = bf16[128,896]{1,0:T(8,128)(2,1)S(1)} collective-permute-done((bf16[128,896]{1,0:T(8,128)(2,1)}, bf16[128,896]{1,0:T(8,128)(2,1)S(1)}, u32[]{:S(2)}, u32[]{:S(2)}) %collective-permute-start.8) | collective-permute-done | bytes 229408 | tf_op jit(solution)/shard_map/ppermute | solution.py:372
  158.0 35.1 %all-gather.8.cloned.1.call-done = bf16[7168,384]{1,0:T(8,128)(2,1)} async-done(((bf16[448,384]{1,0:T(8,128)(2,1)}), bf16[7168,384]{1,0:T(8,128)(2,1)}) %all-gather.8.cloned.1.call-update) | async-done | bytes 5505040 | tf_op jit(solution)/shard_map/all_gather | solution.py:491
  193.2 5.6 %shard_map.141 = bf16[384,128]{1,0:T(8,128)(2,1)} custom-call(bf16[7168,384]{1,0:T(8,128)(2,1)} %all-gather.8.cloned.1.call-done, bf16[256,7168]{1,0:T(8,128)(2,1)} %bitcast.89), custom_call_target="tpu_custom_call" | custom-call | flops 1409286144 | bytes 9175040 | tf_op jit(solution)/shard_map/pallas_call | solution.py:179
  211.8 2.9 %collective-permute-start.19 = (bf16[384,640]{1,0:T(8,128)(2,1)S(1)}, bf16[384,640]{1,0:T(8,128)(2,1)}, u32[]{:S(2)}, u32[]{:S(2)}) collective-permute-start(bf16[384,640]{1,0:T(8,128)(2,1)S(1)} %constant_dynamic-update-slice_fusion.refs_0_), channel_id=1, source_target_pairs={{0,1},{1,0},{2,3},{3,2},{4,5},{5,4},{6,7},{7,6},{8,9},{9,8},{10,11... | collective-permute-start | bytes 1474568 | tf_op jit(solution)/shard_map/ppermute | solution.py:369
  214.8 2.7 %collective-permute-start.18 = (bf16[192,128]{1,0:T(8,128)(2,1)S(1)}, bf16[192,128]{1,0:T(8,128)(2,1)S(1)}, u32[]{:S(2)}, u32[]{:S(2)}) collective-permute-start(bf16[192,128]{1,0:T(8,128)(2,1)S(1)} %slice.58), channel_id=1, source_target_pairs={{0,14},{2,0},{4,2},{6,4},{8,6},{10,8},{12,10},{14,12},{1,15},{3,1}... | collective-permute-start | bytes 147464 | tf_op jit(solution)/shard_map/ppermute | solution.py:372
  219.0 3.6 %collective-permute-start.20 = (bf16[384,384]{1,0:T(8,128)(2,1)S(1)}, bf16[384,384]{1,0:T(8,128)(2,1)}, u32[]{:S(2)}, u32[]{:S(2)}) collective-permute-start(bf16[384,384]{1,0:T(8,128)(2,1)S(1)} %pad_maximum_fusion.3.refs_1_), channel_id=1, source_target_pairs={{0,1},{1,0},{2,3},{3,2},{4,5},{5,4},{6,7},{7,6},{8,9},{9,8},{10,11... | collective-permute-start | bytes 884744 | tf_op jit(solution)/shard_map/ppermute | solution.py:369
  223.9 3.9 %shard_map.142 = bf16[384,448]{1,0:T(8,128)(2,1)} custom-call(bf16[8,128,448]{2,1,0:T(8,128)(2,1)} %get-tuple-element.116.mine_weight_ref, bf16[8,128,448]{2,1,0:T(8,128)(2,1)} %copy.88.other_weight_ref, bf16[384,640]{1,0:T(8,128)(2,1)} %copy-done.3, bf16[384,384]{1,0:T(8,128)(2,1)} %copy-done.2, bf16[384,640]{1,0:T(8,128)(2,1)} %collective-permute-done.19.refs_2_, ...), custom_call_target="tpu_custom_call" | custom-call | flops 704643072 | bytes 5242880 | tf_op jit(solution)/shard_map/pallas_call | solution.py:301
  227.8 15.9 %all_to_all.25 = bf16[16,24,448]{2,1,0:T(8,128)(2,1)} all-to-all(bf16[16,24,448]{2,1,0:T(8,128)(2,1)} %bitcast.99), channel_id=1, replica_groups=mesh['dp'=16,'ep'=8,'tp'=2] {'dp'}, dimensions={0} | all-to-all | bytes 688128 | tf_op jit(solution)/shard_map/all_to_all | solution.py:514
  245.6 15.5 %all_to_all.26 = bf16[16,8,448]{2,1,0:T(8,128)(2,1)S(1)} all-to-all(bf16[16,8,448]{2,1,0:T(8,128)(2,1)} %bitcast.103), channel_id=1, replica_groups=mesh['dp'=16,'ep'=8,'tp'=2] {'ep','tp'}, dimensions={0} | all-to-all | bytes 229376 | tf_op jit(solution)/shard_map/all_to_all | solution.py:517
  (138 shorter events, 63.1 us)
Async XLA Ops:
  6.5 81.8 %all-gather.6.cloned.1.call-start = ((), (), s32[]{:S(2)}) async-start(), calls=%async_computation.5 | async-start | bytes 7798784 | tf_op jit(solution)/shard_map/all_gather | solution.py:385
  7.8 4.4 %collective-permute-start.3 = (bf16[224,512]{1,0:T(8,128)(2,1)S(1)}, bf16[224,512]{1,0:T(8,128)(2,1)S(1)}, u32[]{:S(2)}, u32[]{:S(2)}) collective-permute-start(bf16[224,512]{1,0:T(8,128)(2,1)S(1)} %get-tuple-element.132), channel_id=1, source_target_pairs={{0,1},{1,0},{2,3},{3,2},{4,5},{5,4},{6,7},{7,6},{8,9},{9,8},{10,11... | collective-permute-start | bytes 688136 | tf_op jit(solution)/shard_map/ppermute | solution.py:369
  14.4 18.8 %all-to-all-start = ((bf16[16,2,16,576]{3,2,1,0:T(8,128)(2,1)}), bf16[16,2,16,576]{3,2,1,0:T(8,128)(2,1)S(1)}, u32[]{:S(2)}, u32[]{:S(2)}) async-start(bf16[16,2,16,576]{3,2,1,0:T(8,128)(2,1)} %broadcast_in_dim.12), calls=%async_computation | async-start | bytes 1310720 | tf_op jit(solution)/shard_map/all_to_all | solution.py:379
  21.9 11.3 %collective-permute-start = (bf16[128,896]{1,0:T(8,128)(2,1)}, bf16[128,896]{1,0:T(8,128)(2,1)S(1)}, u32[]{:S(2)}, u32[]{:S(2)}) collective-permute-start(bf16[128,896]{1,0:T(8,128)(2,1)} %get-tuple-element.68), channel_id=1, source_target_pairs={{0,2},{2,4},{4,6},{6,8},{8,10},{10,12},{12,14},{14,0},{1,3},{3,5},... | collective-permute-start | bytes 688136 | tf_op jit(solution)/shard_map/ppermute | solution.py:372
  23.6 9.6 %collective-permute-start.1 = (bf16[128,896]{1,0:T(8,128)(2,1)}, bf16[128,896]{1,0:T(8,128)(2,1)S(1)}, u32[]{:S(2)}, u32[]{:S(2)}) collective-permute-start(bf16[128,896]{1,0:T(8,128)(2,1)} %get-tuple-element.69), channel_id=1, source_target_pairs={{0,14},{2,0},{4,2},{6,4},{8,6},{10,8},{12,10},{14,12},{1,15},{3,1}... | collective-permute-start | bytes 688136 | tf_op jit(solution)/shard_map/ppermute | solution.py:372
  59.5 24.4 %collective-permute-start.4 = (bf16[128,896]{1,0:T(8,128)(2,1)}, bf16[128,896]{1,0:T(8,128)(2,1)}, u32[]{:S(2)}, u32[]{:S(2)}) collective-permute-start(bf16[128,896]{1,0:T(8,128)(2,1)} %get-tuple-element.75), channel_id=1, source_target_pairs={{0,6},{2,8},{4,10},{6,12},{8,14},{10,0},{12,2},{14,4},{1,7},{3,9},... | collective-permute-start | bytes 688136 | tf_op jit(solution)/shard_map/ppermute | solution.py:372
  59.5 28.8 %collective-permute-start.5 = (bf16[128,896]{1,0:T(8,128)(2,1)}, bf16[128,896]{1,0:T(8,128)(2,1)S(1)}, u32[]{:S(2)}, u32[]{:S(2)}) collective-permute-start(bf16[128,896]{1,0:T(8,128)(2,1)} %get-tuple-element.76), channel_id=1, source_target_pairs={{0,10},{2,12},{4,14},{6,0},{8,2},{10,4},{12,6},{14,8},{1,11},{3,13... | collective-permute-start | bytes 688136 | tf_op jit(solution)/shard_map/ppermute | solution.py:372
  64.0 18.1 %collective-permute-start.6 = (bf16[64,896]{1,0:T(8,128)(2,1)}, bf16[64,896]{1,0:T(8,128)(2,1)S(1)}, u32[]{:S(2)}, u32[]{:S(2)}) collective-permute-start(bf16[64,896]{1,0:T(8,128)(2,1)} %get-tuple-element.77), channel_id=1, source_target_pairs={{0,8},{2,10},{4,12},{6,14},{8,0},{10,2},{12,4},{14,6},{1,9},{3,11}... | collective-permute-start | bytes 344072 | tf_op jit(solution)/shard_map/ppermute | solution.py:372
  64.9 18.3 %collective-permute-start.7 = (bf16[64,896]{1,0:T(8,128)(2,1)}, bf16[64,896]{1,0:T(8,128)(2,1)S(1)}, u32[]{:S(2)}, u32[]{:S(2)}) collective-permute-start(bf16[64,896]{1,0:T(8,128)(2,1)} %get-tuple-element.78), channel_id=1, source_target_pairs={{0,8},{2,10},{4,12},{6,14},{8,0},{10,2},{12,4},{14,6},{1,9},{3,11}... | collective-permute-start | bytes 344072 | tf_op jit(solution)/shard_map/ppermute | solution.py:372
  93.6 33.2 %all-to-all-start.1 = ((bf16[8,448,128]{2,1,0:T(8,128)(2,1)}), bf16[8,448,128]{2,1,0:T(8,128)(2,1)S(1)}, u32[]{:S(2)}, u32[]{:S(2)}) async-start(bf16[8,448,128]{2,1,0:T(8,128)(2,1)} %shard_map.139), calls=%async_computation.1 | async-start | bytes 1835008 | tf_op jit(solution)/shard_map/all_to_all | solution.py:469
  130.1 15.1 %all-to-all-start.2 = ((bf16[16,24,448]{2,1,0:T(8,128)(2,1)}), bf16[16,24,448]{2,1,0:T(8,128)(2,1)S(1)}, u32[]{:S(2)}, u32[]{:S(2)}) async-start(bf16[16,24,448]{2,1,0:T(8,128)(2,1)} %bitcast.107), calls=%async_computation.2 | async-start | bytes 786432 | tf_op jit(solution)/shard_map/all_to_all | solution.py:478
  134.7 58.5 %all-gather.8.cloned.1.call-start = ((), (), s32[]{:S(2)}) async-start(), calls=%async_computation.6 | async-start | bytes 5849088 | tf_op jit(solution)/shard_map/all_gather | solution.py:491
  134.8 9.8 %collective-permute-start.8 = (bf16[128,896]{1,0:T(8,128)(2,1)}, bf16[128,896]{1,0:T(8,128)(2,1)S(1)}, u32[]{:S(2)}, u32[]{:S(2)}) collective-permute-start(bf16[128,896]{1,0:T(8,128)(2,1)} %get-tuple-element.97), channel_id=1, source_target_pairs={{0,4},{2,6},{4,8},{6,10},{8,12},{10,14},{12,0},{14,2},{1,5},{3,7},... | collective-permute-start | bytes 688136 | tf_op jit(solution)/shard_map/ppermute | solution.py:372
  134.8 10.3 %collective-permute-start.9 = (bf16[128,896]{1,0:T(8,128)(2,1)}, bf16[128,896]{1,0:T(8,128)(2,1)}, u32[]{:S(2)}, u32[]{:S(2)}) collective-permute-start(bf16[128,896]{1,0:T(8,128)(2,1)} %get-tuple-element.98), channel_id=1, source_target_pairs={{0,12},{2,14},{4,0},{6,2},{8,4},{10,6},{12,8},{14,10},{1,13},{3,15... | collective-permute-start | bytes 688136 | tf_op jit(solution)/shard_map/ppermute | solution.py:372
  153.1 4.9 %collective-permute-start.10 = (bf16[8,128,448]{1,2,0:T(8,128)(2,1)}, bf16[8,128,448]{1,2,0:T(8,128)(2,1)S(1)}, u32[]{:S(2)}, u32[]{:S(2)}) collective-permute-start(bf16[8,128,448]{1,2,0:T(8,128)(2,1)} %copy.87), channel_id=1, source_target_pairs={{0,1},{1,0},{2,3},{3,2},{4,5},{5,4},{6,7},{7,6},{8,9},{9,8},{10,11... | collective-permute-start | bytes 2752520 | tf_op jit(solution)/shard_map/ppermute | solution.py:369
  198.8 5.6 %collective-permute-start.11 = (bf16[384,128]{1,0:T(8,128)(2,1)}, bf16[384,128]{1,0:T(8,128)(2,1)S(1)}, u32[]{:S(2)}, u32[]{:S(2)}) collective-permute-start(bf16[384,128]{1,0:T(8,128)(2,1)} %shard_map.141), channel_id=1, source_target_pairs={{0,2},{2,4},{4,6},{6,8},{8,10},{10,12},{12,14},{14,0},{1,3},{3,5},... | collective-permute-start | bytes 294920 | tf_op jit(solution)/shard_map/ppermute | solution.py:372
  199.8 4.6 %collective-permute-start.12 = (bf16[384,128]{1,0:T(8,128)(2,1)}, bf16[384,128]{1,0:T(8,128)(2,1)S(1)}, u32[]{:S(2)}, u32[]{:S(2)}) collective-permute-start(bf16[384,128]{1,0:T(8,128)(2,1)} %shard_map.141), channel_id=1, source_target_pairs={{0,14},{2,0},{4,2},{6,4},{8,6},{10,8},{12,10},{14,12},{1,15},{3,1}... | collective-permute-start | bytes 294920 | tf_op jit(solution)/shard_map/ppermute | solution.py:372
  204.4 4.7 %collective-permute-start.13 = (bf16[384,128]{1,0:T(8,128)(2,1)S(1)}, bf16[384,128]{1,0:T(8,128)(2,1)S(1)}, u32[]{:S(2)}, u32[]{:S(2)}) collective-permute-start(bf16[384,128]{1,0:T(8,128)(2,1)S(1)} %collective-permute-done.11), channel_id=1, source_target_pairs={{0,2},{2,4},{4,6},{6,8},{8,10},{10,12},{12,14},{14,0},{1,3},{3,5},... | collective-permute-start | bytes 294920 | tf_op jit(solution)/shard_map/ppermute | solution.py:372
  204.4 4.7 %collective-permute-start.14 = (bf16[384,128]{1,0:T(8,128)(2,1)S(1)}, bf16[384,128]{1,0:T(8,128)(2,1)S(1)}, u32[]{:S(2)}, u32[]{:S(2)}) collective-permute-start(bf16[384,128]{1,0:T(8,128)(2,1)S(1)} %collective-permute-done.12), channel_id=1, source_target_pairs={{0,14},{2,0},{4,2},{6,4},{8,6},{10,8},{12,10},{14,12},{1,15},{3,1}... | collective-permute-start | bytes 294920 | tf_op jit(solution)/shard_map/ppermute | solution.py:372
  209.0 5.6 %collective-permute-start.15 = (bf16[384,128]{1,0:T(8,128)(2,1)S(1)}, bf16[384,128]{1,0:T(8,128)(2,1)S(1)}, u32[]{:S(2)}, u32[]{:S(2)}) collective-permute-start(bf16[384,128]{1,0:T(8,128)(2,1)S(1)} %collective-permute-done.13), channel_id=1, source_target_pairs={{0,2},{2,4},{4,6},{6,8},{8,10},{10,12},{12,14},{14,0},{1,3},{3,5},... | collective-permute-start | bytes 294920 | tf_op jit(solution)/shard_map/ppermute | solution.py:372
  209.0 5.7 %collective-permute-start.17 = (bf16[384,128]{1,0:T(8,128)(2,1)S(1)}, bf16[384,128]{1,0:T(8,128)(2,1)S(1)}, u32[]{:S(2)}, u32[]{:S(2)}) collective-permute-start(bf16[384,128]{1,0:T(8,128)(2,1)S(1)} %collective-permute-done.14), channel_id=1, source_target_pairs={{0,14},{2,0},{4,2},{6,4},{8,6},{10,8},{12,10},{14,12},{1,15},{3,1}... | collective-permute-start | bytes 294920 | tf_op jit(solution)/shard_map/ppermute | solution.py:372
  211.8 12.1 %collective-permute-start.19 = (bf16[384,640]{1,0:T(8,128)(2,1)S(1)}, bf16[384,640]{1,0:T(8,128)(2,1)}, u32[]{:S(2)}, u32[]{:S(2)}) collective-permute-start(bf16[384,640]{1,0:T(8,128)(2,1)S(1)} %constant_dynamic-update-slice_fusion.refs_0_), channel_id=1, source_target_pairs={{0,1},{1,0},{2,3},{3,2},{4,5},{5,4},{6,7},{7,6},{8,9},{9,8},{10,11... | collective-permute-start | bytes 1474568 | tf_op jit(solution)/shard_map/ppermute | solution.py:369
  214.7 4.2 %collective-permute-start.16 = (bf16[192,128]{1,0:T(8,128)(2,1)S(1)}, bf16[192,128]{1,0:T(8,128)(2,1)S(1)}, u32[]{:S(2)}, u32[]{:S(2)}) collective-permute-start(bf16[192,128]{1,0:T(8,128)(2,1)S(1)} %slice.57), channel_id=1, source_target_pairs={{0,2},{2,4},{4,6},{6,8},{8,10},{10,12},{12,14},{14,0},{1,3},{3,5},... | collective-permute-start | bytes 147464 | tf_op jit(solution)/shard_map/ppermute | solution.py:372
  219.0 4.9 %collective-permute-start.20 = (bf16[384,384]{1,0:T(8,128)(2,1)S(1)}, bf16[384,384]{1,0:T(8,128)(2,1)}, u32[]{:S(2)}, u32[]{:S(2)}) collective-permute-start(bf16[384,384]{1,0:T(8,128)(2,1)S(1)} %pad_maximum_fusion.3.refs_1_), channel_id=1, source_target_pairs={{0,1},{1,0},{2,3},{3,2},{4,5},{5,4},{6,7},{7,6},{8,9},{9,8},{10,11... | collective-permute-start | bytes 884744 | tf_op jit(solution)/shard_map/ppermute | solution.py:369
  (21 other events, 241.8 us)
Sparse Core Ops, SparseCore 0:
  13.2 72.6 all-gather.5
  146.3 46.7 all-gather.7

commit v9 on v8

--- a/solution.py
+++ b/solution.py
@@ -397,9 +397,9 @@
     moved = lax.all_gather(chosen, MEM, axis=0)
 
     window, held = lax.optimization_barrier(
-        ((slices[3], slices[nz - 3], slices[middle], slices[nz]), (cache, routes, moved))
-    )
-    cache, routes, moved = held
+        ((slices[3], slices[nz - 3], slices[middle], slices[nz]), (routes, moved))
+    )
+    routes, moved = held
     window = (
         along(window[0], 3),
         along(window[1], -3),

time: 270 us -> 272 us (level)
  starting transfers between devices: 60.3 us -> 64.1 us
  blocking collectives: 55.9 us -> 52.5 us
    all_gather x1, blocking collectives: 24.6 us -> 21.2 us  [per_device(): moved = lax.all_gather(chosen, MEM, axis=0)]
    unnamed x48 -> x50, local copies, waits for them, and re-layouts: 5.78 us -> 5.05 us
  transfers between devices with their start and end apart: 26 -> 26, of which waited for: 12 -> 13; matrix products, arithmetic and copies ran while one was open for 11% -> 11% of each run, Pallas kernels for 4% -> 4%
where the time goes in v9:
time: 272 us; the launch traced here: 271 us
  waiting for transfers between devices  72.3 us (27%)
  starting transfers between devices  64.1 us (24%)
  blocking collectives  52.5 us (19%)
  Pallas kernels  28.9 us (11%)
  local copies, waits for them, and re-layouts  22.6 us (8%)
  between operations  17.4 us (6%)
  other arithmetic  12.9 us (5%)
    all_gather x1, waiting for transfers between devices, per_device(): rows_in = lax.all_gather(received, MEM, axis=0)  35.2 us
    ppermute x16, starting transfers between devices, along(): return lax.ppermute(array, 'ep', [(z, (z + hops) % nz) for z in range(nz)])  30.1 us
    all_gather x1, blocking collectives, per_device(): moved = lax.all_gather(chosen, MEM, axis=0)  21.2 us
    ppermute x16, waiting for transfers between devices, along(): return lax.ppermute(array, 'ep', [(z, (z + hops) % nz) for z in range(nz)])  17.8 us
    all_to_all x1, blocking collectives, per_device(): returned = lax.all_to_all(expert_out, DP, 0, 0, tiled=True)  15.9 us
    all_to_all x1, blocking collectives, per_device(): lax.all_to_all(total.reshape(members, group, col), MEM, 0, 0, tiled=True)  15.5 us
    ppermute x5, starting transfers between devices, other_core(): return lax.ppermute(array, 'tp', [(0, 1), (1, 0)])  13.6 us
    all_to_all x1, waiting for transfers between devices, per_device(): shares = lax.all_to_all(shares, 'ep', 0, 0, tiled=True)  13.2 us
  transfers between devices with their start and end apart: 26, of which 13 were waited for; matrix products, arithmetic and copies ran while one was open for 11% of the time, Pallas kernels for 4%

profile of v9, /device:TPU:1, one launch (start us, length us, event | category | flops | bytes accessed | tf_op | source)
XLA Modules:
  0.0 270.7 jit_solution(1366938892459307983)
XLA Ops:
  7.8 3.3 %collective-permute-start.3 = (bf16[224,512]{1,0:T(8,128)(2,1)S(1)}, bf16[224,512]{1,0:T(8,128)(2,1)S(1)}, u32[]{:S(2)}, u32[]{:S(2)}) collective-permute-start(bf16[224,512]{1,0:T(8,128)(2,1)S(1)} %get-tuple-element.130), channel_id=1, source_target_pairs={{0,1},{1,0},{2,3},{3,2},{4,5},{5,4},{6,7},{7,6},{8,9},{9,8},{10,11... | collective-permute-start | bytes 688136 | tf_op jit(solution)/shard_map/ppermute | solution.py:369
  14.4 5.0 %all-to-all-start = ((bf16[16,2,16,576]{3,2,1,0:T(8,128)(2,1)}), bf16[16,2,16,576]{3,2,1,0:T(8,128)(2,1)S(1)}, u32[]{:S(2)}, u32[]{:S(2)}) async-start(bf16[16,2,16,576]{3,2,1,0:T(8,128)(2,1)} %broadcast_in_dim.12), calls=%async_computation | async-start | bytes 1310720 | tf_op jit(solution)/shard_map/all_to_all | solution.py:379
  23.6 4.0 %collective-permute-start.1 = (bf16[128,896]{1,0:T(8,128)(2,1)}, bf16[128,896]{1,0:T(8,128)(2,1)S(1)}, u32[]{:S(2)}, u32[]{:S(2)}) collective-permute-start(bf16[128,896]{1,0:T(8,128)(2,1)} %get-tuple-element.70), channel_id=1, source_target_pairs={{0,14},{2,0},{4,2},{6,4},{8,6},{10,8},{12,10},{14,12},{1,15},{3,1}... | collective-permute-start | bytes 688136 | tf_op jit(solution)/shard_map/ppermute | solution.py:372
  32.8 3.8 %shard_map.136 = (bf16[64,512]{1,0:T(8,128)(2,1)}, bf16[2,128,576]{2,1,0:T(8,128)(2,1)}) custom-call(s32[1]{0:T(128)} %bitcast.rank_ref, s32[64]{0:T(128)} %lengths_ref.3, s32[2,16]{1,0:T(2,128)} %destination_ref.3, bf16[4,576,128]{2,1,0:T(8,128)(2,1)} %bitcast.101, bf16[4,576,256]{2,1,0:T(8,128)(2,1)} %bitcast.92, bf16[4,32,576]{2,1,0:T(8,128)(2,1)} %span_ref.3, ...), custom_call_target="tpu_custom_call" | custom-call | flops 193986560 | bytes 2097152 | tf_op jit(solution)/shard_map/pallas_call | solution.py:100
  36.8 21.2 %all-gather = bf16[32,16,576]{2,1,0:T(8,128)(2,1)} all-gather(bf16[2,16,576]{2,1,0:T(8,128)(2,1)S(1)} %pad_maximum_fusion.7), channel_id=2, replica_groups=mesh['dp'=16,'ep'=8,'tp'=2] {'ep','tp'}, dimensions={0}, use_global_device_ids=true | all-gather | bytes 626688 | tf_op jit(solution)/shard_map/all_gather | solution.py:397
  60.0 4.0 %collective-permute-start.5 = (bf16[128,896]{1,0:T(8,128)(2,1)}, bf16[128,896]{1,0:T(8,128)(2,1)S(1)}, u32[]{:S(2)}, u32[]{:S(2)}) collective-permute-start(bf16[128,896]{1,0:T(8,128)(2,1)} %get-tuple-element.74), channel_id=1, source_target_pairs={{0,10},{2,12},{4,14},{6,0},{8,2},{10,4},{12,6},{14,8},{1,11},{3,13... | collective-permute-start | bytes 688136 | tf_op jit(solution)/shard_map/ppermute | solution.py:372
  65.4 4.0 %collective-permute-start.7 = (bf16[64,896]{1,0:T(8,128)(2,1)}, bf16[64,896]{1,0:T(8,128)(2,1)S(1)}, u32[]{:S(2)}, u32[]{:S(2)}) collective-permute-start(bf16[64,896]{1,0:T(8,128)(2,1)} %get-tuple-element.76), channel_id=1, source_target_pairs={{0,8},{2,10},{4,12},{6,14},{8,0},{10,2},{12,4},{14,6},{1,9},{3,11}... | collective-permute-start | bytes 344072 | tf_op jit(solution)/shard_map/ppermute | solution.py:372
  69.4 3.6 %shard_map.138 = bf16[64,512]{1,0:T(8,128)(2,1)} custom-call(s32[1]{0:T(128)} %bitcast.rank_ref, s32[64]{0:T(128)} %lengths_ref.3, s32[2,16]{1,0:T(2,128)} %destination_ref.3, bf16[2,128,576]{2,1,0:T(8,128)(2,1)} %get-tuple-element.63.rows_ref, bf16[16,2,16,576]{3,2,1,0:T(8,128)(2,1)} %bitcast.93, bf16[4,32,576]{2,1,0:T(8,128)(2,1)} %span_ref.3, ...), custom_call_target="tpu_custom_call" | custom-call | flops 193986560 | bytes 2097152 | tf_op jit(solution)/shard_map/pallas_call | solution.py:100
  86.0 5.2 %shard_map.139 = bf16[8,448,128]{2,1,0:T(8,128)(2,1)} custom-call(bf16[128,1024]{1,0:T(8,128)(2,1)} %pad_maximum_fusion.4.values_ref, bf16[16,224,1024]{2,1,0:T(8,128)(2,1)} %bitcast.91), custom_call_target="tpu_custom_call" | custom-call | flops 939524096 | bytes 8519680 | tf_op jit(solution)/shard_map/pallas_call | solution.py:131
  91.2 9.1 %all-to-all-start.1 = ((bf16[8,448,128]{2,1,0:T(8,128)(2,1)}), bf16[8,448,128]{2,1,0:T(8,128)(2,1)S(1)}, u32[]{:S(2)}, u32[]{:S(2)}) async-start(bf16[8,448,128]{2,1,0:T(8,128)(2,1)} %shard_map.139), calls=%async_computation.1 | async-start | bytes 1835008 | tf_op jit(solution)/shard_map/all_to_all | solution.py:469
  105.1 5.9 %copy.85 = bf16[7168,256]{0,1:T(8,128)(2,1)} copy(bf16[7168,256]{1,0:T(8,128)(2,1)} %bitcast.90) | data formatting | bytes 7340032 | tf_op jit(solution)/shard_map/reshape | solution.py:468
  113.4 13.2 %all-to-all-done.1.shares_ref = bf16[8,448,128]{2,1,0:T(8,128)(2,1)S(1)} async-done(((bf16[8,448,128]{2,1,0:T(8,128)(2,1)}), bf16[8,448,128]{2,1,0:T(8,128)(2,1)S(1)}, u32[]{:S(2)}, u32[]{:S(2)}) %all-to-all-start.1) | async-done | bytes 917536 | tf_op jit(solution)/shard_map/all_to_all | solution.py:469
  129.9 6.2 %all-to-all-start.2 = ((bf16[16,24,448]{2,1,0:T(8,128)(2,1)}), bf16[16,24,448]{2,1,0:T(8,128)(2,1)S(1)}, u32[]{:S(2)}, u32[]{:S(2)}) async-start(bf16[16,24,448]{2,1,0:T(8,128)(2,1)} %bitcast.107), calls=%async_computation.2 | async-start | bytes 786432 | tf_op jit(solution)/shard_map/all_to_all | solution.py:478
  136.3 3.6 %collective-permute-start.9 = (bf16[128,896]{1,0:T(8,128)(2,1)}, bf16[128,896]{1,0:T(8,128)(2,1)}, u32[]{:S(2)}, u32[]{:S(2)}) collective-permute-start(bf16[128,896]{1,0:T(8,128)(2,1)} %get-tuple-element.96), channel_id=1, source_target_pairs={{0,12},{2,14},{4,0},{6,2},{8,4},{10,6},{12,8},{14,10},{1,13},{3,15... | collective-permute-start | bytes 688136 | tf_op jit(solution)/shard_map/ppermute | solution.py:372
  139.8 6.5 %collective-permute-done.8 = bf16[128,896]{1,0:T(8,128)(2,1)S(1)} collective-permute-done((bf16[128,896]{1,0:T(8,128)(2,1)}, bf16[128,896]{1,0:T(8,128)(2,1)S(1)}, u32[]{:S(2)}, u32[]{:S(2)}) %collective-permute-start.8) | collective-permute-done | bytes 229408 | tf_op jit(solution)/shard_map/ppermute | solution.py:372
  159.7 35.2 %all-gather.8.cloned.1.call-done = bf16[7168,384]{1,0:T(8,128)(2,1)} async-done(((bf16[448,384]{1,0:T(8,128)(2,1)}), bf16[7168,384]{1,0:T(8,128)(2,1)}) %all-gather.8.cloned.1.call-update) | async-done | bytes 5505040 | tf_op jit(solution)/shard_map/all_gather | solution.py:491
  194.9 5.6 %shard_map.141 = bf16[384,128]{1,0:T(8,128)(2,1)} custom-call(bf16[7168,384]{1,0:T(8,128)(2,1)} %all-gather.8.cloned.1.call-done, bf16[256,7168]{1,0:T(8,128)(2,1)} %bitcast.89), custom_call_target="tpu_custom_call" | custom-call | flops 1409286144 | bytes 9175040 | tf_op jit(solution)/shard_map/pallas_call | solution.py:179
  210.8 2.7 collective-permute-start.17
  213.5 2.9 %collective-permute-start.19 = (bf16[384,640]{1,0:T(8,128)(2,1)S(1)}, bf16[384,640]{1,0:T(8,128)(2,1)}, u32[]{:S(2)}, u32[]{:S(2)}) collective-permute-start(bf16[384,640]{1,0:T(8,128)(2,1)S(1)} %constant_dynamic-update-slice_fusion.refs_0_), channel_id=1, source_target_pairs={{0,1},{1,0},{2,3},{3,2},{4,5},{5,4},{6,7},{7,6},{8,9},{9,8},{10,11... | collective-permute-start | bytes 1474568 | tf_op jit(solution)/shard_map/ppermute | solution.py:369
  216.5 2.7 %collective-permute-start.18 = (bf16[192,128]{1,0:T(8,128)(2,1)S(1)}, bf16[192,128]{1,0:T(8,128)(2,1)S(1)}, u32[]{:S(2)}, u32[]{:S(2)}) collective-permute-start(bf16[192,128]{1,0:T(8,128)(2,1)S(1)} %slice.58), channel_id=1, source_target_pairs={{0,14},{2,0},{4,2},{6,4},{8,6},{10,8},{12,10},{14,12},{1,15},{3,1}... | collective-permute-start | bytes 147464 | tf_op jit(solution)/shard_map/ppermute | solution.py:372
  220.7 3.6 %collective-permute-start.20 = (bf16[384,384]{1,0:T(8,128)(2,1)S(1)}, bf16[384,384]{1,0:T(8,128)(2,1)}, u32[]{:S(2)}, u32[]{:S(2)}) collective-permute-start(bf16[384,384]{1,0:T(8,128)(2,1)S(1)} %pad_maximum_fusion.3.refs_1_), channel_id=1, source_target_pairs={{0,1},{1,0},{2,3},{3,2},{4,5},{5,4},{6,7},{7,6},{8,9},{9,8},{10,11... | collective-permute-start | bytes 884744 | tf_op jit(solution)/shard_map/ppermute | solution.py:369
  225.6 3.9 %shard_map.142 = bf16[384,448]{1,0:T(8,128)(2,1)} custom-call(bf16[8,128,448]{2,1,0:T(8,128)(2,1)} %get-tuple-element.114.mine_weight_ref, bf16[8,128,448]{2,1,0:T(8,128)(2,1)} %copy.88.other_weight_ref, bf16[384,640]{1,0:T(8,128)(2,1)} %copy-done.3, bf16[384,384]{1,0:T(8,128)(2,1)} %copy-done.2, bf16[384,640]{1,0:T(8,128)(2,1)} %collective-permute-done.19.refs_2_, ...), custom_call_target="tpu_custom_call" | custom-call | flops 704643072 | bytes 5242880 | tf_op jit(solution)/shard_map/pallas_call | solution.py:301
  229.5 15.9 %all_to_all.25 = bf16[16,24,448]{2,1,0:T(8,128)(2,1)} all-to-all(bf16[16,24,448]{2,1,0:T(8,128)(2,1)} %bitcast.99), channel_id=1, replica_groups=mesh['dp'=16,'ep'=8,'tp'=2] {'dp'}, dimensions={0} | all-to-all | bytes 688128 | tf_op jit(solution)/shard_map/all_to_all | solution.py:514
  247.4 15.5 %all_to_all.26 = bf16[16,8,448]{2,1,0:T(8,128)(2,1)S(1)} all-to-all(bf16[16,8,448]{2,1,0:T(8,128)(2,1)} %bitcast.103), channel_id=1, replica_groups=mesh['dp'=16,'ep'=8,'tp'=2] {'ep','tp'}, dimensions={0} | all-to-all | bytes 229376 | tf_op jit(solution)/shard_map/all_to_all | solution.py:517
  (140 shorter events, 66.7 us)
Async XLA Ops:
  6.5 79.4 %all-gather.6.cloned.1.call-start = ((), (), s32[]{:S(2)}) async-start(), calls=%async_computation.5 | async-start | bytes 7798784 | tf_op jit(solution)/shard_map/all_gather | solution.py:385
  7.8 4.4 %collective-permute-start.3 = (bf16[224,512]{1,0:T(8,128)(2,1)S(1)}, bf16[224,512]{1,0:T(8,128)(2,1)S(1)}, u32[]{:S(2)}, u32[]{:S(2)}) collective-permute-start(bf16[224,512]{1,0:T(8,128)(2,1)S(1)} %get-tuple-element.130), channel_id=1, source_target_pairs={{0,1},{1,0},{2,3},{3,2},{4,5},{5,4},{6,7},{7,6},{8,9},{9,8},{10,11... | collective-permute-start | bytes 688136 | tf_op jit(solution)/shard_map/ppermute | solution.py:369
  14.4 22.3 %all-to-all-start = ((bf16[16,2,16,576]{3,2,1,0:T(8,128)(2,1)}), bf16[16,2,16,576]{3,2,1,0:T(8,128)(2,1)S(1)}, u32[]{:S(2)}, u32[]{:S(2)}) async-start(bf16[16,2,16,576]{3,2,1,0:T(8,128)(2,1)} %broadcast_in_dim.12), calls=%async_computation | async-start | bytes 1310720 | tf_op jit(solution)/shard_map/all_to_all | solution.py:379
  21.9 14.8 %collective-permute-start = (bf16[128,896]{1,0:T(8,128)(2,1)}, bf16[128,896]{1,0:T(8,128)(2,1)S(1)}, u32[]{:S(2)}, u32[]{:S(2)}) collective-permute-start(bf16[128,896]{1,0:T(8,128)(2,1)} %get-tuple-element.69), channel_id=1, source_target_pairs={{0,2},{2,4},{4,6},{6,8},{8,10},{10,12},{12,14},{14,0},{1,3},{3,5},... | collective-permute-start | bytes 688136 | tf_op jit(solution)/shard_map/ppermute | solution.py:372
  23.6 13.1 %collective-permute-start.1 = (bf16[128,896]{1,0:T(8,128)(2,1)}, bf16[128,896]{1,0:T(8,128)(2,1)S(1)}, u32[]{:S(2)}, u32[]{:S(2)}) collective-permute-start(bf16[128,896]{1,0:T(8,128)(2,1)} %get-tuple-element.70), channel_id=1, source_target_pairs={{0,14},{2,0},{4,2},{6,4},{8,6},{10,8},{12,10},{14,12},{1,15},{3,1}... | collective-permute-start | bytes 688136 | tf_op jit(solution)/shard_map/ppermute | solution.py:372
  59.5 23.8 %collective-permute-start.4 = (bf16[128,896]{1,0:T(8,128)(2,1)}, bf16[128,896]{1,0:T(8,128)(2,1)S(1)}, u32[]{:S(2)}, u32[]{:S(2)}) collective-permute-start(bf16[128,896]{1,0:T(8,128)(2,1)} %get-tuple-element.73), channel_id=1, source_target_pairs={{0,6},{2,8},{4,10},{6,12},{8,14},{10,0},{12,2},{14,4},{1,7},{3,9},... | collective-permute-start | bytes 688136 | tf_op jit(solution)/shard_map/ppermute | solution.py:372
  60.0 23.3 %collective-permute-start.5 = (bf16[128,896]{1,0:T(8,128)(2,1)}, bf16[128,896]{1,0:T(8,128)(2,1)S(1)}, u32[]{:S(2)}, u32[]{:S(2)}) collective-permute-start(bf16[128,896]{1,0:T(8,128)(2,1)} %get-tuple-element.74), channel_id=1, source_target_pairs={{0,10},{2,12},{4,14},{6,0},{8,2},{10,4},{12,6},{14,8},{1,11},{3,13... | collective-permute-start | bytes 688136 | tf_op jit(solution)/shard_map/ppermute | solution.py:372
  64.0 16.1 %collective-permute-start.6 = (bf16[64,896]{1,0:T(8,128)(2,1)}, bf16[64,896]{1,0:T(8,128)(2,1)S(1)}, u32[]{:S(2)}, u32[]{:S(2)}) collective-permute-start(bf16[64,896]{1,0:T(8,128)(2,1)} %get-tuple-element.75), channel_id=1, source_target_pairs={{0,8},{2,10},{4,12},{6,14},{8,0},{10,2},{12,4},{14,6},{1,9},{3,11}... | collective-permute-start | bytes 344072 | tf_op jit(solution)/shard_map/ppermute | solution.py:372
  65.4 17.2 %collective-permute-start.7 = (bf16[64,896]{1,0:T(8,128)(2,1)}, bf16[64,896]{1,0:T(8,128)(2,1)S(1)}, u32[]{:S(2)}, u32[]{:S(2)}) collective-permute-start(bf16[64,896]{1,0:T(8,128)(2,1)} %get-tuple-element.76), channel_id=1, source_target_pairs={{0,8},{2,10},{4,12},{6,14},{8,0},{10,2},{12,4},{14,6},{1,9},{3,11}... | collective-permute-start | bytes 344072 | tf_op jit(solution)/shard_map/ppermute | solution.py:372
  91.2 35.4 %all-to-all-start.1 = ((bf16[8,448,128]{2,1,0:T(8,128)(2,1)}), bf16[8,448,128]{2,1,0:T(8,128)(2,1)S(1)}, u32[]{:S(2)}, u32[]{:S(2)}) async-start(bf16[8,448,128]{2,1,0:T(8,128)(2,1)} %shard_map.139), calls=%async_computation.1 | async-start | bytes 1835008 | tf_op jit(solution)/shard_map/all_to_all | solution.py:469
  129.9 17.2 %all-to-all-start.2 = ((bf16[16,24,448]{2,1,0:T(8,128)(2,1)}), bf16[16,24,448]{2,1,0:T(8,128)(2,1)S(1)}, u32[]{:S(2)}, u32[]{:S(2)}) async-start(bf16[16,24,448]{2,1,0:T(8,128)(2,1)} %bitcast.107), calls=%async_computation.2 | async-start | bytes 786432 | tf_op jit(solution)/shard_map/all_to_all | solution.py:478
  136.1 58.8 %all-gather.8.cloned.1.call-start = ((), (), s32[]{:S(2)}) async-start(), calls=%async_computation.6 | async-start | bytes 5849088 | tf_op jit(solution)/shard_map/all_gather | solution.py:491
  136.2 10.1 %collective-permute-start.8 = (bf16[128,896]{1,0:T(8,128)(2,1)}, bf16[128,896]{1,0:T(8,128)(2,1)S(1)}, u32[]{:S(2)}, u32[]{:S(2)}) collective-permute-start(bf16[128,896]{1,0:T(8,128)(2,1)} %get-tuple-element.95), channel_id=1, source_target_pairs={{0,4},{2,6},{4,8},{6,10},{8,12},{10,14},{12,0},{14,2},{1,5},{3,7},... | collective-permute-start | bytes 688136 | tf_op jit(solution)/shard_map/ppermute | solution.py:372
  136.3 10.8 %collective-permute-start.9 = (bf16[128,896]{1,0:T(8,128)(2,1)}, bf16[128,896]{1,0:T(8,128)(2,1)}, u32[]{:S(2)}, u32[]{:S(2)}) collective-permute-start(bf16[128,896]{1,0:T(8,128)(2,1)} %get-tuple-element.96), channel_id=1, source_target_pairs={{0,12},{2,14},{4,0},{6,2},{8,4},{10,6},{12,8},{14,10},{1,13},{3,15... | collective-permute-start | bytes 688136 | tf_op jit(solution)/shard_map/ppermute | solution.py:372
  154.9 4.8 %collective-permute-start.10 = (bf16[8,128,448]{1,2,0:T(8,128)(2,1)}, bf16[8,128,448]{1,2,0:T(8,128)(2,1)S(1)}, u32[]{:S(2)}, u32[]{:S(2)}) collective-permute-start(bf16[8,128,448]{1,2,0:T(8,128)(2,1)} %copy.87), channel_id=1, source_target_pairs={{0,1},{1,0},{2,3},{3,2},{4,5},{5,4},{6,7},{7,6},{8,9},{9,8},{10,11... | collective-permute-start | bytes 2752520 | tf_op jit(solution)/shard_map/ppermute | solution.py:369
  200.5 5.6 %collective-permute-start.11 = (bf16[384,128]{1,0:T(8,128)(2,1)}, bf16[384,128]{1,0:T(8,128)(2,1)S(1)}, u32[]{:S(2)}, u32[]{:S(2)}) collective-permute-start(bf16[384,128]{1,0:T(8,128)(2,1)} %shard_map.141), channel_id=1, source_target_pairs={{0,2},{2,4},{4,6},{6,8},{8,10},{10,12},{12,14},{14,0},{1,3},{3,5},... | collective-permute-start | bytes 294920 | tf_op jit(solution)/shard_map/ppermute | solution.py:372
  201.6 4.5 %collective-permute-start.12 = (bf16[384,128]{1,0:T(8,128)(2,1)}, bf16[384,128]{1,0:T(8,128)(2,1)S(1)}, u32[]{:S(2)}, u32[]{:S(2)}) collective-permute-start(bf16[384,128]{1,0:T(8,128)(2,1)} %shard_map.141), channel_id=1, source_target_pairs={{0,14},{2,0},{4,2},{6,4},{8,6},{10,8},{12,10},{14,12},{1,15},{3,1}... | collective-permute-start | bytes 294920 | tf_op jit(solution)/shard_map/ppermute | solution.py:372
  206.1 4.7 %collective-permute-start.13 = (bf16[384,128]{1,0:T(8,128)(2,1)S(1)}, bf16[384,128]{1,0:T(8,128)(2,1)S(1)}, u32[]{:S(2)}, u32[]{:S(2)}) collective-permute-start(bf16[384,128]{1,0:T(8,128)(2,1)S(1)} %collective-permute-done.11), channel_id=1, source_target_pairs={{0,2},{2,4},{4,6},{6,8},{8,10},{10,12},{12,14},{14,0},{1,3},{3,5},... | collective-permute-start | bytes 294920 | tf_op jit(solution)/shard_map/ppermute | solution.py:372
  206.1 4.7 %collective-permute-start.14 = (bf16[384,128]{1,0:T(8,128)(2,1)S(1)}, bf16[384,128]{1,0:T(8,128)(2,1)S(1)}, u32[]{:S(2)}, u32[]{:S(2)}) collective-permute-start(bf16[384,128]{1,0:T(8,128)(2,1)S(1)} %collective-permute-done.12), channel_id=1, source_target_pairs={{0,14},{2,0},{4,2},{6,4},{8,6},{10,8},{12,10},{14,12},{1,15},{3,1}... | collective-permute-start | bytes 294920 | tf_op jit(solution)/shard_map/ppermute | solution.py:372
  210.8 5.6 %collective-permute-start.15 = (bf16[384,128]{1,0:T(8,128)(2,1)S(1)}, bf16[384,128]{1,0:T(8,128)(2,1)S(1)}, u32[]{:S(2)}, u32[]{:S(2)}) collective-permute-start(bf16[384,128]{1,0:T(8,128)(2,1)S(1)} %collective-permute-done.13), channel_id=1, source_target_pairs={{0,2},{2,4},{4,6},{6,8},{8,10},{10,12},{12,14},{14,0},{1,3},{3,5},... | collective-permute-start | bytes 294920 | tf_op jit(solution)/shard_map/ppermute | solution.py:372
  210.8 5.7 %collective-permute-start.17 = (bf16[384,128]{1,0:T(8,128)(2,1)S(1)}, bf16[384,128]{1,0:T(8,128)(2,1)S(1)}, u32[]{:S(2)}, u32[]{:S(2)}) collective-permute-start(bf16[384,128]{1,0:T(8,128)(2,1)S(1)} %collective-permute-done.14), channel_id=1, source_target_pairs={{0,14},{2,0},{4,2},{6,4},{8,6},{10,8},{12,10},{14,12},{1,15},{3,1}... | collective-permute-start | bytes 294920 | tf_op jit(solution)/shard_map/ppermute | solution.py:372
  213.5 12.1 %collective-permute-start.19 = (bf16[384,640]{1,0:T(8,128)(2,1)S(1)}, bf16[384,640]{1,0:T(8,128)(2,1)}, u32[]{:S(2)}, u32[]{:S(2)}) collective-permute-start(bf16[384,640]{1,0:T(8,128)(2,1)S(1)} %constant_dynamic-update-slice_fusion.refs_0_), channel_id=1, source_target_pairs={{0,1},{1,0},{2,3},{3,2},{4,5},{5,4},{6,7},{7,6},{8,9},{9,8},{10,11... | collective-permute-start | bytes 1474568 | tf_op jit(solution)/shard_map/ppermute | solution.py:369
  216.4 4.2 %collective-permute-start.16 = (bf16[192,128]{1,0:T(8,128)(2,1)S(1)}, bf16[192,128]{1,0:T(8,128)(2,1)S(1)}, u32[]{:S(2)}, u32[]{:S(2)}) collective-permute-start(bf16[192,128]{1,0:T(8,128)(2,1)S(1)} %slice.57), channel_id=1, source_target_pairs={{0,2},{2,4},{4,6},{6,8},{8,10},{10,12},{12,14},{14,0},{1,3},{3,5},... | collective-permute-start | bytes 147464 | tf_op jit(solution)/shard_map/ppermute | solution.py:372
  220.7 4.9 %collective-permute-start.20 = (bf16[384,384]{1,0:T(8,128)(2,1)S(1)}, bf16[384,384]{1,0:T(8,128)(2,1)}, u32[]{:S(2)}, u32[]{:S(2)}) collective-permute-start(bf16[384,384]{1,0:T(8,128)(2,1)S(1)} %pad_maximum_fusion.3.refs_1_), channel_id=1, source_target_pairs={{0,1},{1,0},{2,3},{3,2},{4,5},{5,4},{6,7},{7,6},{8,9},{9,8},{10,11... | collective-permute-start | bytes 884744 | tf_op jit(solution)/shard_map/ppermute | solution.py:369
  (22 other events, 338.5 us)
Sparse Core Ops, SparseCore 0:
  13.2 72.6 all-gather.5
  148.2 46.6 all-gather.7
